TPU v7x, 256 devices: a whole 4x4x8 slice. The times are simulated.
256 devices in a mesh: dp: 32 (over y, x, core), mp: 8 (over z).
Axes of the slice: x: 4, y: 4, z: 8, core: 2. Of those that a mesh axis runs over, the one named last changes fastest.
Arguments:
- inputs: bfloat16 [16384, 6144], P('dp', 'mp'), may hold values from -13 to 13, as said below
- out_grad: bfloat16 [16384, 3072], P('dp', 'mp'), may hold values from -6 to 6
- weight: bfloat16 [6144, 3072], P('dp', 'mp'), may hold values from -2 to 2, as said below
- momentum: float32 [6144, 3072], P('dp', 'mp'), may hold values from -6 to 6
- variance: float32 [6144, 3072], P('dp', 'mp'), may hold values from 0.25 to 4
- server_error: float32 [6144, 3072], P('dp', 'mp'), may hold values from -4 to 4
- worker_error: bfloat16 [32, 6144, 3072], P('dp', None, 'mp'), may hold values from -1.5 to 1.5
Outputs:
- input_grad: bfloat16 [16384, 6144], P('dp', 'mp')
- momentum_next: float32 [6144, 3072], P('dp', 'mp')
- server_next: float32 [6144, 3072], P('dp', 'mp')
- worker_next: bfloat16 [32, 6144, 3072], P('dp', None, 'mp')
- refreshed: bfloat16 [16384, 3072], P('dp', 'mp')
Inputs may be any that keep to these rules, and one draw needn't show every extreme that they name: `inputs`: activations whose features have different scales. `weight`: A projection whose rows have different scales.
All inputs are finite; a program needn't handle non-finite values. Where the computation divides by a largest or mean magnitude, that divisor is 1e-20 or more.
Results may differ from a plain program's by a relative error of at most 0.009.
Values may be sent and summed in bfloat16 or wider, within the bound.
No kernel may reach another device: no remote copies, remote signals or barrier semaphores. Data moves between devices by JAX's collectives and lax.ppermute only.
A program may use at most 128 MiB of HBM per device.

v0:
```python
import math

import jax
import jax.numpy as jnp
from jax import lax
from jax.sharding import PartitionSpec as P


def squash(values, rows, cols):
    total_rows, total_cols = values.shape
    blocks = values.reshape(total_rows // rows, rows, total_cols // cols, cols)
    level = jnp.mean(jnp.abs(blocks), axis=(1, 3), keepdims=True) + 1e-06
    return (level * jnp.tanh(blocks / level)).reshape(total_rows, total_cols)


def shards(inputs, out_grad, weight, momentum, variance, server_error, worker_error):
    groups = lax.axis_size("dp")
    rows = weight.shape[0]
    cols = weight.shape[1]
    factor = 1.0 / math.sqrt(inputs.shape[0] * groups)
    gathered = lax.all_gather(inputs, "mp", axis=1, tiled=True)
    terms = jnp.dot(
        out_grad,
        lax.all_gather(weight, "dp", axis=0, tiled=True).T,
        preferred_element_type=jnp.float32,
    )
    input_grad = lax.psum_scatter(terms, "mp", scatter_dimension=1, tiled=True).astype(jnp.bfloat16)
    partial_value = (
        lax.dot_general(
            gathered, out_grad, (((0,), (0,)), ((), ())), preferred_element_type=jnp.float32
        )
        * factor
    )
    corrected = partial_value + worker_error[0].astype(jnp.float32)
    packed = squash(corrected, rows, cols).astype(jnp.bfloat16)
    worker_next = (corrected - packed.astype(jnp.float32)).astype(jnp.bfloat16)[None]
    gradient = jnp.sum(
        lax.all_to_all(
            packed.reshape(groups, rows, cols), "dp", split_axis=0, concat_axis=0, tiled=True
        ).astype(jnp.float32),
        axis=0,
    )
    momentum_next = 0.9 * momentum + 0.1 * gradient
    held = momentum_next + server_error
    squeezed = squash(held, rows, cols)
    server_next = held - squeezed
    direction = (squeezed / (jnp.sqrt(variance) + 1e-06)).astype(jnp.bfloat16)
    step_sq = jnp.sum(jnp.square(direction.astype(jnp.float32)))
    weight_sq, step_sq = lax.psum(
        (jnp.sum(jnp.square(weight.astype(jnp.float32))), step_sq), ("dp", "mp")
    )
    ratio = jnp.sqrt(weight_sq / (step_sq + 1e-12))
    new_block = (weight.astype(jnp.float32) - 0.25 * ratio * direction.astype(jnp.float32)).astype(
        jnp.bfloat16
    )
    result = jnp.dot(
        gathered,
        lax.all_gather(new_block, "dp", axis=0, tiled=True),
        preferred_element_type=jnp.float32,
    )
    refreshed = result.astype(jnp.bfloat16)
    return (input_grad, momentum_next, server_next, worker_next, refreshed)


def solution(mesh):
    return jax.shard_map(
        shards,
        mesh=mesh,
        in_specs=(
            P("dp", "mp"),
            P("dp", "mp"),
            P("dp", "mp"),
            P("dp", "mp"),
            P("dp", "mp"),
            P("dp", "mp"),
            P("dp", None, "mp"),
        ),
        out_specs=(P("dp", "mp"), P("dp", "mp"), P("dp", "mp"), P("dp", None, "mp"), P("dp", "mp")),
        check_vma=False,
    )
```

profile of v0, /device:TPU:2, one launch (start us, length us, event | category | flops | bytes accessed | tf_op | source)
XLA Modules:
  0.0 453.7 jit_solution(756978013976376642)
XLA Ops:
  7.2 0.0 copy-start
  7.2 0.0 all-gather.6.cloned.1.call-start
  7.2 0.7 all-gather.6.cloned.1.call-update
  7.9 0.0 all-gather.4.cloned.1.call-start
  8.0 0.7 all-gather.4.cloned.1.call-update
  8.7 0.0 all-gather.8.cloned.1.call-start
  8.7 78.6 %all-gather.6.cloned.1.call-done = bf16[512,6144]{1,0:T(8,128)(2,1)} async-done(((bf16[512,768]{1,0:T(8,128)(2,1)}), bf16[512,6144]{1,0:T(8,128)(2,1)}) %all-gather.6.cloned.1.call-update) | async-done | bytes 6291472 | tf_op jit(solution)/shard_map/all_gather | solution.py:21
  87.3 0.0 copy-done
  87.3 11.5 %abs_reduce_fusion = (f32[6144]{0:T(1024)S(1)}, f32[6144,384]{1,0:T(8,128)}) fusion(bf16[1,6144,384]{2,1,0:T(8,128)(2,1)} %param.13, bf16[512,6144]{1,0:T(8,128)(2,1)} %all-gather.6.cloned.1.call-done, bf16[512,384]{1,0:T(8,128)(2,1)S(1)} %copy-done), kind=kOutput, calls=%fused_computation.4 | convolution fusion | flops 2427709440 | bytes 20865024 | tf_op jit(solution)/shard_map/dot_general | solution.py:29
  98.8 0.1 reduce_sum.53
  98.8 0.1 reduce_sum.54
  99.0 0.1 mul.52
  99.0 0.1 mul.53
  99.1 7.6 %fusion = (bf16[1,6144,384]{2,1,0:T(8,128)(2,1)}, bf16[6144,384]{1,0:T(8,128)(2,1)S(1)}) fusion(f32[6144,384]{1,0:T(8,128)} %get-tuple-element.26, f32[6144]{0:T(1024)S(1)} %mul.53), kind=kLoop, calls=%fused_computation.5 | loop fusion | flops 14155776 | bytes 18898944 | tf_op jit(solution)/shard_map/broadcast_in_dim | solution.py:36
  106.8 0.0 copy-start.3
  106.8 0.0 copy-start.4
  106.8 0.0 copy-start.1
  106.8 0.0 copy-start.2
  106.8 72.3 %all_to_all.5 = bf16[32,192,384]{2,1,0:T(8,128)(2,1)S(1)} all-to-all(bf16[32,192,384]{2,1,0:T(8,128)(2,1)S(1)} %bitcast.14), channel_id=1, replica_groups=mesh['dp'=32,'mp'=8] {'dp'}, dimensions={0} | all-to-all | bytes 9437184 | tf_op jit(solution)/shard_map/all_to_all | solution.py:38
  179.1 0.7 convert_reduce_fusion
  179.7 0.0 copy-done.3
  179.7 0.0 copy-done.4
  179.7 1.4 abs_reduce_fusion.1
  181.8 0.0 copy-done.1
  181.8 0.0 copy-done.2
  181.8 1.5 fusion.4
  183.3 74.3 %all-reduce = (f32[]{:T(128)}, f32[]{:T(128)}) all-reduce(f32[]{:T(128)} %get-tuple-element.27, f32[]{:T(128)} %get-tuple-element.17), channel_id=1, replica_groups=mesh['dp'=32,'mp'=8] {'dp','mp'}, use_global_device_ids=true, to_apply=%region_6.0 | all-reduce | flops 2 | bytes 16 | tf_op jit(solution)/shard_map/psum | solution.py:49
  259.0 0.7 fusion.3
  259.7 0.0 all-gather.8.cloned.1.call-update
  259.7 0.2 reduce-scatter.2.cloned.1.call-start
  259.9 0.0 all-gather.4.cloned.1.call-done
  260.0 8.8 %fusion.6 = f32[512,6144]{1,0:T(8,128)} fusion(bf16[512,384]{1,0:T(8,128)(2,1)S(1)} %copy-done, bf16[6144,384]{1,0:T(8,128)(2,1)} %all-gather.4.cloned.1.call-done), kind=kOutput, calls=%fused_computation.21 | convolution fusion | flops 2415919104 | bytes 17694720 | tf_op jit(solution)/shard_map/dot_general | solution.py:22
  268.8 0.0 reduce-scatter.2.cloned.1.call-update
  268.8 39.3 %all-gather.8.cloned.1.call-done = bf16[6144,384]{1,0:T(8,128)(2,1)} async-done(((bf16[192,384]{1,0:T(8,128)(2,1)}), bf16[6144,384]{1,0:T(8,128)(2,1)}) %all-gather.8.cloned.1.call-update) | async-done | bytes 4718608 | tf_op jit(solution)/shard_map/all_gather | solution.py:58
  308.1 6.9 %fusion.1 = bf16[512,384]{0,1:T(8,128)(2,1)S(1)} fusion(bf16[6144,384]{1,0:T(8,128)(2,1)} %all-gather.8.cloned.1.call-done, bf16[512,6144]{1,0:T(8,128)(2,1)} %all-gather.6.cloned.1.call-done), kind=kOutput, calls=%fused_computation.7 | convolution fusion | flops 2416115712 | bytes 11403264 | tf_op jit(solution)/shard_map/dot_general | solution.py:56
  314.9 0.9 copy.13
  315.9 128.9 %reduce-scatter.2.cloned.1.call-done = f32[512,768]{1,0:T(8,128)} async-done(((f32[512,6144]{1,0:T(8,128)}), f32[512,768]{1,0:T(8,128)}) %reduce-scatter.2.cloned.1.call-update) | async-done | bytes 1572880 | tf_op jit(solution)/shard_map/reduce_scatter | solution.py:27
  444.8 2.4 convert_element_type.41
  (1 shorter events, 0.0 us)
Async XLA Ops:
  7.2 80.1 %copy-start = (bf16[512,384]{1,0:T(8,128)(2,1)S(1)}, bf16[512,384]{1,0:T(8,128)(2,1)}, u32[]{:S(2)}) copy-start(bf16[512,384]{1,0:T(8,128)(2,1)} %param.8) | copy-start | bytes 1179652
  7.2 80.1 %all-gather.6.cloned.1.call-start = ((), (), s32[]{:S(2)}) async-start(), calls=%async_computation.4 | async-start | bytes 7077888 | tf_op jit(solution)/shard_map/all_gather | solution.py:21
  7.9 252.0 %all-gather.4.cloned.1.call-start = ((), (), s32[]{:S(2)}) async-start(), calls=%async_computation.2 | async-start | bytes 4866048 | tf_op jit(solution)/shard_map/all_gather | solution.py:24
  8.7 299.4 %all-gather.8.cloned.1.call-start = ((), (), s32[]{:S(2)}) async-start(), calls=%async_computation.5 | async-start | bytes 4866048 | tf_op jit(solution)/shard_map/all_gather | solution.py:58
  106.8 72.9 %copy-start.3 = (f32[192,384]{1,0:T(8,128)S(1)}, f32[192,384]{1,0:T(8,128)}, u32[]{:S(2)}) copy-start(f32[192,384]{1,0:T(8,128)} %param.12) | copy-start | bytes 884740
  106.8 72.9 %copy-start.4 = (f32[192,384]{1,0:T(8,128)S(1)}, f32[192,384]{1,0:T(8,128)}, u32[]{:S(2)}) copy-start(f32[192,384]{1,0:T(8,128)} %param.10) | copy-start | bytes 884740
  106.8 75.0 %copy-start.1 = (bf16[192,384]{1,0:T(8,128)(2,1)S(1)}, bf16[192,384]{1,0:T(8,128)(2,1)}, u32[]{:S(2)}) copy-start(bf16[192,384]{1,0:T(8,128)(2,1)} %param.9) | copy-start | bytes 442372
  106.8 75.0 %copy-start.2 = (f32[192,384]{1,0:T(8,128)S(1)}, f32[192,384]{1,0:T(8,128)}, u32[]{:S(2)}) copy-start(f32[192,384]{1,0:T(8,128)} %param.11) | copy-start | bytes 884740
  259.7 185.1 %reduce-scatter.2.cloned.1.call-start = ((), (), s32[]{:S(2)}) async-start(), calls=%async_computation.3 | async-start | bytes 14155776 | tf_op jit(solution)/shard_map/reduce_scatter | solution.py:27
Sparse Core Ops, SparseCore 0:
  9.8 77.4 all-gather.5
  89.8 86.1 all-gather.3
  259.8 48.1 all-gather.7
  310.5 134.2 reduce-scatter.1
where the time goes:
time: 455 us; the launch traced here: 454 us
  waiting for transfers between devices  248 us (55%)
  blocking collectives  147 us (32%)
  matrix products  27.2 us (6%)
  between operations  15.8 us (3%)
  other arithmetic  14.4 us (3%)
    reduce_scatter x1, waiting for transfers between devices, shards(): lax.psum_scatter(terms, 'mp', scatter_dimension=1, tiled=True)  129 us
    all_gather x1, waiting for transfers between devices, shards(): gathered = lax.all_gather(inputs, 'mp', axis=1, tiled=True)  78.6 us
    psum x1, blocking collectives, shards(): lax.psum((jnp.sum(jnp.square(weight.astype(jnp.float32))), step_sq), ('dp...  74.3 us
    all_to_all x1, blocking collectives, shards(): lax.all_to_all(packed.reshape(groups, rows, cols), 'dp', split_axis=0, co...  72.3 us
    all_gather x1, waiting for transfers between devices, shards(): lax.all_gather(new_block, 'dp', axis=0, tiled=True)  39.3 us
    dot_general x1, matrix products, shards(): lax.dot_general(gathered, out_grad, (((0,), (0,)), ((), ())), preferred_e...  11.5 us
  transfers between devices with their start and end apart: 4, of which 3 were waited for; matrix products, arithmetic and copies ran while one was open for 9% of the time, Pallas kernels for 0%

commit v1 on v0

v1 whole, which is shorter than its diff:
```python
import functools
import math

import jax
import jax.numpy as jnp
from jax import lax
from jax.experimental import pallas as pl
from jax.experimental.pallas import tpu as pltpu
from jax.sharding import PartitionSpec as P

BF = jnp.bfloat16
F32 = jnp.float32
NY, NX, NC, NZ = 4, 4, 2, 8
VMEM_LIMIT = 48 * 1024 * 1024


def flat_dp(y, x, c):
    return (y * NX + x) * NC + c


def coords(d):
    return d // (NX * NC), (d // NC) % NX, d % NC


def x_shift(r):
    return [(d, flat_dp(y, (x + r) % NX, c)) for d in range(32) for y, x, c in [coords(d)]]


def y_shift(r):
    return [(d, flat_dp((y + r) % NY, x, c)) for d in range(32) for y, x, c in [coords(d)]]


def xor_perm(n, bit):
    return [(i, i ^ bit) for i in range(n)]


NEAR = [(z, z ^ 1) for z in range(NZ)]
FAR = [(z, (z - 1) % NZ if z % 2 == 0 else (z + 1) % NZ) for z in range(NZ)]


def params():
    return pltpu.CompilerParams(vmem_limit_bytes=VMEM_LIMIT)


def shard_body(halves, fresh_next, fresh_pair, factor, sc, *refs):
    n_a = 2 if halves else 1
    a_refs = refs[:n_a]
    og_ref, we_ref = refs[n_a], refs[n_a + 1]
    skip = (0 if fresh_next else 1) + (0 if fresh_pair else 2)
    wn_ref, keep_ref, send_ref = refs[n_a + 2 + skip :]
    half = pl.program_id(0)
    if halves:
        a = jnp.where(half == 0, a_refs[0][...], a_refs[1][...])
    else:
        a = a_refs[0][...]
    partial = lax.dot_general(a, og_ref[...], (((0,), (0,)), ((), ())), preferred_element_type=F32)
    corrected = partial * factor + we_ref[0].astype(F32)
    rows = corrected.shape[0] // 2
    out = []
    for b in range(2):
        block = corrected[b * rows : (b + 1) * rows]
        level = jnp.sum(jnp.abs(block), axis=(0, 1), keepdims=True) * (1.0 / block.size) + 1e-06
        packed = (level * jnp.tanh(block / level)).astype(BF)
        wn_ref[0, b * rows : (b + 1) * rows] = (block - packed.astype(F32)).astype(BF)
        out.append(packed)
    first = sc[1] == 0
    keep_ref[0] = jnp.where(first, out[0], out[1])
    send_ref[0] = jnp.where(first, out[1], out[0])


def shard_grad(parts, og, worker_error, m, core, slot, wn, pair, factor):
    tokens, cols = og.shape
    wide = worker_error.shape[1] // NZ // 2
    halves = len(parts) == 2
    fresh_next, fresh_pair = wn is None, pair is None
    in_specs = (
        [pl.BlockSpec((tokens, wide), lambda h, s: (0, 0))] * 2
        if halves
        else [pl.BlockSpec((tokens, wide), lambda h, s: (0, h))]
    )
    in_specs += [
        pl.BlockSpec((tokens, cols), lambda h, s: (0, 0)),
        pl.BlockSpec((1, wide, cols), lambda h, s: (0, 2 * s[0] + h, 0)),
    ]
    args = list(parts) + [og, worker_error]
    aliases = {}
    if not fresh_next:
        aliases[1 + len(args)] = 0
        args.append(wn)
        in_specs.append(pl.BlockSpec(memory_space=pl.ANY))
    if not fresh_pair:
        for k in range(2):
            aliases[1 + len(args)] = 1 + k
            args.append(pair[k])
            in_specs.append(pl.BlockSpec(memory_space=pl.ANY))
    out = pl.pallas_call(
        functools.partial(shard_body, halves, fresh_next, fresh_pair, factor),
        grid_spec=pltpu.PrefetchScalarGridSpec(
            num_scalar_prefetch=1,
            grid=(2,),
            in_specs=in_specs,
            out_specs=[
                pl.BlockSpec((1, wide, cols), lambda h, s: (0, 2 * s[0] + h, 0)),
                pl.BlockSpec((1, wide // 2, cols), lambda h, s: (2 * slot + h, 0, 0)),
                pl.BlockSpec((1, wide // 2, cols), lambda h, s: (2 * slot + h, 0, 0)),
            ],
        ),
        out_shape=[
            jax.ShapeDtypeStruct(worker_error.shape, BF),
            jax.ShapeDtypeStruct((4, wide // 2, cols), BF),
            jax.ShapeDtypeStruct((4, wide // 2, cols), BF),
        ],
        input_output_aliases=aliases,
        compiler_params=params(),
        cost_estimate=pl.CostEstimate(
            flops=2 * tokens * 2 * wide * cols, bytes_accessed=4 * 2 * wide * cols * 2, transcendentals=0
        ),
        name="shard_grad",
    )(jnp.stack([m, core]).astype(jnp.int32), *args)
    return out[0], (out[1], out[2])


def core_sum_body(sc, keep_ref, recv_ref, *outs):
    for r in range(NX):
        x = lax.rem(sc[0] + r, NX)
        at = jnp.bitwise_xor(x // 2, sc[1]) * 2 + lax.rem(x, 2)
        outs[r][...] = (keep_ref[at].astype(F32) + recv_ref[at].astype(F32)).astype(BF)


def core_sum(keep, recv, x, parity):
    whole = pl.BlockSpec(keep.shape, lambda i, s: (0, 0, 0))
    one = pl.BlockSpec(keep.shape[1:], lambda i, s: (0, 0))
    return pl.pallas_call(
        core_sum_body,
        grid_spec=pltpu.PrefetchScalarGridSpec(
            num_scalar_prefetch=1, grid=(1,), in_specs=[whole] * 2, out_specs=[one] * 4
        ),
        out_shape=[jax.ShapeDtypeStruct(keep.shape[1:], BF)] * 4,
        compiler_params=params(),
        cost_estimate=pl.CostEstimate(flops=keep.size, bytes_accessed=6 * keep.size, transcendentals=0),
        name="core_sum",
    )(jnp.stack([x, parity]).astype(jnp.int32), keep, recv)


def x_sum_body(sc, a, b, c, d, *rest):
    rest[-1][0] = (
        a[...].astype(F32) + b[...].astype(F32) + c[...].astype(F32) + d[...].astype(F32)
    ).astype(BF)


def x_sum(blocks, slot, held):
    shape = blocks[0].shape
    one = pl.BlockSpec(shape, lambda i, s: (0, 0))
    args = list(blocks)
    in_specs = [one] * 4
    aliases = {}
    if held is not None:
        aliases[1 + len(args)] = 0
        args.append(held)
        in_specs = in_specs + [pl.BlockSpec(memory_space=pl.ANY)]
    return pl.pallas_call(
        x_sum_body,
        grid_spec=pltpu.PrefetchScalarGridSpec(
            num_scalar_prefetch=1,
            grid=(1,),
            in_specs=in_specs,
            out_specs=pl.BlockSpec((1,) + shape, lambda i, s: (s[0], 0, 0)),
        ),
        out_shape=jax.ShapeDtypeStruct((4,) + shape, BF),
        input_output_aliases=aliases,
        compiler_params=params(),
        name="x_sum",
    )(slot[None].astype(jnp.int32), *args)


def update_body(g0, g1, g2, g3, w, mom, var, err, mom_out, err_out, dir_out, sums):
    gradient = (
        g0[0].astype(F32) + g1[...].astype(F32) + g2[...].astype(F32) + g3[...].astype(F32)
    )
    momentum = 0.9 * mom[...] + 0.1 * gradient
    mom_out[...] = momentum
    held = momentum + err[...]
    level = jnp.sum(jnp.abs(held), axis=(0, 1), keepdims=True) * (1.0 / held.size) + 1e-06
    squeezed = level * jnp.tanh(held / level)
    err_out[...] = held - squeezed
    direction = (squeezed / (jnp.sqrt(var[...]) + 1e-06)).astype(BF)
    dir_out[...] = direction
    wf = w[...].astype(F32)
    df = direction.astype(F32)
    total_w = jnp.sum(wf * wf, axis=(0, 1), keepdims=True)
    total_d = jnp.sum(df * df, axis=(0, 1), keepdims=True)
    row = lax.broadcasted_iota(jnp.int32, sums.shape, 0)
    sums[...] = jnp.where(row == 0, total_w, total_d)


def update(xr, got, weight, momentum, variance, server_error):
    shape = weight.shape
    one = pl.BlockSpec(shape, lambda i: (0, 0))
    return pl.pallas_call(
        update_body,
        grid=(1,),
        in_specs=[pl.BlockSpec((1,) + shape, lambda i: (0, 0, 0))] + [one] * 7,
        out_specs=[one, one, one, pl.BlockSpec((8, 128), lambda i: (0, 0))],
        out_shape=[
            jax.ShapeDtypeStruct(shape, F32),
            jax.ShapeDtypeStruct(shape, F32),
            jax.ShapeDtypeStruct(shape, BF),
            jax.ShapeDtypeStruct((8, 128), F32),
        ],
        compiler_params=params(),
        name="update",
    )(xr, *got, weight, momentum, variance, server_error)


def product(sc, shards_in, b_ref):
    total = None
    for k, a in enumerate(shards_in):
        part = jnp.dot(a, b_ref[sc[k]], preferred_element_type=F32)
        total = part if total is None else total + part
    return total


def forward_body(sc, *refs):
    b_ref, out = refs[9], refs[10]
    mats = [r[...] for r in refs[:7]] + [jnp.concatenate([refs[7][...], refs[8][...]], axis=1)]
    out[...] = product(sc, mats, b_ref)


def forward_end_body(sc, *refs):
    b_ref, base, scale, out = refs[9:]
    mats = [r[...] for r in refs[:7]] + [jnp.concatenate([refs[7][...], refs[8][...]], axis=1)]
    out[...] = (base[...] - scale[...] * product(sc, mats, b_ref)).astype(BF)


def forward(parts, ms, matrix, base=None, scale=None):
    tokens = parts[0].shape[0]
    cols = matrix.shape[-1]
    blocks = matrix.reshape(NZ, -1, cols)
    args = list(parts) + [blocks] + ([] if base is None else [base, scale])
    in_specs = [pl.BlockSpec(v.shape, lambda i, s, n=v.ndim: (0,) * n) for v in args]
    return pl.pallas_call(
        forward_body if base is None else forward_end_body,
        grid_spec=pltpu.PrefetchScalarGridSpec(
            num_scalar_prefetch=1,
            grid=(1,),
            in_specs=in_specs,
            out_specs=pl.BlockSpec((tokens, cols), lambda i, s: (0, 0)),
        ),
        out_shape=jax.ShapeDtypeStruct((tokens, cols), F32 if base is None else BF),
        compiler_params=params(),
        cost_estimate=pl.CostEstimate(
            flops=2 * tokens * cols * matrix.size // cols, bytes_accessed=2 * matrix.size * 3, transcendentals=0
        ),
        name="forward",
    )(jnp.stack(ms).astype(jnp.int32), *args)


def input_grad_body(og, w, out, acc):
    j = pl.program_id(0)
    part = lax.dot_general(og[0], w[0], (((1,), (1,)), ((), ())), preferred_element_type=F32)

    @pl.when(j == 0)
    def _():
        acc[...] = part

    @pl.when(j > 0)
    def _():
        acc[...] += part

    @pl.when(j == NZ - 1)
    def _():
        out[...] = acc[...].astype(BF)


def input_grad_of(og_all, rows):
    _, tokens, cols = og_all.shape
    width = rows.shape[1]
    return pl.pallas_call(
        input_grad_body,
        grid=(NZ,),
        in_specs=[
            pl.BlockSpec((1, tokens, cols), lambda j: (j, 0, 0)),
            pl.BlockSpec((1, width, cols), lambda j: (j, 0, 0)),
        ],
        out_specs=pl.BlockSpec((tokens, width), lambda j: (0, 0)),
        out_shape=jax.ShapeDtypeStruct((tokens, width), BF),
        scratch_shapes=[pltpu.VMEM((tokens, width), F32)],
        compiler_params=params(),
        cost_estimate=pl.CostEstimate(
            flops=2 * NZ * tokens * cols * width, bytes_accessed=2 * (og_all.size + rows.size), transcendentals=0
        ),
        name="input_grad",
    )(og_all, rows)


def shards(inputs, out_grad, weight, momentum, variance, server_error, worker_error):
    groups = lax.axis_size("dp")
    factor = 1.0 / math.sqrt(inputs.shape[0] * groups)
    rows, cols = weight.shape
    z = lax.axis_index("mp")
    d = lax.axis_index("dp")
    y, x, core = d // (NX * NC), (d // NC) % NX, d % NC
    parity = z % 2
    sign = 1 - 2 * parity
    wide = inputs.shape[1] // 2

    columns = lax.all_gather(weight, "dp", axis=0, tiled=True)
    perm = [
        (dp * NZ + mp, (4 * mp + dp % 4) * NZ + dp // 4) for dp in range(32) for mp in range(NZ)
    ]
    moved = lax.ppermute(weight, ("dp", "mp"), perm)
    plane = lax.all_gather(moved, "dp", axis=0, tiled=True).reshape(NZ, 4 * rows, cols)

    def near(a):
        return lax.ppermute(a, "mp", NEAR)

    def away(a):
        return lax.ppermute(a, "mp", FAR)

    u1, v1 = near(inputs), away(inputs)
    u2, v2 = near(v1), away(u1)
    u3, v3 = near(v2), away(u2)
    f0, f1 = near(v3[:, :wide]), away(u3[:, wide:])

    def at(k):
        return lax.rem(z + k * sign + 2 * NZ, NZ)

    order = [(inputs,), (u1,), (v2,), (v1,), (u2,), (u3,), (f0, f1), (v3,)]
    ms = [at(0), at(1), at(-2), at(-1), at(2), at(3), at(4), at(-3)]
    sequence = [(0, 1), (3, 2), (4, 5), (7, 6)]
    wn, held = None, None
    for p, pair_of in enumerate(sequence):
        pair = None
        for k in pair_of:
            wn, pair = shard_grad(
                order[k], out_grad, worker_error, ms[k], core, k % 2, wn, pair, factor
            )
        keep, send = pair
        recv = lax.ppermute(send, "dp", xor_perm(32, 1))
        mine = core_sum(keep, recv, x, parity)
        blocks = [mine[0]] + [lax.ppermute(mine[r], "dp", x_shift(r)) for r in (1, 2, 3)]
        owner = ms[2 * p] // 2
        held = x_sum(blocks, lax.rem(owner - y + NY, NY), held)
    got = [lax.ppermute(held[r], "dp", y_shift(r)) for r in (1, 2, 3)]
    momentum_next, server_next, direction, sums = update(
        held, got, weight, momentum, variance, server_error
    )
    directions = lax.all_gather(direction, "dp", axis=0, tiled=True)
    for axis, n, bit in (
        ("dp", 32, 1),
        ("dp", 32, 2),
        ("dp", 32, 4),
        ("dp", 32, 8),
        ("dp", 32, 16),
        ("mp", NZ, 1),
        ("mp", NZ, 2),
        ("mp", NZ, 4),
    ):
        sums = sums + lax.ppermute(sums, axis, xor_perm(n, bit))
    ratio = jnp.sqrt(sums[0:1, 0:1] / (sums[1:2, 0:1] + 1e-12))

    later = out_grad + (f0[0, 0] * 0 + f1[0, 0] * 0)
    og_all = lax.all_gather(later, "mp", axis=0, tiled=False)
    input_grad = input_grad_of(og_all, plane)

    parts = [inputs, u1, v2, v1, u2, u3, v3, f0, f1]
    slots = ms[:6] + [ms[7], ms[6]]
    base = forward(parts, slots, columns)
    refreshed = forward(parts, slots, directions, base, 0.25 * ratio)
    return (input_grad, momentum_next, server_next, wn, refreshed)


def solution(mesh):
    return jax.shard_map(
        shards,
        mesh=mesh,
        in_specs=(
            P("dp", "mp"),
            P("dp", "mp"),
            P("dp", "mp"),
            P("dp", "mp"),
            P("dp", "mp"),
            P("dp", "mp"),
            P("dp", None, "mp"),
        ),
        out_specs=(P("dp", "mp"), P("dp", "mp"), P("dp", "mp"), P("dp", None, "mp"), P("dp", "mp")),
        check_vma=False,
    )
```

time: 455 us -> 283 us (0.62)
  waiting for transfers between devices: 248 us -> 90.4 us
  blocking collectives: 147 us -> 0 us
  starting transfers between devices: 0.34 us -> 67.9 us
  Pallas kernels: 0 us -> 65.4 us
  local copies, waits for them, and re-layouts: 1.18 us -> 38.1 us
  matrix products: 27.2 us -> 0 us
  other arithmetic: 14.4 us -> 2.48 us
    reduce_scatter x1 -> x0, waiting for transfers between devices: 129 us -> none  [shards(): lax.psum_scatter(terms, 'mp', scatter_dimension=1, tiled=True)]
    all_gather x3 -> x4, waiting for transfers between devices: 118 us -> 0.03 us  [the longest x1 0.02 us: shards(): columns = lax.all_gather(weight, 'dp', axis=0, tiled=True)]
    ppermute x0 -> x36, waiting for transfers between devices: none -> 89.6 us  [the longest x4 29.6 us: near(): return lax.ppermute(a, 'mp', NEAR)]
    psum x1 -> x0, blocking collectives: 74.3 us -> none  [shards(): lax.psum((jnp.sum(jnp.square(weight.astype(jnp.float32))), step_sq), ('dp...]
    all_to_all x1 -> x0, blocking collectives: 72.3 us -> none  [shards(): lax.all_to_all(packed.reshape(groups, rows, cols), 'dp', split_axis=0, co...]
    ppermute x0 -> x36, starting transfers between devices: none -> 67.7 us  [the longest x12 30.7 us: shards(): lax.ppermute(mine[r], 'dp', x_shift(r))]
    pallas_call x0 -> x20, Pallas kernels: none -> 65.4 us  [the longest x8 29.9 us: shard_grad(): pl.pallas_call(functools.partial(shard_body, halves, fresh_next, fresh_pa...]
    unnamed x11 -> x118, local copies, waits for them, and re-layouts: 0.94 us -> 36.3 us
  transfers between devices with their start and end apart: 4 -> 40, of which waited for: 3 -> 16; matrix products, arithmetic and copies ran while one was open for 9% -> 2% of each run, Pallas kernels for 0% -> 21%
where the time goes in v1:
time: 283 us; the launch traced here: 281 us
  waiting for transfers between devices  90.4 us (32%)
  starting transfers between devices  67.9 us (24%)
  Pallas kernels  65.4 us (23%)
  local copies, waits for them, and re-layouts  38.1 us (13%)
  between operations  16.8 us (6%)
    unnamed x118, local copies, waits for them, and re-layouts  36.3 us
    ppermute x12, starting transfers between devices, shards(): lax.ppermute(mine[r], 'dp', x_shift(r))  30.7 us
    pallas_call x8, Pallas kernels, shard_grad(): pl.pallas_call(functools.partial(shard_body, halves, fresh_next, fresh_pa...  29.9 us
    ppermute x4, waiting for transfers between devices, near(): return lax.ppermute(a, 'mp', NEAR)  29.6 us
    ppermute x8, waiting for transfers between devices, shards(): sums = sums + lax.ppermute(sums, axis, xor_perm(n, bit))  29.3 us
    ppermute x4, waiting for transfers between devices, away(): return lax.ppermute(a, 'mp', FAR)  23.7 us
    pallas_call x2, Pallas kernels, forward(): pl.pallas_call(forward_body if base is None else forward_end_body, grid_s...  14.4 us
    ppermute x4, starting transfers between devices, away(): return lax.ppermute(a, 'mp', FAR)  14.4 us
  transfers between devices with their start and end apart: 40, of which 16 were waited for; matrix products, arithmetic and copies ran while one was open for 2% of the time, Pallas kernels for 21%

profile of v1, /device:TPU:2, one launch (start us, length us, event | category | flops | bytes accessed | tf_op | source)
XLA Modules:
  0.0 281.0 jit_solution(17914966442903862627)
XLA Ops:
  8.0 2.0 collective-permute-start.4
  10.0 4.9 %collective-permute-start = (bf16[512,768]{1,0:T(8,128)(2,1)}, bf16[512,768]{1,0:T(8,128)(2,1)S(1)}, u32[]{:S(2)}, u32[]{:S(2)}) collective-permute-start(bf16[512,768]{1,0:T(8,128)(2,1)} %refs_0_.5), channel_id=1, source_target_pairs={{0,7},{1,2},{2,1},{3,4},{4,3},{5,6},{6,5},{7,0},{8,15},{9,10},{10,... | collective-permute-start | bytes 2359304 | tf_op jit(solution)/shard_map/ppermute | solution.py:318
  14.9 12.8 %collective-permute-done.4.refs_0_.refs_1_ = bf16[512,768]{1,0:T(8,128)(2,1)S(1)} collective-permute-done((bf16[512,768]{1,0:T(8,128)(2,1)}, bf16[512,768]{1,0:T(8,128)(2,1)S(1)}, u32[]{:S(2)}, u32[]{:S(2)}) %collective-permute-start.4) | collective-permute-done | bytes 786464 | tf_op jit(solution)/shard_map/ppermute | solution.py:315
  27.7 5.7 %collective-permute-start.5 = (bf16[512,768]{1,0:T(8,128)(2,1)S(1)}, bf16[512,768]{1,0:T(8,128)(2,1)S(1)}, u32[]{:S(2)}, u32[]{:S(2)}) collective-permute-start(bf16[512,768]{1,0:T(8,128)(2,1)S(1)} %collective-permute-done.4.refs_0_.refs_1_), channel_id=1, source_target_pairs={{0,7},{1,2},{2,1},{3,4},{4,3},{5,6},{6,5},{7,0},{8,15},{9,10},{10,... | collective-permute-start | bytes 2359304 | tf_op jit(solution)/shard_map/ppermute | solution.py:318
  34.3 15.8 %collective-permute-done.5.refs_0_.refs_2_ = bf16[512,768]{1,0:T(8,128)(2,1)S(1)} collective-permute-done((bf16[512,768]{1,0:T(8,128)(2,1)S(1)}, bf16[512,768]{1,0:T(8,128)(2,1)S(1)}, u32[]{:S(2)}, u32[]{:S(2)}) %collective-permute-start.5) | collective-permute-done | bytes 786464 | tf_op jit(solution)/shard_map/ppermute | solution.py:318
  50.1 1.9 collective-permute-done.1.refs_0_.refs_4_
  52.0 1.5 collective-permute-start.2
  53.5 14.8 %collective-permute-done.6.refs_0_.refs_5_ = bf16[512,768]{1,0:T(8,128)(2,1)S(1)} collective-permute-done((bf16[512,768]{1,0:T(8,128)(2,1)S(1)}, bf16[512,768]{1,0:T(8,128)(2,1)S(1)}, u32[]{:S(2)}, u32[]{:S(2)}) %collective-permute-start.6) | collective-permute-done | bytes 786464 | tf_op jit(solution)/shard_map/ppermute | solution.py:315
  68.4 2.2 collective-permute-start.7
  70.8 7.9 %collective-permute-done.7.refs_1_.refs_8_ = bf16[512,384]{1,0:T(8,128)(2,1)S(1)} collective-permute-done((bf16[512,384]{1,0:T(8,128)(2,1)S(1)}, bf16[512,384]{1,0:T(8,128)(2,1)S(1)}, u32[]{:S(2)}, u32[]{:S(2)}) %collective-permute-start.7) | collective-permute-done | bytes 393248 | tf_op jit(solution)/shard_map/ppermute | solution.py:318
  82.5 1.8 broadcast_add_fusion
  84.4 2.8 %collective-permute-start.8 = (bf16[192,384]{1,0:T(8,128)(2,1)}, bf16[192,384]{1,0:T(8,128)(2,1)}, u32[]{:S(2)}, u32[]{:S(2)}) collective-permute-start(bf16[192,384]{1,0:T(8,128)(2,1)} %w.1), channel_id=1, source_target_pairs={{0,0},{1,32},{2,64},{3,96},{4,128},{5,160},{6,192},{7,224},{8,8},{... | collective-permute-start | bytes 442376 | tf_op jit(solution)/shard_map/ppermute | solution.py:311
  87.4 1.0 copy-done
  88.4 1.1 copy-done.5
  89.5 3.7 %shard_grad.8 = (bf16[1,6144,384]{2,1,0:T(8,128)(2,1)}, bf16[4,192,384]{2,1,0:T(8,128)(2,1)S(1)}, bf16[4,192,384]{2,1,0:T(8,128)(2,1)}) custom-call(s32[2]{0:T(128)S(1)} %pad_add_fusion.8.sc, bf16[512,768]{1,0:T(8,128)(2,1)S(1)} %copy-done.5, bf16[512,384]{1,0:T(8,128)(2,1)S(1)} %copy-done, bf16[1,6144,384]{2,1,0:T(8,128)(2,1)} %refs_3_.1), custom_call_target="tpu_custom_call" | custom-call | flops 301989888 | bytes 2359296 | tf_op jit(solution)/shard_map/shard_grad/pallas_call | solution.py:96
  93.8 3.7 %shard_grad.9 = (bf16[1,6144,384]{2,1,0:T(8,128)(2,1)}, bf16[4,192,384]{2,1,0:T(8,128)(2,1)S(1)}, bf16[4,192,384]{2,1,0:T(8,128)(2,1)}) custom-call(s32[2]{0:T(128)S(1)} %pad_add_fusion.7.sc, bf16[512,768]{1,0:T(8,128)(2,1)S(1)} %collective-permute-done.4.refs_0_.refs_1_, ...), custom_call_target="tpu_custom_call", output_to_operand_aliasing={{0}: (4, {}), {1}: (5, {}), {2}: (6, {})} | custom-call | flops 301989888 | bytes 2359296 | tf_op jit(solution)/shard_map/shard_grad/pallas_call | solution.py:96
  97.6 3.8 %shard_grad.10 = (bf16[1,6144,384]{2,1,0:T(8,128)(2,1)}, bf16[4,192,384]{2,1,0:T(8,128)(2,1)S(1)}, bf16[4,192,384]{2,1,0:T(8,128)(2,1)}) custom-call(s32[2]{0:T(128)S(1)} %pad_add_fusion.6.sc, bf16[512,768]{1,0:T(8,128)(2,1)S(1)} %copy-done.8, bf16[512,384]{1,0:T(8,128)(2,1)S(1)} %copy-done.1, ...), custom_call_target="tpu_custom_call", output_to_operand_aliasing={{0}: (4, {})} | custom-call | flops 301989888 | bytes 2359296 | tf_op jit(solution)/shard_map/shard_grad/pallas_call | solution.py:96
  101.3 3.8 %shard_grad.11 = (bf16[1,6144,384]{2,1,0:T(8,128)(2,1)}, bf16[4,192,384]{2,1,0:T(8,128)(2,1)S(1)}, bf16[4,192,384]{2,1,0:T(8,128)(2,1)}) custom-call(s32[2]{0:T(128)S(1)} %pad_add_fusion.5.sc, bf16[512,768]{1,0:T(8,128)(2,1)S(1)} %collective-permute-done.5.refs_0_.refs_2_, ...), custom_call_target="tpu_custom_call", output_to_operand_aliasing={{0}: (4, {}), {1}: (5, {}), {2}: (6, {})} | custom-call | flops 301989888 | bytes 2359296 | tf_op jit(solution)/shard_map/shard_grad/pallas_call | solution.py:96
  105.6 3.7 %shard_grad.12 = (bf16[1,6144,384]{2,1,0:T(8,128)(2,1)}, bf16[4,192,384]{2,1,0:T(8,128)(2,1)S(1)}, bf16[4,192,384]{2,1,0:T(8,128)(2,1)}) custom-call(s32[2]{0:T(128)S(1)} %pad_add_fusion.4.sc, bf16[512,768]{1,0:T(8,128)(2,1)S(1)} %copy-done.12, bf16[512,384]{1,0:T(8,128)(2,1)S(1)} %copy-done.1, ...), custom_call_target="tpu_custom_call", output_to_operand_aliasing={{0}: (4, {})} | custom-call | flops 301989888 | bytes 2359296 | tf_op jit(solution)/shard_map/shard_grad/pallas_call | solution.py:96
  109.3 3.7 %shard_grad.13 = (bf16[1,6144,384]{2,1,0:T(8,128)(2,1)}, bf16[4,192,384]{2,1,0:T(8,128)(2,1)S(1)}, bf16[4,192,384]{2,1,0:T(8,128)(2,1)}) custom-call(s32[2]{0:T(128)S(1)} %pad_add_fusion.3.sc, bf16[512,768]{1,0:T(8,128)(2,1)S(1)} %collective-permute-done.6.refs_0_.refs_5_, ...), custom_call_target="tpu_custom_call", output_to_operand_aliasing={{0}: (4, {}), {1}: (5, {}), {2}: (6, {})} | custom-call | flops 301989888 | bytes 2359296 | tf_op jit(solution)/shard_map/shard_grad/pallas_call | solution.py:96
  113.1 3.8 %shard_grad.14 = (bf16[1,6144,384]{2,1,0:T(8,128)(2,1)}, bf16[4,192,384]{2,1,0:T(8,128)(2,1)S(1)}, bf16[4,192,384]{2,1,0:T(8,128)(2,1)}) custom-call(s32[2]{0:T(128)S(1)} %pad_add_fusion.2.sc, bf16[512,768]{1,0:T(8,128)(2,1)S(1)} %collective-permute-done.2.refs_0_.refs_6_, bf16[512,384]{1,0:T(8,128)(2,1)S(1)} %copy-done.1, ...), custom_call_target="tpu_custom_call", output_to_operand_aliasing={{0}: (4, {})} | custom-call | flops 301989888 | bytes 2359296 | tf_op jit(solution)/shard_map/shard_grad/pallas_call | solution.py:96
  116.9 3.7 %shard_grad.15 = (bf16[1,6144,384]{2,1,0:T(8,128)(2,1)}, bf16[4,192,384]{2,1,0:T(8,128)(2,1)S(1)}, bf16[4,192,384]{2,1,0:T(8,128)(2,1)}) custom-call(s32[2]{0:T(128)S(1)} %pad_add_fusion.1.sc, bf16[512,384]{1,0:T(8,128)(2,1)S(1)} %copy-done.19, bf16[512,384]{1,0:T(8,128)(2,1)S(1)} %copy-done.16, ...), custom_call_target="tpu_custom_call", output_to_operand_aliasing={{0}: (5, {}), {1}: (6, {}), {2}: (7, {})} | custom-call | flops 301989888 | bytes 2359296 | tf_op jit(solution)/shard_map/shard_grad/pallas_call | solution.py:96
  121.9 1.7 core_sum.7
  124.4 15.1 %collective-permute-start.22 = (bf16[192,384]{1,0:T(8,128)(2,1)S(1)}, bf16[192,384]{1,0:T(8,128)(2,1)S(1)}, u32[]{:S(2)}, u32[]{:S(2)}) collective-permute-start(bf16[192,384]{1,0:T(8,128)(2,1)S(1)} %get-tuple-element.85), channel_id=1, source_target_pairs={{0,16},{8,24},{16,32},{24,40},{32,48},{40,56},{48,0},{56,8},{64,80... | collective-permute-start | bytes 442376 | tf_op jit(solution)/shard_map/ppermute | solution.py:341
  139.5 1.2 collective-permute-start.23
  140.7 2.6 collective-permute-start.24
  143.4 1.8 core_sum.6
  145.8 1.1 copy-done.28
  146.9 2.4 core_sum.5
  149.9 2.9 %collective-permute-start.19 = (bf16[192,384]{1,0:T(8,128)(2,1)S(1)}, bf16[192,384]{1,0:T(8,128)(2,1)S(1)}, u32[]{:S(2)}, u32[]{:S(2)}) collective-permute-start(bf16[192,384]{1,0:T(8,128)(2,1)S(1)} %get-tuple-element.80), channel_id=1, source_target_pairs={{0,32},{8,40},{16,48},{24,56},{32,0},{40,8},{48,16},{56,24},{64,96... | collective-permute-start | bytes 442376 | tf_op jit(solution)/shard_map/ppermute | solution.py:341
  152.8 2.0 collective-permute-start.14
  154.8 1.1 copy-done.30
  155.9 2.4 core_sum.4
  159.6 1.8 collective-permute-start.15
  163.6 1.2 collective-permute-start.10
  165.5 2.9 %collective-permute-start.11 = (bf16[192,384]{1,0:T(8,128)(2,1)}, bf16[192,384]{1,0:T(8,128)(2,1)}, u32[]{:S(2)}, u32[]{:S(2)}) collective-permute-start(bf16[192,384]{1,0:T(8,128)(2,1)} %get-tuple-element.68), channel_id=1, source_target_pairs={{0,32},{8,40},{16,48},{24,56},{32,0},{40,8},{48,16},{56,24},{64,96... | collective-permute-start | bytes 442376 | tf_op jit(solution)/shard_map/ppermute | solution.py:341
  172.8 1.0 copy-done.45
  178.5 1.1 x_sum.6.rest_0_
  180.5 1.1 x_sum.7.g0
  181.7 10.5 %collective-permute-start.27 = (bf16[192,384]{1,0:T(8,128)(2,1)S(1)}, bf16[192,384]{1,0:T(8,128)(2,1)S(1)}, u32[]{:S(2)}, u32[]{:S(2)}) collective-permute-start(bf16[192,384]{1,0:T(8,128)(2,1)S(1)} %get-tuple-element.93), channel_id=1, source_target_pairs={{0,192},{8,200},{16,208},{24,216},{32,224},{40,232},{48,240},{56,2... | collective-permute-start | bytes 442376 | tf_op jit(solution)/shard_map/ppermute | solution.py:344
  193.1 3.3 %collective-permute-done.27.g3 = bf16[192,384]{1,0:T(8,128)(2,1)S(1)} collective-permute-done((bf16[192,384]{1,0:T(8,128)(2,1)S(1)}, bf16[192,384]{1,0:T(8,128)(2,1)S(1)}, u32[]{:S(2)}, u32[]{:S(2)}) %collective-permute-start.27) | collective-permute-done | bytes 147488 | tf_op jit(solution)/shard_map/ppermute | solution.py:344
  196.4 2.5 collective-permute-done.26.g2
  198.9 1.2 collective-permute-done.25.g1
  201.0 1.0 copy-done.32
  203.9 1.4 update.1
  206.1 1.2 collective-permute-done.28
  207.2 2.5 collective-permute-start.29
  209.7 1.6 collective-permute-done.29
  211.3 2.0 collective-permute-start.30
  213.3 3.1 %collective-permute-done.30 = f32[8,128]{1,0:T(8,128)S(1)} collective-permute-done((f32[8,128]{1,0:T(8,128)S(1)}, f32[8,128]{1,0:T(8,128)S(1)}, u32[]{:S(2)}, u32[]{:S(2)}) %collective-permute-start.30) | collective-permute-done | bytes 4128 | tf_op jit(solution)/shard_map/ppermute | solution.py:359
  216.4 3.6 %collective-permute-done.31 = f32[8,128]{1,0:T(8,128)S(1)} collective-permute-done((f32[8,128]{1,0:T(8,128)S(1)}, f32[8,128]{1,0:T(8,128)S(1)}, u32[]{:S(2)}, u32[]{:S(2)}) %collective-permute-start.31) | collective-permute-done | bytes 4128 | tf_op jit(solution)/shard_map/ppermute | solution.py:359
  220.7 4.4 %collective-permute-done.32 = f32[8,128]{1,0:T(8,128)S(1)} collective-permute-done((f32[8,128]{1,0:T(8,128)S(1)}, f32[8,128]{1,0:T(8,128)S(1)}, u32[]{:S(2)}, u32[]{:S(2)}) %collective-permute-start.32) | collective-permute-done | bytes 4128 | tf_op jit(solution)/shard_map/ppermute | solution.py:359
  225.1 3.6 %collective-permute-done.33 = f32[8,128]{1,0:T(8,128)S(1)} collective-permute-done((f32[8,128]{1,0:T(8,128)S(1)}, f32[8,128]{1,0:T(8,128)S(1)}, u32[]{:S(2)}, u32[]{:S(2)}) %collective-permute-start.33) | collective-permute-done | bytes 4128 | tf_op jit(solution)/shard_map/ppermute | solution.py:359
  228.7 4.5 %collective-permute-done.34 = f32[8,128]{1,0:T(8,128)S(1)} collective-permute-done((f32[8,128]{1,0:T(8,128)S(1)}, f32[8,128]{1,0:T(8,128)S(1)}, u32[]{:S(2)}, u32[]{:S(2)}) %collective-permute-start.34) | collective-permute-done | bytes 4128 | tf_op jit(solution)/shard_map/ppermute | solution.py:359
  233.3 7.4 %collective-permute-done.35 = f32[8,128]{1,0:T(8,128)S(1)} collective-permute-done((f32[8,128]{1,0:T(8,128)S(1)}, f32[8,128]{1,0:T(8,128)S(1)}, u32[]{:S(2)}, u32[]{:S(2)}) %collective-permute-start.35) | collective-permute-done | bytes 4128 | tf_op jit(solution)/shard_map/ppermute | solution.py:359
  242.7 1.2 copy-done.13
  243.9 1.0 copy-done.20
  244.9 6.9 %forward.2.refs_10_ = f32[512,384]{1,0:T(8,128)S(1)} custom-call(s32[8]{0:T(128)S(1)} %stack.116.sc, bf16[512,768]{1,0:T(8,128)(2,1)S(1)} %copy-done.6, bf16[512,768]{1,0:T(8,128)(2,1)S(1)} %collective-permute-done.4.refs_0_.refs_1_, bf16[512,768]{1,0:T(8,128)(2,1)S(1)} %collective-permute-done.5.refs_0_.refs_2_, bf16[512,768]{1,0:T(8,128)(2,1)S(1)} %copy-done.9, ...), custom_call_target="tpu_custom_call" | custom-call | flops 2415919104 | bytes 14155776 | tf_op jit(solution)/shard_map/forward/pallas_call | solution.py:241
  252.7 2.0 copy-done.58
  254.7 9.1 %input_grad.1 = bf16[512,768]{1,0:T(8,128)(2,1)} custom-call(bf16[8,512,384]{2,1,0:T(8,128)(2,1)S(1)} %bitcast.26, bf16[8,768,384]{2,1,0:T(8,128)(2,1)} %bitcast.29), custom_call_target="tpu_custom_call" | custom-call | flops 2415919104 | bytes 7864320 | tf_op jit(solution)/shard_map/input_grad/pallas_call | solution.py:278
  263.7 1.1 copy-done.10
  264.9 1.1 copy-done.14
  266.0 1.0 copy-done.21
  267.0 7.5 %forward.3 = bf16[512,384]{1,0:T(8,128)(2,1)} custom-call(s32[8]{0:T(128)S(1)} %stack.116.sc, bf16[512,768]{1,0:T(8,128)(2,1)S(1)} %copy-done.6, bf16[512,768]{1,0:T(8,128)(2,1)S(1)} %collective-permute-done.4.refs_0_.refs_1_, bf16[512,768]{1,0:T(8,128)(2,1)S(1)} %collective-permute-done.5.refs_0_.refs_2_, bf16[512,768]{1,0:T(8,128)(2,1)S(1)} %copy-done.10, ...), custom_call_target="tpu_custom_call" | custom-call | flops 2415919104 | bytes 14155776 | tf_op jit(solution)/shard_map/forward/pallas_call | solution.py:241
  (183 shorter events, 30.0 us)
Async XLA Ops:
  7.2 86.6 %copy-start.1 = (bf16[512,384]{1,0:T(8,128)(2,1)S(1)}, bf16[512,384]{1,0:T(8,128)(2,1)}, u32[]{:S(2)}) copy-start(bf16[512,384]{1,0:T(8,128)(2,1)} %refs_2_.15) | copy-start | bytes 1179652
  7.2 235.5 %all-gather.10.cloned.1.call-start = ((), (), s32[]{:S(2)}) async-start(), calls=%async_computation.2 | async-start | bytes 4866048 | tf_op jit(solution)/shard_map/all_gather | solution.py:307
  7.9 244.8 %all-gather.12.cloned.1.call-start = ((), (), s32[]{:S(2)}) async-start(), calls=%async_computation.3 | async-start | bytes 3538944 | tf_op jit(solution)/shard_map/all_gather | solution.py:363
  8.0 19.8 %collective-permute-start.4 = (bf16[512,768]{1,0:T(8,128)(2,1)}, bf16[512,768]{1,0:T(8,128)(2,1)S(1)}, u32[]{:S(2)}, u32[]{:S(2)}) collective-permute-start(bf16[512,768]{1,0:T(8,128)(2,1)} %refs_0_.5), channel_id=1, source_target_pairs={{0,1},{1,0},{2,3},{3,2},{4,5},{5,4},{6,7},{7,6},{8,9},{9,8},{10,11... | collective-permute-start | bytes 2359304 | tf_op jit(solution)/shard_map/ppermute | solution.py:315
  10.0 23.4 %collective-permute-start = (bf16[512,768]{1,0:T(8,128)(2,1)}, bf16[512,768]{1,0:T(8,128)(2,1)S(1)}, u32[]{:S(2)}, u32[]{:S(2)}) collective-permute-start(bf16[512,768]{1,0:T(8,128)(2,1)} %refs_0_.5), channel_id=1, source_target_pairs={{0,7},{1,2},{2,1},{3,4},{4,3},{5,6},{6,5},{7,0},{8,15},{9,10},{10,... | collective-permute-start | bytes 2359304 | tf_op jit(solution)/shard_map/ppermute | solution.py:318
  27.7 22.3 %collective-permute-start.5 = (bf16[512,768]{1,0:T(8,128)(2,1)S(1)}, bf16[512,768]{1,0:T(8,128)(2,1)S(1)}, u32[]{:S(2)}, u32[]{:S(2)}) collective-permute-start(bf16[512,768]{1,0:T(8,128)(2,1)S(1)} %collective-permute-done.4.refs_0_.refs_1_), channel_id=1, source_target_pairs={{0,7},{1,2},{2,1},{3,4},{4,3},{5,6},{6,5},{7,0},{8,15},{9,10},{10,... | collective-permute-start | bytes 2359304 | tf_op jit(solution)/shard_map/ppermute | solution.py:318
  33.4 18.6 %collective-permute-start.1 = (bf16[512,768]{1,0:T(8,128)(2,1)S(1)}, bf16[512,768]{1,0:T(8,128)(2,1)S(1)}, u32[]{:S(2)}, u32[]{:S(2)}) collective-permute-start(bf16[512,768]{1,0:T(8,128)(2,1)S(1)} %collective-permute-done.refs_0_.refs_3_), channel_id=1, source_target_pairs={{0,1},{1,0},{2,3},{3,2},{4,5},{5,4},{6,7},{7,6},{8,9},{9,8},{10,11... | collective-permute-start | bytes 2359304 | tf_op jit(solution)/shard_map/ppermute | solution.py:315
  50.1 18.3 %collective-permute-start.6 = (bf16[512,768]{1,0:T(8,128)(2,1)S(1)}, bf16[512,768]{1,0:T(8,128)(2,1)S(1)}, u32[]{:S(2)}, u32[]{:S(2)}) collective-permute-start(bf16[512,768]{1,0:T(8,128)(2,1)S(1)} %collective-permute-done.5.refs_0_.refs_2_), channel_id=1, source_target_pairs={{0,1},{1,0},{2,3},{3,2},{4,5},{5,4},{6,7},{7,6},{8,9},{9,8},{10,11... | collective-permute-start | bytes 2359304 | tf_op jit(solution)/shard_map/ppermute | solution.py:315
  52.0 18.6 %copy-start.11 = (bf16[512,768]{1,0:T(8,128)(2,1)}, bf16[512,768]{1,0:T(8,128)(2,1)S(1)}, u32[]{:S(2)}) copy-start(bf16[512,768]{1,0:T(8,128)(2,1)S(1)} %collective-permute-done.1.refs_0_.refs_4_) | copy-start | bytes 2359300
  52.0 18.6 %collective-permute-start.2 = (bf16[512,768]{1,0:T(8,128)(2,1)S(1)}, bf16[512,768]{1,0:T(8,128)(2,1)S(1)}, u32[]{:S(2)}, u32[]{:S(2)}) collective-permute-start(bf16[512,768]{1,0:T(8,128)(2,1)S(1)} %collective-permute-done.1.refs_0_.refs_4_), channel_id=1, source_target_pairs={{0,7},{1,2},{2,1},{3,4},{4,3},{5,6},{6,5},{7,0},{8,15},{9,10},{10,... | collective-permute-start | bytes 2359304 | tf_op jit(solution)/shard_map/ppermute | solution.py:318
  68.4 40.9 %copy-start.2 = (bf16[512,768]{1,0:T(8,128)(2,1)}, bf16[512,768]{1,0:T(8,128)(2,1)S(1)}, u32[]{:S(2)}) copy-start(bf16[512,768]{1,0:T(8,128)(2,1)S(1)} %collective-permute-done.6.refs_0_.refs_5_) | copy-start | bytes 2359300
  68.4 10.3 %collective-permute-start.7 = (bf16[512,384]{1,0:T(8,128)(2,1)S(1)}, bf16[512,384]{1,0:T(8,128)(2,1)S(1)}, u32[]{:S(2)}, u32[]{:S(2)}) collective-permute-start(bf16[512,384]{1,0:T(8,128)(2,1)S(1)} %slice.38), channel_id=1, source_target_pairs={{0,7},{1,2},{2,1},{3,4},{4,3},{5,6},{6,5},{7,0},{8,15},{9,10},{10,... | collective-permute-start | bytes 1179656 | tf_op jit(solution)/shard_map/ppermute | solution.py:318
  70.6 42.5 %copy-start.4 = (bf16[512,768]{1,0:T(8,128)(2,1)}, bf16[512,768]{1,0:T(8,128)(2,1)S(1)}, u32[]{:S(2)}) copy-start(bf16[512,768]{1,0:T(8,128)(2,1)S(1)} %collective-permute-done.2.refs_0_.refs_6_) | copy-start | bytes 2359300
  70.7 9.3 %collective-permute-start.3 = (bf16[512,384]{1,0:T(8,128)(2,1)S(1)}, bf16[512,384]{1,0:T(8,128)(2,1)S(1)}, u32[]{:S(2)}, u32[]{:S(2)}) collective-permute-start(bf16[512,384]{1,0:T(8,128)(2,1)S(1)} %slice.36), channel_id=1, source_target_pairs={{0,1},{1,0},{2,3},{3,2},{4,5},{5,4},{6,7},{7,6},{8,9},{9,8},{10,11... | collective-permute-start | bytes 1179656 | tf_op jit(solution)/shard_map/ppermute | solution.py:315
  84.3 168.4 %all-gather.6.cloned.1.call-start = ((), (), s32[]{:S(2)}) async-start(), calls=%async_computation | async-start | bytes 4866048 | tf_op jit(solution)/shard_map/all_gather | solution.py:312
  84.4 2.8 %collective-permute-start.8 = (bf16[192,384]{1,0:T(8,128)(2,1)}, bf16[192,384]{1,0:T(8,128)(2,1)}, u32[]{:S(2)}, u32[]{:S(2)}) collective-permute-start(bf16[192,384]{1,0:T(8,128)(2,1)} %w.1), channel_id=1, source_target_pairs={{0,0},{1,32},{2,64},{3,96},{4,128},{5,160},{6,192},{7,224},{8,8},{... | collective-permute-start | bytes 442376 | tf_op jit(solution)/shard_map/ppermute | solution.py:311
  87.2 176.5 %all-gather.8.cloned.1.call-start = ((), (), s32[]{:S(2)}) async-start(), calls=%async_computation.1 | async-start | bytes 4866048 | tf_op jit(solution)/shard_map/all_gather | solution.py:348
  88.4 1.1 copy-start.5
  93.8 3.7 %copy-start.8 = (bf16[512,768]{1,0:T(8,128)(2,1)S(1)}, bf16[512,768]{1,0:T(8,128)(2,1)}, u32[]{:S(2)}) copy-start(bf16[512,768]{1,0:T(8,128)(2,1)} %copy-done.7) | copy-start | bytes 2359300
  97.6 3.8 %copy-start.23 = (bf16[4,192,384]{2,1,0:T(8,128)(2,1)}, bf16[4,192,384]{2,1,0:T(8,128)(2,1)S(1)}, u32[]{:S(2)}) copy-start(bf16[4,192,384]{2,1,0:T(8,128)(2,1)S(1)} %get-tuple-element.82.keep_ref) | copy-start | bytes 1769476
  97.6 24.4 %collective-permute-start.21 = (bf16[4,192,384]{2,1,0:T(8,128)(2,1)}, bf16[4,192,384]{2,1,0:T(8,128)(2,1)}, u32[]{:S(2)}, u32[]{:S(2)}) collective-permute-start(bf16[4,192,384]{2,1,0:T(8,128)(2,1)} %get-tuple-element.83), channel_id=1, source_target_pairs={{0,8},{8,0},{16,24},{24,16},{32,40},{40,32},{48,56},{56,48},{64,72... | collective-permute-start | bytes 1769480 | tf_op jit(solution)/shard_map/ppermute | solution.py:339
  101.3 4.3 %copy-start.12 = (bf16[512,768]{1,0:T(8,128)(2,1)S(1)}, bf16[512,768]{1,0:T(8,128)(2,1)}, u32[]{:S(2)}) copy-start(bf16[512,768]{1,0:T(8,128)(2,1)} %copy-done.11) | copy-start | bytes 2359300
  105.1 4.2 %copy-start.25 = (bf16[4,192,384]{2,1,0:T(8,128)(2,1)}, bf16[4,192,384]{2,1,0:T(8,128)(2,1)S(1)}, u32[]{:S(2)}) copy-start(bf16[4,192,384]{2,1,0:T(8,128)(2,1)S(1)} %get-tuple-element.76.keep_ref) | copy-start | bytes 1769476
  105.1 35.6 %collective-permute-start.17 = (bf16[4,192,384]{2,1,0:T(8,128)(2,1)}, bf16[4,192,384]{2,1,0:T(8,128)(2,1)}, u32[]{:S(2)}, u32[]{:S(2)}) collective-permute-start(bf16[4,192,384]{2,1,0:T(8,128)(2,1)} %get-tuple-element.77), channel_id=1, source_target_pairs={{0,8},{8,0},{16,24},{24,16},{32,40},{40,32},{48,56},{56,48},{64,72... | collective-permute-start | bytes 1769480 | tf_op jit(solution)/shard_map/ppermute | solution.py:339
  113.1 3.8 %copy-start.27 = (bf16[4,192,384]{2,1,0:T(8,128)(2,1)}, bf16[4,192,384]{2,1,0:T(8,128)(2,1)S(1)}, u32[]{:S(2)}) copy-start(bf16[4,192,384]{2,1,0:T(8,128)(2,1)S(1)} %get-tuple-element.70.keep_ref) | copy-start | bytes 1769476
  113.1 32.7 %collective-permute-start.13 = (bf16[4,192,384]{2,1,0:T(8,128)(2,1)}, bf16[4,192,384]{2,1,0:T(8,128)(2,1)}, u32[]{:S(2)}, u32[]{:S(2)}) collective-permute-start(bf16[4,192,384]{2,1,0:T(8,128)(2,1)} %get-tuple-element.71), channel_id=1, source_target_pairs={{0,8},{8,0},{16,24},{24,16},{32,40},{40,32},{48,56},{56,48},{64,72... | collective-permute-start | bytes 1769480 | tf_op jit(solution)/shard_map/ppermute | solution.py:339
  113.1 3.8 %copy-start.16 = (bf16[512,384]{1,0:T(8,128)(2,1)S(1)}, bf16[512,384]{1,0:T(8,128)(2,1)}, u32[]{:S(2)}) copy-start(bf16[512,384]{1,0:T(8,128)(2,1)} %copy-done.15) | copy-start | bytes 1179652
  113.1 3.8 %copy-start.19 = (bf16[512,384]{1,0:T(8,128)(2,1)S(1)}, bf16[512,384]{1,0:T(8,128)(2,1)}, u32[]{:S(2)}) copy-start(bf16[512,384]{1,0:T(8,128)(2,1)} %copy-done.18) | copy-start | bytes 1179652
  116.9 5.1 %copy-start.24 = (bf16[4,192,384]{2,1,0:T(8,128)(2,1)S(1)}, bf16[4,192,384]{2,1,0:T(8,128)(2,1)}, u32[]{:S(2)}) copy-start(bf16[4,192,384]{2,1,0:T(8,128)(2,1)} %copy-done.23) | copy-start | bytes 1769476
  116.9 26.5 %copy-start.26 = (bf16[4,192,384]{2,1,0:T(8,128)(2,1)S(1)}, bf16[4,192,384]{2,1,0:T(8,128)(2,1)}, u32[]{:S(2)}) copy-start(bf16[4,192,384]{2,1,0:T(8,128)(2,1)} %copy-done.25) | copy-start | bytes 1769476
  121.4 31.4 %collective-permute-start.9 = (bf16[4,192,384]{2,1,0:T(8,128)(2,1)}, bf16[4,192,384]{2,1,0:T(8,128)(2,1)}, u32[]{:S(2)}, u32[]{:S(2)}) collective-permute-start(bf16[4,192,384]{2,1,0:T(8,128)(2,1)} %get-tuple-element.65), channel_id=1, source_target_pairs={{0,8},{8,0},{16,24},{24,16},{32,40},{40,32},{48,56},{56,48},{64,72... | collective-permute-start | bytes 1769480 | tf_op jit(solution)/shard_map/ppermute | solution.py:339
  124.4 25.5 %collective-permute-start.22 = (bf16[192,384]{1,0:T(8,128)(2,1)S(1)}, bf16[192,384]{1,0:T(8,128)(2,1)S(1)}, u32[]{:S(2)}, u32[]{:S(2)}) collective-permute-start(bf16[192,384]{1,0:T(8,128)(2,1)S(1)} %get-tuple-element.85), channel_id=1, source_target_pairs={{0,16},{8,24},{16,32},{24,40},{32,48},{40,56},{48,0},{56,8},{64,80... | collective-permute-start | bytes 442376 | tf_op jit(solution)/shard_map/ppermute | solution.py:341
  139.5 13.3 %collective-permute-start.23 = (bf16[192,384]{1,0:T(8,128)(2,1)S(1)}, bf16[192,384]{1,0:T(8,128)(2,1)S(1)}, u32[]{:S(2)}, u32[]{:S(2)}) collective-permute-start(bf16[192,384]{1,0:T(8,128)(2,1)S(1)} %get-tuple-element.86), channel_id=1, source_target_pairs={{0,32},{8,40},{16,48},{24,56},{32,0},{40,8},{48,16},{56,24},{64,96... | collective-permute-start | bytes 442376 | tf_op jit(solution)/shard_map/ppermute | solution.py:341
  140.7 18.2 %collective-permute-start.24 = (bf16[192,384]{1,0:T(8,128)(2,1)S(1)}, bf16[192,384]{1,0:T(8,128)(2,1)S(1)}, u32[]{:S(2)}, u32[]{:S(2)}) collective-permute-start(bf16[192,384]{1,0:T(8,128)(2,1)S(1)} %get-tuple-element.87), channel_id=1, source_target_pairs={{0,48},{8,56},{16,0},{24,8},{32,16},{40,24},{48,32},{56,40},{64,11... | collective-permute-start | bytes 442376 | tf_op jit(solution)/shard_map/ppermute | solution.py:341
  145.8 15.7 %collective-permute-start.18 = (bf16[192,384]{1,0:T(8,128)(2,1)S(1)}, bf16[192,384]{1,0:T(8,128)(2,1)S(1)}, u32[]{:S(2)}, u32[]{:S(2)}) collective-permute-start(bf16[192,384]{1,0:T(8,128)(2,1)S(1)} %get-tuple-element.79), channel_id=1, source_target_pairs={{0,16},{8,24},{16,32},{24,40},{32,48},{40,56},{48,0},{56,8},{64,80... | collective-permute-start | bytes 442376 | tf_op jit(solution)/shard_map/ppermute | solution.py:341
  149.9 8.4 %copy-start.38 = (bf16[192,384]{1,0:T(8,128)(2,1)}, bf16[192,384]{1,0:T(8,128)(2,1)S(1)}, u32[]{:S(2)}) copy-start(bf16[192,384]{1,0:T(8,128)(2,1)S(1)} %collective-permute-done.22.b) | copy-start | bytes 442372
  149.9 13.1 %collective-permute-start.19 = (bf16[192,384]{1,0:T(8,128)(2,1)S(1)}, bf16[192,384]{1,0:T(8,128)(2,1)S(1)}, u32[]{:S(2)}, u32[]{:S(2)}) collective-permute-start(bf16[192,384]{1,0:T(8,128)(2,1)S(1)} %get-tuple-element.80), channel_id=1, source_target_pairs={{0,32},{8,40},{16,48},{24,56},{32,0},{40,8},{48,16},{56,24},{64,96... | collective-permute-start | bytes 442376 | tf_op jit(solution)/shard_map/ppermute | solution.py:341
  152.8 6.2 %copy-start.40 = (bf16[192,384]{1,0:T(8,128)(2,1)}, bf16[192,384]{1,0:T(8,128)(2,1)S(1)}, u32[]{:S(2)}) copy-start(bf16[192,384]{1,0:T(8,128)(2,1)S(1)} %collective-permute-done.23.c) | copy-start | bytes 442372
  152.8 12.0 %collective-permute-start.20 = (bf16[192,384]{1,0:T(8,128)(2,1)S(1)}, bf16[192,384]{1,0:T(8,128)(2,1)S(1)}, u32[]{:S(2)}, u32[]{:S(2)}) collective-permute-start(bf16[192,384]{1,0:T(8,128)(2,1)S(1)} %get-tuple-element.81), channel_id=1, source_target_pairs={{0,48},{8,56},{16,0},{24,8},{32,16},{40,24},{48,32},{56,40},{64,11... | collective-permute-start | bytes 442376 | tf_op jit(solution)/shard_map/ppermute | solution.py:341
  152.8 15.6 %collective-permute-start.14 = (bf16[192,384]{1,0:T(8,128)(2,1)S(1)}, bf16[192,384]{1,0:T(8,128)(2,1)S(1)}, u32[]{:S(2)}, u32[]{:S(2)}) collective-permute-start(bf16[192,384]{1,0:T(8,128)(2,1)S(1)} %get-tuple-element.73), channel_id=1, source_target_pairs={{0,16},{8,24},{16,32},{24,40},{32,48},{40,56},{48,0},{56,8},{64,80... | collective-permute-start | bytes 442376 | tf_op jit(solution)/shard_map/ppermute | solution.py:341
  159.6 17.0 %collective-permute-start.15 = (bf16[192,384]{1,0:T(8,128)(2,1)}, bf16[192,384]{1,0:T(8,128)(2,1)}, u32[]{:S(2)}, u32[]{:S(2)}) collective-permute-start(bf16[192,384]{1,0:T(8,128)(2,1)} %get-tuple-element.74), channel_id=1, source_target_pairs={{0,32},{8,40},{16,48},{24,56},{32,0},{40,8},{48,16},{56,24},{64,96... | collective-permute-start | bytes 442376 | tf_op jit(solution)/shard_map/ppermute | solution.py:341
  162.1 14.5 %collective-permute-start.16 = (bf16[192,384]{1,0:T(8,128)(2,1)}, bf16[192,384]{1,0:T(8,128)(2,1)}, u32[]{:S(2)}, u32[]{:S(2)}) collective-permute-start(bf16[192,384]{1,0:T(8,128)(2,1)} %get-tuple-element.75), channel_id=1, source_target_pairs={{0,48},{8,56},{16,0},{24,8},{32,16},{40,24},{48,32},{56,40},{64,11... | collective-permute-start | bytes 442376 | tf_op jit(solution)/shard_map/ppermute | solution.py:341
  163.6 16.0 %collective-permute-start.10 = (bf16[192,384]{1,0:T(8,128)(2,1)}, bf16[192,384]{1,0:T(8,128)(2,1)}, u32[]{:S(2)}, u32[]{:S(2)}) collective-permute-start(bf16[192,384]{1,0:T(8,128)(2,1)} %get-tuple-element.67), channel_id=1, source_target_pairs={{0,16},{8,24},{16,32},{24,40},{32,48},{40,56},{48,0},{56,8},{64,80... | collective-permute-start | bytes 442376 | tf_op jit(solution)/shard_map/ppermute | solution.py:341
  165.5 14.1 %collective-permute-start.11 = (bf16[192,384]{1,0:T(8,128)(2,1)}, bf16[192,384]{1,0:T(8,128)(2,1)}, u32[]{:S(2)}, u32[]{:S(2)}) collective-permute-start(bf16[192,384]{1,0:T(8,128)(2,1)} %get-tuple-element.68), channel_id=1, source_target_pairs={{0,32},{8,40},{16,48},{24,56},{32,0},{40,8},{48,16},{56,24},{64,96... | collective-permute-start | bytes 442376 | tf_op jit(solution)/shard_map/ppermute | solution.py:341
  169.0 10.5 %collective-permute-start.12 = (bf16[192,384]{1,0:T(8,128)(2,1)}, bf16[192,384]{1,0:T(8,128)(2,1)}, u32[]{:S(2)}, u32[]{:S(2)}) collective-permute-start(bf16[192,384]{1,0:T(8,128)(2,1)} %get-tuple-element.69), channel_id=1, source_target_pairs={{0,48},{8,56},{16,0},{24,8},{32,16},{40,24},{48,32},{56,40},{64,11... | collective-permute-start | bytes 442376 | tf_op jit(solution)/shard_map/ppermute | solution.py:341
  172.7 70.0 %copy-start.6 = (bf16[512,768]{1,0:T(8,128)(2,1)S(1)}, bf16[512,768]{1,0:T(8,128)(2,1)}, u32[]{:S(2)}) copy-start(bf16[512,768]{1,0:T(8,128)(2,1)} %refs_0_.5) | copy-start | bytes 2359300
  172.7 70.0 %copy-start.9 = (bf16[512,768]{1,0:T(8,128)(2,1)S(1)}, bf16[512,768]{1,0:T(8,128)(2,1)}, u32[]{:S(2)}) copy-start(bf16[512,768]{1,0:T(8,128)(2,1)} %copy-done.7) | copy-start | bytes 2359300
  172.7 70.0 %copy-start.17 = (bf16[512,384]{1,0:T(8,128)(2,1)S(1)}, bf16[512,384]{1,0:T(8,128)(2,1)}, u32[]{:S(2)}) copy-start(bf16[512,384]{1,0:T(8,128)(2,1)} %copy-done.15) | copy-start | bytes 1179652
  181.7 14.7 %collective-permute-start.27 = (bf16[192,384]{1,0:T(8,128)(2,1)S(1)}, bf16[192,384]{1,0:T(8,128)(2,1)S(1)}, u32[]{:S(2)}, u32[]{:S(2)}) collective-permute-start(bf16[192,384]{1,0:T(8,128)(2,1)S(1)} %get-tuple-element.93), channel_id=1, source_target_pairs={{0,192},{8,200},{16,208},{24,216},{32,224},{40,232},{48,240},{56,2... | collective-permute-start | bytes 442376 | tf_op jit(solution)/shard_map/ppermute | solution.py:344
  192.2 6.8 %collective-permute-start.26 = (bf16[192,384]{1,0:T(8,128)(2,1)S(1)}, bf16[192,384]{1,0:T(8,128)(2,1)S(1)}, u32[]{:S(2)}, u32[]{:S(2)}) collective-permute-start(bf16[192,384]{1,0:T(8,128)(2,1)S(1)} %get-tuple-element.94), channel_id=1, source_target_pairs={{0,128},{8,136},{16,144},{24,152},{32,160},{40,168},{48,176},{56,1... | collective-permute-start | bytes 442376 | tf_op jit(solution)/shard_map/ppermute | solution.py:344
  192.2 7.9 %collective-permute-start.25 = (bf16[192,384]{1,0:T(8,128)(2,1)S(1)}, bf16[192,384]{1,0:T(8,128)(2,1)S(1)}, u32[]{:S(2)}, u32[]{:S(2)}) collective-permute-start(bf16[192,384]{1,0:T(8,128)(2,1)S(1)} %get-tuple-element.95), channel_id=1, source_target_pairs={{0,64},{8,72},{16,80},{24,88},{32,96},{40,104},{48,112},{56,120},{... | collective-permute-start | bytes 442376 | tf_op jit(solution)/shard_map/ppermute | solution.py:344
  206.0 1.3 collective-permute-start.28
  207.2 4.1 %collective-permute-start.29 = (f32[8,128]{1,0:T(8,128)S(1)}, f32[8,128]{1,0:T(8,128)S(1)}, u32[]{:S(2)}, u32[]{:S(2)}) collective-permute-start(f32[8,128]{1,0:T(8,128)S(1)} %add.138), channel_id=1, source_target_pairs={{0,16},{8,24},{16,0},{24,8},{32,48},{40,56},{48,32},{56,40},{64,80... | collective-permute-start | bytes 12296 | tf_op jit(solution)/shard_map/ppermute | solution.py:359
  211.3 5.1 %collective-permute-start.30 = (f32[8,128]{1,0:T(8,128)S(1)}, f32[8,128]{1,0:T(8,128)S(1)}, u32[]{:S(2)}, u32[]{:S(2)}) collective-permute-start(f32[8,128]{1,0:T(8,128)S(1)} %add.139), channel_id=1, source_target_pairs={{0,32},{8,40},{16,48},{24,56},{32,0},{40,8},{48,16},{56,24},{64,96... | collective-permute-start | bytes 12296 | tf_op jit(solution)/shard_map/ppermute | solution.py:359
  216.4 3.6 %collective-permute-start.31 = (f32[8,128]{1,0:T(8,128)S(1)}, f32[8,128]{1,0:T(8,128)S(1)}, u32[]{:S(2)}, u32[]{:S(2)}) collective-permute-start(f32[8,128]{1,0:T(8,128)S(1)} %add.140), channel_id=1, source_target_pairs={{0,64},{8,72},{16,80},{24,88},{32,96},{40,104},{48,112},{56,120},{... | collective-permute-start | bytes 12296 | tf_op jit(solution)/shard_map/ppermute | solution.py:359
  220.0 5.1 %collective-permute-start.32 = (f32[8,128]{1,0:T(8,128)S(1)}, f32[8,128]{1,0:T(8,128)S(1)}, u32[]{:S(2)}, u32[]{:S(2)}) collective-permute-start(f32[8,128]{1,0:T(8,128)S(1)} %add.141), channel_id=1, source_target_pairs={{0,128},{8,136},{16,144},{24,152},{32,160},{40,168},{48,176},{56,1... | collective-permute-start | bytes 12296 | tf_op jit(solution)/shard_map/ppermute | solution.py:359
  225.1 3.6 %collective-permute-start.33 = (f32[8,128]{1,0:T(8,128)S(1)}, f32[8,128]{1,0:T(8,128)S(1)}, u32[]{:S(2)}, u32[]{:S(2)}) collective-permute-start(f32[8,128]{1,0:T(8,128)S(1)} %add.142), channel_id=1, source_target_pairs={{0,1},{1,0},{2,3},{3,2},{4,5},{5,4},{6,7},{7,6},{8,9},{9,8},{10,11... | collective-permute-start | bytes 12296 | tf_op jit(solution)/shard_map/ppermute | solution.py:359
  228.7 4.5 %collective-permute-start.34 = (f32[8,128]{1,0:T(8,128)S(1)}, f32[8,128]{1,0:T(8,128)S(1)}, u32[]{:S(2)}, u32[]{:S(2)}) collective-permute-start(f32[8,128]{1,0:T(8,128)S(1)} %add.143), channel_id=1, source_target_pairs={{0,2},{1,3},{2,0},{3,1},{4,6},{5,7},{6,4},{7,5},{8,10},{9,11},{10,... | collective-permute-start | bytes 12296 | tf_op jit(solution)/shard_map/ppermute | solution.py:359
  233.2 7.5 %collective-permute-start.35 = (f32[8,128]{1,0:T(8,128)S(1)}, f32[8,128]{1,0:T(8,128)S(1)}, u32[]{:S(2)}, u32[]{:S(2)}) collective-permute-start(f32[8,128]{1,0:T(8,128)S(1)} %add.144), channel_id=1, source_target_pairs={{0,4},{1,5},{2,6},{3,7},{4,0},{5,1},{6,2},{7,3},{8,12},{9,13},{10,... | collective-permute-start | bytes 12296 | tf_op jit(solution)/shard_map/ppermute | solution.py:359
  242.7 1.2 copy-start.13
  252.7 11.0 %copy-start.3 = (bf16[512,768]{1,0:T(8,128)(2,1)S(1)}, bf16[512,768]{1,0:T(8,128)(2,1)}, u32[]{:S(2)}) copy-start(bf16[512,768]{1,0:T(8,128)(2,1)} %copy-done.2) | copy-start | bytes 2359300
  252.7 2.0 copy-start.58
  263.7 1.1 copy-start.10
  264.9 1.1 copy-start.14
  (35 other events, 29.8 us)
Sparse Core Ops, SparseCore 0:
  10.6 54.4 all-gather.9
  84.5 49.0 all-gather.11
  136.1 56.1 all-gather.5
  206.1 45.7 all-gather.7

commit v2 on v1

v2 whole, which is shorter than its diff:
```python
import functools
import math

import jax
import jax.numpy as jnp
from jax import lax
from jax.experimental import pallas as pl
from jax.experimental.pallas import tpu as pltpu
from jax.sharding import PartitionSpec as P

BF = jnp.bfloat16
F32 = jnp.float32
NY, NX, NC, NZ = 4, 4, 2, 8
MIB = 1024 * 1024


def flat_dp(y, x, c):
    return (y * NX + x) * NC + c


def coords(d):
    return d // (NX * NC), (d // NC) % NX, d % NC


def x_shift(r):
    return [(d, flat_dp(y, (x + r) % NX, c)) for d in range(32) for y, x, c in [coords(d)]]


def y_shift(r):
    return [(d, flat_dp((y + r) % NY, x, c)) for d in range(32) for y, x, c in [coords(d)]]


def xor_perm(n, bit):
    return [(i, i ^ bit) for i in range(n)]


NEAR = [(z, z ^ 1) for z in range(NZ)]
FAR = [(z, (z - 1) % NZ if z % 2 == 0 else (z + 1) % NZ) for z in range(NZ)]


def params(mib=60):
    return pltpu.CompilerParams(vmem_limit_bytes=mib * MIB)


CORE, X, PARITY, SLOT = 8, 9, 10, 11


def shard_body(n_parts, ks, fresh, factor, sc, *refs):
    at = 0
    step = pl.program_id(0)
    values = []
    for n in n_parts:
        if n == 2:
            values.append(jnp.where(step % 2 == 0, refs[at][...], refs[at + 1][...]))
        else:
            values.append(refs[at][...])
        at += n
    og_ref, we_ref = refs[at], refs[at + 1]
    wn_ref, keep_ref, send_ref = refs[at + (2 if fresh else 3) :]
    a = values[0] if len(values) == 1 else jnp.where(step < 2, values[0], values[1])
    partial = lax.dot_general(a, og_ref[...], (((0,), (0,)), ((), ())), preferred_element_type=F32)
    corrected = partial * factor + we_ref[0].astype(F32)
    rows = corrected.shape[0] // 2
    out = []
    for b in range(2):
        block = corrected[b * rows : (b + 1) * rows]
        level = jnp.sum(jnp.abs(block), axis=(0, 1), keepdims=True) * (1.0 / block.size) + 1e-06
        packed = (level * jnp.tanh(block / level)).astype(BF)
        wn_ref[0, b * rows : (b + 1) * rows] = (block - packed.astype(F32)).astype(BF)
        out.append(packed)
    first = sc[CORE] == 0
    keep_ref[0] = jnp.where(first, out[0], out[1])
    send_ref[0] = jnp.where(first, out[1], out[0])


def shard_grad(sc, parts, ks, og, worker_error, wn, factor):
    tokens, cols = og.shape
    wide = worker_error.shape[1] // NZ // 2
    count = 2 * len(parts)
    in_specs, args = [], []
    for k, part in enumerate(parts):
        for piece in part:
            if len(part) == 2:
                in_specs.append(pl.BlockSpec((tokens, wide), lambda g, s: (0, 0)))
            else:
                in_specs.append(
                    pl.BlockSpec(
                        (tokens, wide), lambda g, s, k=k: (0, jnp.clip(g - 2 * k, 0, 1))
                    )
                )
            args.append(piece)

    def error_at(g, s):
        m = s[ks[0]] if len(ks) == 1 else jnp.where(g < 2, s[ks[0]], s[ks[1]])
        return (0, 2 * m + g % 2, 0)

    in_specs += [
        pl.BlockSpec((tokens, cols), lambda g, s: (0, 0)),
        pl.BlockSpec((1, wide, cols), error_at),
    ]
    args += [og, worker_error]
    aliases = {}
    if wn is not None:
        aliases[1 + len(args)] = 0
        args.append(wn)
        in_specs.append(pl.BlockSpec(memory_space=pl.ANY))
    block = pl.BlockSpec((1, wide // 2, cols), lambda g, s: (g, 0, 0))
    half = jax.ShapeDtypeStruct((count, wide // 2, cols), BF)
    return pl.pallas_call(
        functools.partial(shard_body, [len(p) for p in parts], ks, wn is None, factor),
        grid_spec=pltpu.PrefetchScalarGridSpec(
            num_scalar_prefetch=1,
            grid=(count,),
            in_specs=in_specs,
            out_specs=[pl.BlockSpec((1, wide, cols), error_at), block, block],
        ),
        out_shape=[jax.ShapeDtypeStruct(worker_error.shape, BF), half, half],
        input_output_aliases=aliases,
        compiler_params=params(),
        cost_estimate=pl.CostEstimate(
            flops=2 * tokens * count * wide * cols,
            bytes_accessed=6 * count * wide * cols,
            transcendentals=0,
        ),
        name="shard_grad",
    )(sc, *args)


def core_sum_body(n, sc, *refs):
    outs = refs[4 * n :]
    for r in range(NX):
        x = lax.rem(sc[X] + r, NX)
        same = jnp.bitwise_xor(x // 2, sc[PARITY]) == 0
        h = lax.rem(x, 2)
        for p in range(n):
            a, ra, b, rb = refs[4 * p : 4 * p + 4]
            first = a[h].astype(F32) + ra[h].astype(F32)
            second = b[h].astype(F32) + rb[h].astype(F32)
            outs[r][p] = jnp.where(same, first, second).astype(outs[r].dtype)


def core_sum(sc, pairs):
    tail = pairs[0][0][0].shape[1:]
    n = len(pairs)
    args, in_specs = [], []
    for pair in pairs:
        for keep, recv, half in pair:
            args += [keep, recv]
            in_specs += [pl.BlockSpec((2,) + tail, lambda i, s, half=half: (half, 0, 0))] * 2
    one = pl.BlockSpec((n,) + tail, lambda i, s: (0, 0, 0))
    return pl.pallas_call(
        functools.partial(core_sum_body, n),
        grid_spec=pltpu.PrefetchScalarGridSpec(
            num_scalar_prefetch=1, grid=(1,), in_specs=in_specs, out_specs=[one] * 4
        ),
        out_shape=[jax.ShapeDtypeStruct((n,) + tail, F32 if r == 0 else BF) for r in range(NX)],
        compiler_params=params(),
        name="core_sum",
    )(sc, *args)


def x_sum_body(counts, sc, *refs):
    outs, held = refs[-5:-1], refs[-1]
    at, p = 0, 0
    for n in counts:
        for k in range(n):
            held[sc[SLOT + p]] = sum(refs[at + r][k].astype(F32) for r in range(NX))
            p += 1
        at += NX
    for r in range(NY):
        outs[r][...] = held[r].astype(outs[r].dtype)


def x_sum(sc, groups):
    tail = groups[0][0].shape[1:]
    args = [v for group in groups for v in group]
    one = pl.BlockSpec(tail, lambda i, s: (0, 0))
    return pl.pallas_call(
        functools.partial(x_sum_body, [g[0].shape[0] for g in groups]),
        grid_spec=pltpu.PrefetchScalarGridSpec(
            num_scalar_prefetch=1,
            grid=(1,),
            in_specs=[pl.BlockSpec(v.shape, lambda i, s: (0, 0, 0)) for v in args],
            out_specs=[one] * 4,
            scratch_shapes=[pltpu.VMEM((NY,) + tail, F32)],
        ),
        out_shape=[jax.ShapeDtypeStruct(tail, F32 if r == 0 else BF) for r in range(NY)],
        compiler_params=params(),
        name="x_sum",
    )(sc, *args)


def update_body(g0, g1, g2, g3, w, mom, var, err, mom_out, err_out, dir_out, sums):
    gradient = (
        g0[...] + g1[...].astype(F32) + g2[...].astype(F32) + g3[...].astype(F32)
    )
    momentum = 0.9 * mom[...] + 0.1 * gradient
    mom_out[...] = momentum
    held = momentum + err[...]
    level = jnp.sum(jnp.abs(held), axis=(0, 1), keepdims=True) * (1.0 / held.size) + 1e-06
    squeezed = level * jnp.tanh(held / level)
    err_out[...] = held - squeezed
    direction = (squeezed / (jnp.sqrt(var[...]) + 1e-06)).astype(BF)
    dir_out[...] = direction
    wf = w[...].astype(F32)
    df = direction.astype(F32)
    total_w = jnp.sum(wf * wf, axis=(0, 1), keepdims=True)
    total_d = jnp.sum(df * df, axis=(0, 1), keepdims=True)
    row = lax.broadcasted_iota(jnp.int32, sums.shape, 0)
    sums[...] = jnp.where(row == 0, total_w, total_d)


def update(mine, got, weight, momentum, variance, server_error):
    shape = weight.shape
    one = pl.BlockSpec(shape, lambda i: (0, 0))
    return pl.pallas_call(
        update_body,
        grid=(1,),
        in_specs=[one] * 8,
        out_specs=[one, one, one, pl.BlockSpec((8, 128), lambda i: (0, 0))],
        out_shape=[
            jax.ShapeDtypeStruct(shape, F32),
            jax.ShapeDtypeStruct(shape, F32),
            jax.ShapeDtypeStruct(shape, BF),
            jax.ShapeDtypeStruct((8, 128), F32),
        ],
        compiler_params=params(),
        name="update",
    )(mine, *got, weight, momentum, variance, server_error)


def forward_body(n_parts, ending, sc, *refs):
    n = sum(n_parts)
    pieces, b_hbm = refs[:n], refs[n]
    base = refs[n + 1 : n + 3] if ending else ()
    out, a_held, b_held, a_sems, b_sems = refs[-5:]
    rows = b_held.shape[1]
    waits = []
    at = 0
    for k, parts in enumerate(n_parts):
        wide = rows // parts
        mine = []
        for j in range(parts):
            target = a_held.at[k] if parts == 1 else a_held.at[k, :, j * wide : (j + 1) * wide]
            mine.append(pltpu.make_async_copy(pieces[at], target, a_sems.at[at]))
            at += 1
        if len(b_hbm.shape) == 5:
            for i in range(4):
                target = b_held.at[k, i * (rows // 4) : (i + 1) * (rows // 4)]
                mine.append(pltpu.make_async_copy(b_hbm.at[sc[k], i, 0], target, b_sems.at[k]))
        else:
            mine.append(pltpu.make_async_copy(b_hbm.at[sc[k]], b_held.at[k], b_sems.at[k]))
        for copy in mine:
            copy.start()
        waits.append(mine)
    total = None
    for k, mine in enumerate(waits):
        for copy in mine:
            copy.wait()
        part = jnp.dot(a_held[k], b_held[k], preferred_element_type=F32)
        total = part if total is None else total + part
    if ending:
        total = base[0][...] - base[1][0:1, 0:1] * total
    out[...] = total.astype(out.dtype)


def forward(sc, parts, matrix, base=None, scale=None):
    tokens = parts[0][0].shape[0]
    rows, cols = parts[0][0].shape[1], matrix.shape[-1]
    args = [v for part in parts for v in part]
    n = len(args)
    args = args + [matrix]
    in_specs = [pl.BlockSpec(memory_space=pl.ANY)] * (n + 1)
    if base is not None:
        args += [base, scale]
        in_specs += [
            pl.BlockSpec((tokens, cols), lambda i, s: (0, 0)),
            pl.BlockSpec(scale.shape, lambda i, s: (0, 0)),
        ]
    return pl.pallas_call(
        functools.partial(forward_body, [len(p) for p in parts], base is not None),
        grid_spec=pltpu.PrefetchScalarGridSpec(
            num_scalar_prefetch=1,
            grid=(1,),
            in_specs=in_specs,
            out_specs=pl.BlockSpec((tokens, cols), lambda i, s: (0, 0)),
            scratch_shapes=[
                pltpu.VMEM((NZ, tokens, rows), BF),
                pltpu.VMEM((NZ, rows, cols), BF),
                pltpu.SemaphoreType.DMA((n,)),
                pltpu.SemaphoreType.DMA((NZ,)),
            ],
        ),
        out_shape=jax.ShapeDtypeStruct((tokens, cols), F32 if base is None else BF),
        compiler_params=params(),
        cost_estimate=pl.CostEstimate(
            flops=2 * NZ * tokens * cols * rows, bytes_accessed=2 * matrix.size * 3, transcendentals=0
        ),
        name="forward",
    )(sc, *args)


def input_grad_body(sc, og, w, out, acc):
    j = pl.program_id(0)
    wide = jnp.concatenate([w[0, i, 0] for i in range(4)])
    part = lax.dot_general(og[0], wide, (((1,), (1,)), ((), ())), preferred_element_type=F32)

    @pl.when(j == 0)
    def _():
        acc[...] = part

    @pl.when(j > 0)
    def _():
        acc[...] += part

    @pl.when(j == NZ - 1)
    def _():
        out[...] = acc[...].astype(BF)


def input_grad_of(sc, og_all, both):
    _, tokens, cols = og_all.shape
    width = 4 * both.shape[3]
    return pl.pallas_call(
        input_grad_body,
        grid_spec=pltpu.PrefetchScalarGridSpec(
            num_scalar_prefetch=1,
            grid=(NZ,),
            in_specs=[
                pl.BlockSpec((1, tokens, cols), lambda j, s: (lax.rem(j - s[0] + NZ, NZ), 0, 0)),
                pl.BlockSpec((1, 4, 1, width // 4, cols), lambda j, s: (j, 0, 1, 0, 0)),
            ],
            out_specs=pl.BlockSpec((tokens, width), lambda j, s: (0, 0)),
            scratch_shapes=[pltpu.VMEM((tokens, width), F32)],
        ),
        out_shape=jax.ShapeDtypeStruct((tokens, width), BF),
        compiler_params=params(),
        cost_estimate=pl.CostEstimate(
            flops=2 * NZ * tokens * cols * width, bytes_accessed=2 * og_all.size, transcendentals=0
        ),
        name="input_grad",
    )(sc, og_all, both)


def shards(inputs, out_grad, weight, momentum, variance, server_error, worker_error):
    groups = lax.axis_size("dp")
    factor = 1.0 / math.sqrt(inputs.shape[0] * groups)
    rows, cols = weight.shape
    z = lax.axis_index("mp")
    d = lax.axis_index("dp")
    y, x, core = d // (NX * NC), (d // NC) % NX, d % NC
    parity = z % 2
    sign = 1 - 2 * parity
    wide = inputs.shape[1] // 2

    spread_perm, along_perm = [], []
    for dp in range(32):
        yy, xx, cc = coords(dp)
        for zz in range(NZ):
            row = 2 * yy + xx // 2
            place = (row + zz) % NZ
            to = flat_dp(place // 2, 2 * (place % 2) + xx % 2, cc)
            spread_perm.append((dp * NZ + zz, to * NZ + zz))
            along_perm.append((to * NZ + zz, to * NZ + row))

    def near(a):
        return lax.ppermute(a, "mp", NEAR)

    def away(a):
        return lax.ppermute(a, "mp", FAR)

    def at(k):
        return lax.rem(z + k * sign + 2 * NZ, NZ)

    ms = [at(0), at(1), at(-1), at(-2), at(2), at(3), at(-3), at(4)]
    slots = [lax.rem(ms[k] // 2 - y + NY, NY) for k in (0, 3, 4, 7)]
    sc = jnp.stack(ms + [core, x, parity] + slots).astype(jnp.int32)
    tie = lax.optimization_barrier

    def grad(parts, ks, wn):
        return shard_grad(sc, parts, ks, out_grad, worker_error, wn, factor)

    def swap(send):
        return lax.ppermute(send, "dp", xor_perm(32, 1))

    def spread(mine):
        return [mine[0]] + [lax.ppermute(mine[r], "dp", x_shift(r)) for r in (1, 2, 3)]

    moved = lax.ppermute(weight, ("dp", "mp"), spread_perm)
    moved = lax.ppermute(moved, ("dp", "mp"), along_perm)
    u1, v1 = near(inputs), away(inputs)
    u1, v1, moved = tie((u1, v1, moved))

    both = lax.all_gather(jnp.concatenate([weight, moved]), "dp", axis=0, tiled=True)
    both = both.reshape(NZ, 4, 2, rows, cols)
    u2, v2 = near(v1), away(u1)
    wn, keep0, send0 = grad([(inputs,)], [0], None)
    recv0 = swap(send0)
    wn, keep1, send1 = grad([(u1,), (v1,)], [1, 2], wn)
    recv1 = swap(send1)
    u2, v2, wn, recv0, recv1 = tie((u2, v2, wn, recv0, recv1))

    u3, v3 = near(v2), away(u2)
    wn, keep2, send2 = grad([(v2,), (u2,)], [3, 4], wn)
    recv2 = swap(send2)
    sums01 = core_sum(
        sc,
        [
            ((keep0, recv0, 0), (keep1, recv1, 0)),
            ((keep2, recv2, 0), (keep1, recv1, 1)),
        ],
    )
    u3, v3, wn, sums01 = tie((u3, v3, wn, sums01))

    g0, g1, wn = tie((v3[:, :wide], u3[:, wide:], wn))
    f0, f1 = near(g0), away(g1)
    wn, keep3, send3 = grad([(u3,), (v3,)], [5, 6], wn)
    f0, f1, wn, send3, later = tie((f0, f1, wn, send3, out_grad))

    og_all = lax.all_gather(later, "mp", axis=0, tiled=False)
    blocks01 = spread(sums01)
    recv3 = swap(send3)
    wn, keep4, send4 = grad([(f0, f1)], [7], wn)
    recv4 = swap(send4)
    sums23 = core_sum(
        sc,
        [
            ((keep2, recv2, 1), (keep3, recv3, 0)),
            ((keep4, recv4, 0), (keep3, recv3, 1)),
        ],
    )
    blocks23 = spread(sums23)
    parts = [(inputs,), (u1,), (v1,), (v2,), (u2,), (u3,), (v3,), (f0, f1)]
    base = forward(sc, parts, both)
    blocks23, base = tie((blocks23, base))
    by_y = x_sum(sc, [blocks01, blocks23])
    got = [lax.ppermute(by_y[r], "dp", y_shift(r)) for r in (1, 2, 3)]
    momentum_next, server_next, direction, sums = update(
        by_y[0], got, weight, momentum, variance, server_error
    )
    directions = lax.all_gather(direction, "dp", axis=0, tiled=True)
    for axis, n, bit in (
        ("dp", 32, 1),
        ("dp", 32, 2),
        ("dp", 32, 4),
        ("dp", 32, 8),
        ("dp", 32, 16),
        ("mp", NZ, 1),
        ("mp", NZ, 2),
        ("mp", NZ, 4),
    ):
        sums = sums + lax.ppermute(sums, axis, xor_perm(n, bit))
    ratio = jnp.sqrt(sums[0:1] / (sums[1:2] + 1e-12))

    input_grad = input_grad_of(sc, og_all, both)

    refreshed = forward(sc, parts, directions.reshape(NZ, 4 * rows, cols), base, 0.25 * ratio)
    return (input_grad, momentum_next, server_next, wn, refreshed)


def solution(mesh):
    return jax.shard_map(
        shards,
        mesh=mesh,
        in_specs=(
            P("dp", "mp"),
            P("dp", "mp"),
            P("dp", "mp"),
            P("dp", "mp"),
            P("dp", "mp"),
            P("dp", "mp"),
            P("dp", None, "mp"),
        ),
        out_specs=(P("dp", "mp"), P("dp", "mp"), P("dp", "mp"), P("dp", None, "mp"), P("dp", "mp")),
        check_vma=False,
    )
```

time: 283 us -> 217 us (0.77)
  local copies, waits for them, and re-layouts: 38.1 us -> 3.76 us
  starting transfers between devices: 67.9 us -> 40.5 us
  waiting for transfers between devices: 90.4 us -> 85.1 us
    unnamed x118 -> x46, local copies, waits for them, and re-layouts: 36.3 us -> 2.99 us
    ppermute x20 -> x16, starting transfers between devices: 45.9 us -> 18.7 us  [the longest x6 10 us: spread(): lax.ppermute(mine[r], 'dp', x_shift(r))]
    ppermute x4, waiting for transfers between devices: 29.6 us -> 9.98 us  [near(): return lax.ppermute(a, 'mp', NEAR)]
    ppermute x20 -> x16, waiting for transfers between devices: 7.02 us -> 24.5 us  [the longest x6 12.5 us: spread(): lax.ppermute(mine[r], 'dp', x_shift(r))]
    ppermute x8, waiting for transfers between devices: 29.3 us -> 21.1 us  [shards(): sums = sums + lax.ppermute(sums, axis, xor_perm(n, bit))]
    all_gather x1, waiting for transfers between devices: 0.01 us -> 7.93 us  [shards(): directions = lax.all_gather(direction, 'dp', axis=0, tiled=True)]
    ppermute x4, starting transfers between devices: 14.4 us -> 10.2 us  [away(): return lax.ppermute(a, 'mp', FAR)]
    ppermute x8, starting transfers between devices: 5.36 us -> 8.53 us  [shards(): sums = sums + lax.ppermute(sums, axis, xor_perm(n, bit))]
  transfers between devices with their start and end apart: 40 -> 35, of which waited for: 16 -> 24; matrix products, arithmetic and copies ran while one was open for 2% -> 1% of each run, Pallas kernels for 21% -> 28%
where the time goes in v2:
time: 217 us; the launch traced here: 214 us
  waiting for transfers between devices  85.1 us (39%)
  Pallas kernels  67.8 us (31%)
  starting transfers between devices  40.5 us (19%)
  between operations  14 us (6%)
  local copies, waits for them, and re-layouts  3.76 us (2%)
  other arithmetic  3.02 us (1%)
    pallas_call x5, Pallas kernels, shard_grad(): pl.pallas_call(functools.partial(shard_body, [len(p) for p in parts], ks,...  27.5 us
    ppermute x4, waiting for transfers between devices, away(): return lax.ppermute(a, 'mp', FAR)  21.7 us
    ppermute x8, waiting for transfers between devices, shards(): sums = sums + lax.ppermute(sums, axis, xor_perm(n, bit))  21.1 us
    pallas_call x2, Pallas kernels, forward(): pl.pallas_call(functools.partial(forward_body, [len(p) for p in parts], b...  16.4 us
    ppermute x6, waiting for transfers between devices, spread(): lax.ppermute(mine[r], 'dp', x_shift(r))  12.5 us
    pallas_call x1, Pallas kernels, input_grad_of(): pl.pallas_call(input_grad_body, grid_spec=pltpu.PrefetchScalarGridSpec(nu...  10.4 us
    ppermute x4, starting transfers between devices, away(): return lax.ppermute(a, 'mp', FAR)  10.2 us
    ppermute x6, starting transfers between devices, spread(): lax.ppermute(mine[r], 'dp', x_shift(r))  10 us
  transfers between devices with their start and end apart: 35, of which 24 were waited for; matrix products, arithmetic and copies ran while one was open for 1% of the time, Pallas kernels for 28%

profile of v2, /device:TPU:2, one launch (start us, length us, event | category | flops | bytes accessed | tf_op | source)
XLA Modules:
  0.0 214.2 jit_solution(6587451817370969638)
XLA Ops:
  7.2 5.9 %collective-permute-start.1 = (bf16[512,768]{1,0:T(8,128)(2,1)}, bf16[512,768]{1,0:T(8,128)(2,1)S(1)}, u32[]{:S(2)}, u32[]{:S(2)}) collective-permute-start(bf16[512,768]{1,0:T(8,128)(2,1)} %refs_0_.5), channel_id=1, source_target_pairs={{0,7},{1,2},{2,1},{3,4},{4,3},{5,6},{6,5},{7,0},{8,15},{9,10},{10,... | collective-permute-start | bytes 2359304 | tf_op jit(solution)/shard_map/ppermute | solution.py:370
  13.2 1.6 collective-permute-start.2
  14.7 0.7 collective-permute-start.3
  15.4 17.0 %collective-permute-done.1.refs_1_.refs_2_ = bf16[512,768]{1,0:T(8,128)(2,1)S(1)} collective-permute-done((bf16[512,768]{1,0:T(8,128)(2,1)}, bf16[512,768]{1,0:T(8,128)(2,1)S(1)}, u32[]{:S(2)}, u32[]{:S(2)}) %collective-permute-start.1) | collective-permute-done | bytes 786464 | tf_op jit(solution)/shard_map/ppermute | solution.py:370
  32.4 4.2 %collective-permute-done.refs_0_.refs_1_ = bf16[512,768]{1,0:T(8,128)(2,1)S(1)} collective-permute-done((bf16[512,768]{1,0:T(8,128)(2,1)}, bf16[512,768]{1,0:T(8,128)(2,1)S(1)}, u32[]{:S(2)}, u32[]{:S(2)}) %collective-permute-start) | collective-permute-done | bytes 786464 | tf_op jit(solution)/shard_map/ppermute | solution.py:367
  36.7 1.8 pad_maximum_fusion
  38.5 2.5 %collective-permute-start.4 = (bf16[512,768]{1,0:T(8,128)(2,1)S(1)}, bf16[512,768]{1,0:T(8,128)(2,1)S(1)}, u32[]{:S(2)}, u32[]{:S(2)}) collective-permute-start(bf16[512,768]{1,0:T(8,128)(2,1)S(1)} %collective-permute-done.1.refs_1_.refs_2_), channel_id=1, source_target_pairs={{0,1},{1,0},{2,3},{3,2},{4,5},{5,4},{6,7},{7,6},{8,9},{9,8},{10,11... | collective-permute-start | bytes 2359304 | tf_op jit(solution)/shard_map/ppermute | solution.py:367
  41.0 1.2 collective-permute-start.5
  42.2 0.7 stack.63.sc
  42.9 4.1 %shard_grad.5 = (bf16[1,6144,384]{2,1,0:T(8,128)(2,1)}, bf16[2,192,384]{2,1,0:T(8,128)(2,1)}, bf16[2,192,384]{2,1,0:T(8,128)(2,1)}) custom-call(s32[15]{0:T(128)} %stack.63.sc, bf16[512,768]{1,0:T(8,128)(2,1)} %refs_0_.5, bf16[512,384]{1,0:T(8,128)(2,1)} %refs_2_.9, bf16[1,6144,384]{2,1,0:T(8,128)(2,1)} %refs_3_.7), custom_call_target="tpu_custom_call" | custom-call | flops 301989888 | bytes 1769472 | tf_op jit(solution)/shard_map/shard_grad/pallas_call | solution.py:109
  47.1 6.5 %shard_grad.6 = (bf16[1,6144,384]{2,1,0:T(8,128)(2,1)}, bf16[4,192,384]{2,1,0:T(8,128)(2,1)}, bf16[4,192,384]{2,1,0:T(8,128)(2,1)}) custom-call(s32[15]{0:T(128)} %stack.63.sc, bf16[512,768]{1,0:T(8,128)(2,1)} %copy-done.3, bf16[512,768]{1,0:T(8,128)(2,1)} %copy-done.2, bf16[512,384]{1,0:T(8,128)(2,1)} %refs_2_.9, ...), custom_call_target="tpu_custom_call", output_to_operand_aliasing={{0}: (5, {})} | custom-call | flops 603979776 | bytes 3538944 | tf_op jit(solution)/shard_map/shard_grad/pallas_call | solution.py:109
  54.0 1.9 collective-permute-done.6.refs_1_
  55.9 1.8 collective-permute-done.4.refs_1_.refs_4_
  57.7 2.7 %collective-permute-done.5.refs_0_.refs_3_ = bf16[512,768]{1,0:T(8,128)(2,1)S(1)} collective-permute-done((bf16[512,768]{1,0:T(8,128)(2,1)S(1)}, bf16[512,768]{1,0:T(8,128)(2,1)S(1)}, u32[]{:S(2)}, u32[]{:S(2)}) %collective-permute-start.5) | collective-permute-done | bytes 786464 | tf_op jit(solution)/shard_map/ppermute | solution.py:370
  60.4 1.1 collective-permute-start.9
  61.4 6.3 %shard_grad.7 = (bf16[1,6144,384]{2,1,0:T(8,128)(2,1)}, bf16[4,192,384]{2,1,0:T(8,128)(2,1)}, bf16[4,192,384]{2,1,0:T(8,128)(2,1)}) custom-call(s32[15]{0:T(128)} %stack.63.sc, bf16[512,768]{1,0:T(8,128)(2,1)} %copy-done.5, bf16[512,768]{1,0:T(8,128)(2,1)} %copy-done.4, bf16[512,384]{1,0:T(8,128)(2,1)} %refs_2_.9, ...), custom_call_target="tpu_custom_call", output_to_operand_aliasing={{0}: (5, {})} | custom-call | flops 603979776 | bytes 3538944 | tf_op jit(solution)/shard_map/shard_grad/pallas_call | solution.py:109
  67.7 2.3 %collective-permute-done.10.refs_5_.refs_1_ = bf16[4,192,384]{2,1,0:T(8,128)(2,1)} collective-permute-done((bf16[4,192,384]{2,1,0:T(8,128)(2,1)}, bf16[4,192,384]{2,1,0:T(8,128)(2,1)}, u32[]{:S(2)}, u32[]{:S(2)}) %collective-permute-start.10) | collective-permute-done | bytes 589856 | tf_op jit(solution)/shard_map/ppermute | solution.py:384
  70.1 3.6 %core_sum.2 = (f32[2,192,384]{2,1,0:T(8,128)}, bf16[2,192,384]{2,1,0:T(8,128)(2,1)}, bf16[2,192,384]{2,1,0:T(8,128)(2,1)}, bf16[2,192,384]{2,1,0:T(8,128)(2,1)}) custom-call(s32[15]{0:T(128)} %stack.63.sc, bf16[2,192,384]{2,1,0:T(8,128)(2,1)} %get-tuple-element.74.refs_0_, bf16[2,192,384]{2,1,0:T(8,128)(2,1)} %copy-done.14, ...), custom_call_target="tpu_custom_call" | custom-call | tf_op jit(solution)/shard_map/core_sum/pallas_call | solution.py:151
  73.6 4.0 %collective-permute-done.8.refs_0_.refs_5_ = bf16[512,768]{1,0:T(8,128)(2,1)S(1)} collective-permute-done((bf16[512,768]{1,0:T(8,128)(2,1)S(1)}, bf16[512,768]{1,0:T(8,128)(2,1)S(1)}, u32[]{:S(2)}, u32[]{:S(2)}) %collective-permute-start.8) | collective-permute-done | bytes 786464 | tf_op jit(solution)/shard_map/ppermute | solution.py:367
  77.6 1.3 collective-permute-done.9.refs_1_.refs_6_
  79.0 0.5 collective-permute-start.11
  79.6 2.0 collective-permute-start.12
  81.5 6.4 %shard_grad.8 = (bf16[1,6144,384]{2,1,0:T(8,128)(2,1)}, bf16[4,192,384]{2,1,0:T(8,128)(2,1)}, bf16[4,192,384]{2,1,0:T(8,128)(2,1)}) custom-call(s32[15]{0:T(128)} %stack.63.sc, bf16[512,768]{1,0:T(8,128)(2,1)} %copy-done, bf16[512,768]{1,0:T(8,128)(2,1)} %copy-done.1, bf16[512,384]{1,0:T(8,128)(2,1)} %refs_2_.9, ...), custom_call_target="tpu_custom_call", output_to_operand_aliasing={{0}: (5, {})} | custom-call | flops 603979776 | bytes 3538944 | tf_op jit(solution)/shard_map/shard_grad/pallas_call | solution.py:109
  87.9 0.7 collective-permute-done.12.refs_1_.refs_8_
  88.7 0.5 copy-done.7
  89.3 4.3 %shard_grad.9 = (bf16[1,6144,384]{2,1,0:T(8,128)(2,1)}, bf16[2,192,384]{2,1,0:T(8,128)(2,1)}, bf16[2,192,384]{2,1,0:T(8,128)(2,1)}) custom-call(s32[15]{0:T(128)} %stack.63.sc, bf16[512,384]{1,0:T(8,128)(2,1)} %copy-done.6, bf16[512,384]{1,0:T(8,128)(2,1)} %copy-done.7, bf16[512,384]{1,0:T(8,128)(2,1)} %refs_2_.9, ...), custom_call_target="tpu_custom_call", output_to_operand_aliasing={{0}: (5, {})} | custom-call | flops 301989888 | bytes 1769472 | tf_op jit(solution)/shard_map/shard_grad/pallas_call | solution.py:109
  93.6 1.8 collective-permute-done.17.refs_5_
  95.4 0.7 copy-done.17
  96.4 3.5 %core_sum.3 = (f32[2,192,384]{2,1,0:T(8,128)}, bf16[2,192,384]{2,1,0:T(8,128)(2,1)}, bf16[2,192,384]{2,1,0:T(8,128)(2,1)}, bf16[2,192,384]{2,1,0:T(8,128)(2,1)}) custom-call(s32[15]{0:T(128)} %stack.63.sc, bf16[4,192,384]{2,1,0:T(8,128)(2,1)} %get-tuple-element.78.refs_4_.refs_0_, bf16[4,192,384]{2,1,0:T(8,128)(2,1)} %collective-permute-done.10.refs_5_.refs_1_, ...), custom_call_target="tpu_custom_call" | custom-call | tf_op jit(solution)/shard_map/core_sum/pallas_call | solution.py:151
  99.9 1.5 collective-permute-start.18
  101.4 1.2 collective-permute-start.19
  102.5 2.1 collective-permute-start.20
  104.6 3.5 %collective-permute-start.14 = (bf16[2,192,384]{2,1,0:T(8,128)(2,1)}, bf16[2,192,384]{2,1,0:T(8,128)(2,1)S(1)}, u32[]{:S(2)}, u32[]{:S(2)}) collective-permute-start(bf16[2,192,384]{2,1,0:T(8,128)(2,1)} %get-tuple-element.96), channel_id=1, source_target_pairs={{0,32},{8,40},{16,48},{24,56},{32,0},{40,8},{48,16},{56,24},{64,96... | collective-permute-start | bytes 884744 | tf_op jit(solution)/shard_map/ppermute | solution.py:387
  108.2 1.8 collective-permute-done.18.refs_5_
  109.9 1.8 collective-permute-start.15
  111.7 8.0 %forward.2.refs_10_ = f32[512,384]{1,0:T(8,128)} custom-call(s32[15]{0:T(128)} %stack.63.sc, bf16[512,768]{1,0:T(8,128)(2,1)} %refs_0_.5, bf16[512,768]{1,0:T(8,128)(2,1)} %copy-done.3, bf16[512,768]{1,0:T(8,128)(2,1)} %copy-done.2, bf16[512,768]{1,0:T(8,128)(2,1)} %copy-done.5, bf16[512,768]{1,0:T(8,128)(2,1)} %copy-done.4, bf16[512,768]{1,0:T(8,128)(2,1)} %copy-done, ...), custom_call_target="tpu_custom_call" | custom-call | flops 2415919104 | bytes 28311552 | tf_op jit(solution)/shard_map/forward/pallas_call | solution.py:280
  119.8 2.8 %collective-permute-done.13.refs_1_ = bf16[2,192,384]{2,1,0:T(8,128)(2,1)S(1)} collective-permute-done((bf16[2,192,384]{2,1,0:T(8,128)(2,1)}, bf16[2,192,384]{2,1,0:T(8,128)(2,1)S(1)}, u32[]{:S(2)}, u32[]{:S(2)}) %collective-permute-start.13) | collective-permute-done | bytes 294944 | tf_op jit(solution)/shard_map/ppermute | solution.py:387
  122.6 3.1 %collective-permute-done.14.refs_2_ = bf16[2,192,384]{2,1,0:T(8,128)(2,1)S(1)} collective-permute-done((bf16[2,192,384]{2,1,0:T(8,128)(2,1)}, bf16[2,192,384]{2,1,0:T(8,128)(2,1)S(1)}, u32[]{:S(2)}, u32[]{:S(2)}) %collective-permute-start.14) | collective-permute-done | bytes 294944 | tf_op jit(solution)/shard_map/ppermute | solution.py:387
  125.7 4.9 %collective-permute-done.15.refs_3_ = bf16[2,192,384]{2,1,0:T(8,128)(2,1)S(1)} collective-permute-done((bf16[2,192,384]{2,1,0:T(8,128)(2,1)S(1)}, bf16[2,192,384]{2,1,0:T(8,128)(2,1)S(1)}, u32[]{:S(2)}, u32[]{:S(2)}) %collective-permute-start.15) | collective-permute-done | bytes 294944 | tf_op jit(solution)/shard_map/ppermute | solution.py:387
  130.6 0.7 copy-done.16
  131.3 3.7 %x_sum.1 = (f32[192,384]{1,0:T(8,128)}, bf16[192,384]{1,0:T(8,128)(2,1)}, bf16[192,384]{1,0:T(8,128)(2,1)}, bf16[192,384]{1,0:T(8,128)(2,1)}) custom-call(s32[15]{0:T(128)} %stack.63.sc, f32[2,192,384]{2,1,0:T(8,128)} %get-tuple-element.94.refs_0_, bf16[2,192,384]{2,1,0:T(8,128)(2,1)} %copy-done.13, bf16[2,192,384]{2,1,0:T(8,128)(2,1)} %copy-done.15, ...), custom_call_target="tpu_custom_call" | custom-call | tf_op jit(solution)/shard_map/x_sum/pallas_call | solution.py:178
  134.9 0.7 collective-permute-start.21
  135.7 3.7 %collective-permute-start.22 = (bf16[192,384]{1,0:T(8,128)(2,1)}, bf16[192,384]{1,0:T(8,128)(2,1)S(1)}, u32[]{:S(2)}, u32[]{:S(2)}) collective-permute-start(bf16[192,384]{1,0:T(8,128)(2,1)} %get-tuple-element.115), channel_id=1, source_target_pairs={{0,128},{8,136},{16,144},{24,152},{32,160},{40,168},{48,176},{56,1... | collective-permute-start | bytes 442376 | tf_op jit(solution)/shard_map/ppermute | solution.py:437
  139.4 1.3 collective-permute-start.23
  140.7 1.5 collective-permute-done.21.g1
  142.3 4.3 %collective-permute-done.22.g2 = bf16[192,384]{1,0:T(8,128)(2,1)S(1)} collective-permute-done((bf16[192,384]{1,0:T(8,128)(2,1)}, bf16[192,384]{1,0:T(8,128)(2,1)S(1)}, u32[]{:S(2)}, u32[]{:S(2)}) %collective-permute-start.22) | collective-permute-done | bytes 147488 | tf_op jit(solution)/shard_map/ppermute | solution.py:437
  146.6 0.6 copy-done.19
  147.3 2.8 %update.1 = (f32[192,384]{1,0:T(8,128)}, f32[192,384]{1,0:T(8,128)}, bf16[192,384]{1,0:T(8,128)(2,1)}, f32[8,128]{1,0:T(8,128)}) custom-call(f32[192,384]{1,0:T(8,128)} %get-tuple-element.113.g0, bf16[192,384]{1,0:T(8,128)(2,1)} %copy-done.18, bf16[192,384]{1,0:T(8,128)(2,1)} %copy-done.19, bf16[192,384]{1,0:T(8,128)(2,1)} %copy-done.20, ...), custom_call_target="tpu_custom_call" | custom-call | tf_op jit(solution)/shard_map/update/pallas_call | solution.py:216
  150.2 1.4 collective-permute-done.24
  151.6 0.7 add.125
  152.5 3.3 %collective-permute-done.25 = f32[8,128]{1,0:T(8,128)S(1)} collective-permute-done((f32[8,128]{1,0:T(8,128)S(1)}, f32[8,128]{1,0:T(8,128)S(1)}, u32[]{:S(2)}, u32[]{:S(2)}) %collective-permute-start.25) | collective-permute-done | bytes 4128 | tf_op jit(solution)/shard_map/ppermute | solution.py:452
  155.8 1.7 collective-permute-start.26
  157.6 3.4 %collective-permute-done.26 = f32[8,128]{1,0:T(8,128)S(1)} collective-permute-done((f32[8,128]{1,0:T(8,128)S(1)}, f32[8,128]{1,0:T(8,128)S(1)}, u32[]{:S(2)}, u32[]{:S(2)}) %collective-permute-start.26) | collective-permute-done | bytes 4128 | tf_op jit(solution)/shard_map/ppermute | solution.py:452
  161.0 1.1 collective-permute-start.27
  162.1 2.5 %collective-permute-done.27 = f32[8,128]{1,0:T(8,128)S(1)} collective-permute-done((f32[8,128]{1,0:T(8,128)S(1)}, f32[8,128]{1,0:T(8,128)S(1)}, u32[]{:S(2)}, u32[]{:S(2)}) %collective-permute-start.27) | collective-permute-done | bytes 4128 | tf_op jit(solution)/shard_map/ppermute | solution.py:452
  164.6 1.8 collective-permute-start.28
  166.4 3.3 %collective-permute-done.28 = f32[8,128]{1,0:T(8,128)S(1)} collective-permute-done((f32[8,128]{1,0:T(8,128)S(1)}, f32[8,128]{1,0:T(8,128)S(1)}, u32[]{:S(2)}, u32[]{:S(2)}) %collective-permute-start.28) | collective-permute-done | bytes 4128 | tf_op jit(solution)/shard_map/ppermute | solution.py:452
  170.1 3.2 %collective-permute-done.29 = f32[8,128]{1,0:T(8,128)S(1)} collective-permute-done((f32[8,128]{1,0:T(8,128)S(1)}, f32[8,128]{1,0:T(8,128)S(1)}, u32[]{:S(2)}, u32[]{:S(2)}) %collective-permute-start.29) | collective-permute-done | bytes 4128 | tf_op jit(solution)/shard_map/ppermute | solution.py:452
  173.8 4.0 %collective-permute-done.30 = f32[8,128]{1,0:T(8,128)S(1)} collective-permute-done((f32[8,128]{1,0:T(8,128)S(1)}, f32[8,128]{1,0:T(8,128)S(1)}, u32[]{:S(2)}, u32[]{:S(2)}) %collective-permute-start.30) | collective-permute-done | bytes 4128 | tf_op jit(solution)/shard_map/ppermute | solution.py:452
  177.8 2.6 %collective-permute-start.31 = (f32[8,128]{1,0:T(8,128)S(1)}, f32[8,128]{1,0:T(8,128)S(1)}, u32[]{:S(2)}, u32[]{:S(2)}) collective-permute-start(f32[8,128]{1,0:T(8,128)S(1)} %add.131), channel_id=1, source_target_pairs={{0,4},{1,5},{2,6},{3,7},{4,0},{5,1},{6,2},{7,3},{8,12},{9,13},{10,... | collective-permute-start | bytes 12296 | tf_op jit(solution)/shard_map/ppermute | solution.py:452
  180.4 10.4 %input_grad.1 = bf16[512,768]{1,0:T(8,128)(2,1)} custom-call(s32[15]{0:T(128)} %stack.63.sc, bf16[8,512,384]{2,1,0:T(8,128)(2,1)} %bitcast.21, bf16[8,4,2,192,384]{4,3,2,1,0:T(8,128)(2,1)} %bitcast.19), custom_call_target="tpu_custom_call" | custom-call | flops 2415919104 | bytes 3145728 | tf_op jit(solution)/shard_map/input_grad/pallas_call | solution.py:324
  190.8 0.5 sqrt_multiply_fusion.refs_11_
  191.3 7.9 %all-gather.7.cloned.1.call-done = bf16[6144,384]{1,0:T(8,128)(2,1)} async-done(((bf16[192,384]{1,0:T(8,128)(2,1)}), bf16[6144,384]{1,0:T(8,128)(2,1)}) %all-gather.7.cloned.1.call-update) | async-done | bytes 4718608 | tf_op jit(solution)/shard_map/all_gather | solution.py:441
  199.2 8.4 %forward.3 = bf16[512,384]{1,0:T(8,128)(2,1)} custom-call(s32[15]{0:T(128)} %stack.63.sc, bf16[512,768]{1,0:T(8,128)(2,1)} %refs_0_.5, bf16[512,768]{1,0:T(8,128)(2,1)} %copy-done.3, bf16[512,768]{1,0:T(8,128)(2,1)} %copy-done.2, bf16[512,768]{1,0:T(8,128)(2,1)} %copy-done.5, bf16[512,768]{1,0:T(8,128)(2,1)} %copy-done.4, bf16[512,768]{1,0:T(8,128)(2,1)} %copy-done, ...), custom_call_target="tpu_custom_call" | custom-call | flops 2415919104 | bytes 14155776 | tf_op jit(solution)/shard_map/forward/pallas_call | solution.py:280
  (80 shorter events, 2.7 us)
Async XLA Ops:
  7.2 104.6 %all-gather.5.cloned.1.call-start = ((), (), s32[]{:S(2)}) async-start(), calls=%async_computation | async-start | bytes 9732096 | tf_op jit(solution)/shard_map/all_gather | solution.py:394
  7.2 25.2 %collective-permute-start.1 = (bf16[512,768]{1,0:T(8,128)(2,1)}, bf16[512,768]{1,0:T(8,128)(2,1)S(1)}, u32[]{:S(2)}, u32[]{:S(2)}) collective-permute-start(bf16[512,768]{1,0:T(8,128)(2,1)} %refs_0_.5), channel_id=1, source_target_pairs={{0,7},{1,2},{2,1},{3,4},{4,3},{5,6},{6,5},{7,0},{8,15},{9,10},{10,... | collective-permute-start | bytes 2359304 | tf_op jit(solution)/shard_map/ppermute | solution.py:370
  13.2 23.5 %collective-permute-start = (bf16[512,768]{1,0:T(8,128)(2,1)}, bf16[512,768]{1,0:T(8,128)(2,1)S(1)}, u32[]{:S(2)}, u32[]{:S(2)}) collective-permute-start(bf16[512,768]{1,0:T(8,128)(2,1)} %refs_0_.5), channel_id=1, source_target_pairs={{0,1},{1,0},{2,3},{3,2},{4,5},{5,4},{6,7},{7,6},{8,9},{9,8},{10,11... | collective-permute-start | bytes 2359304 | tf_op jit(solution)/shard_map/ppermute | solution.py:367
  13.2 1.6 collective-permute-start.2
  14.7 0.7 collective-permute-start.3
  32.4 14.6 %copy-start.2 = (bf16[512,768]{1,0:T(8,128)(2,1)}, bf16[512,768]{1,0:T(8,128)(2,1)S(1)}, u32[]{:S(2)}) copy-start(bf16[512,768]{1,0:T(8,128)(2,1)S(1)} %collective-permute-done.1.refs_1_.refs_2_) | copy-start | bytes 2359300
  36.7 10.4 %copy-start.3 = (bf16[512,768]{1,0:T(8,128)(2,1)}, bf16[512,768]{1,0:T(8,128)(2,1)S(1)}, u32[]{:S(2)}) copy-start(bf16[512,768]{1,0:T(8,128)(2,1)S(1)} %collective-permute-done.refs_0_.refs_1_) | copy-start | bytes 2359300
  38.5 141.9 %all-gather.9.cloned.1.call-start = ((), (), s32[]{:S(2)}) async-start(), calls=%async_computation.2 | async-start | bytes 3538944 | tf_op jit(solution)/shard_map/all_gather | solution.py:420
  38.5 19.2 %collective-permute-start.4 = (bf16[512,768]{1,0:T(8,128)(2,1)S(1)}, bf16[512,768]{1,0:T(8,128)(2,1)S(1)}, u32[]{:S(2)}, u32[]{:S(2)}) collective-permute-start(bf16[512,768]{1,0:T(8,128)(2,1)S(1)} %collective-permute-done.1.refs_1_.refs_2_), channel_id=1, source_target_pairs={{0,1},{1,0},{2,3},{3,2},{4,5},{5,4},{6,7},{7,6},{8,9},{9,8},{10,11... | collective-permute-start | bytes 2359304 | tf_op jit(solution)/shard_map/ppermute | solution.py:367
  41.0 19.4 %collective-permute-start.5 = (bf16[512,768]{1,0:T(8,128)(2,1)S(1)}, bf16[512,768]{1,0:T(8,128)(2,1)S(1)}, u32[]{:S(2)}, u32[]{:S(2)}) collective-permute-start(bf16[512,768]{1,0:T(8,128)(2,1)S(1)} %collective-permute-done.refs_0_.refs_1_), channel_id=1, source_target_pairs={{0,7},{1,2},{2,1},{3,4},{4,3},{5,6},{6,5},{7,0},{8,15},{9,10},{10,... | collective-permute-start | bytes 2359304 | tf_op jit(solution)/shard_map/ppermute | solution.py:370
  47.0 6.5 %copy-start.22 = (bf16[2,192,384]{2,1,0:T(8,128)(2,1)S(1)}, bf16[2,192,384]{2,1,0:T(8,128)(2,1)}, u32[]{:S(2)}) copy-start(bf16[2,192,384]{2,1,0:T(8,128)(2,1)} %get-tuple-element.68) | copy-start | bytes 884740
  53.5 2.4 %collective-permute-start.7 = (bf16[4,192,384]{2,1,0:T(8,128)(2,1)}, bf16[4,192,384]{2,1,0:T(8,128)(2,1)S(1)}, u32[]{:S(2)}, u32[]{:S(2)}) collective-permute-start(bf16[4,192,384]{2,1,0:T(8,128)(2,1)} %get-tuple-element.69), channel_id=1, source_target_pairs={{0,8},{8,0},{16,24},{24,16},{32,40},{40,32},{48,56},{56,48},{64,72... | collective-permute-start | bytes 1769480 | tf_op jit(solution)/shard_map/ppermute | solution.py:384
  53.5 2.4 %collective-permute-start.6 = (bf16[2,192,384]{2,1,0:T(8,128)(2,1)S(1)}, bf16[2,192,384]{2,1,0:T(8,128)(2,1)S(1)}, u32[]{:S(2)}, u32[]{:S(2)}) collective-permute-start(bf16[2,192,384]{2,1,0:T(8,128)(2,1)S(1)} %copy-done.22), channel_id=1, source_target_pairs={{0,8},{8,0},{16,24},{24,16},{32,40},{40,32},{48,56},{56,48},{64,72... | collective-permute-start | bytes 884744 | tf_op jit(solution)/shard_map/ppermute | solution.py:384
  55.9 14.1 %copy-start.14 = (bf16[2,192,384]{2,1,0:T(8,128)(2,1)}, bf16[2,192,384]{2,1,0:T(8,128)(2,1)S(1)}, u32[]{:S(2)}) copy-start(bf16[2,192,384]{2,1,0:T(8,128)(2,1)S(1)} %collective-permute-done.6.refs_1_) | copy-start | bytes 884740
  55.9 4.4 %copy-start.8 = (bf16[4,192,384]{2,1,0:T(8,128)(2,1)}, bf16[4,192,384]{2,1,0:T(8,128)(2,1)S(1)}, u32[]{:S(2)}) copy-start(bf16[4,192,384]{2,1,0:T(8,128)(2,1)S(1)} %collective-permute-done.7.refs_3_.refs_7_) | copy-start | bytes 1769476
  57.7 3.7 %copy-start.4 = (bf16[512,768]{1,0:T(8,128)(2,1)}, bf16[512,768]{1,0:T(8,128)(2,1)S(1)}, u32[]{:S(2)}) copy-start(bf16[512,768]{1,0:T(8,128)(2,1)S(1)} %collective-permute-done.4.refs_1_.refs_4_) | copy-start | bytes 2359300
  60.4 1.1 copy-start.5
  60.4 17.2 %collective-permute-start.8 = (bf16[512,768]{1,0:T(8,128)(2,1)S(1)}, bf16[512,768]{1,0:T(8,128)(2,1)S(1)}, u32[]{:S(2)}, u32[]{:S(2)}) collective-permute-start(bf16[512,768]{1,0:T(8,128)(2,1)S(1)} %collective-permute-done.5.refs_0_.refs_3_), channel_id=1, source_target_pairs={{0,1},{1,0},{2,3},{3,2},{4,5},{5,4},{6,7},{7,6},{8,9},{9,8},{10,11... | collective-permute-start | bytes 2359304 | tf_op jit(solution)/shard_map/ppermute | solution.py:367
  60.4 18.5 %collective-permute-start.9 = (bf16[512,768]{1,0:T(8,128)(2,1)S(1)}, bf16[512,768]{1,0:T(8,128)(2,1)S(1)}, u32[]{:S(2)}, u32[]{:S(2)}) collective-permute-start(bf16[512,768]{1,0:T(8,128)(2,1)S(1)} %collective-permute-done.4.refs_1_.refs_4_), channel_id=1, source_target_pairs={{0,7},{1,2},{2,1},{3,4},{4,3},{5,6},{6,5},{7,0},{8,15},{9,10},{10,... | collective-permute-start | bytes 2359304 | tf_op jit(solution)/shard_map/ppermute | solution.py:370
  67.7 2.3 %collective-permute-start.10 = (bf16[4,192,384]{2,1,0:T(8,128)(2,1)}, bf16[4,192,384]{2,1,0:T(8,128)(2,1)}, u32[]{:S(2)}, u32[]{:S(2)}) collective-permute-start(bf16[4,192,384]{2,1,0:T(8,128)(2,1)} %get-tuple-element.79), channel_id=1, source_target_pairs={{0,8},{8,0},{16,24},{24,16},{32,40},{40,32},{48,56},{56,48},{64,72... | collective-permute-start | bytes 1769480 | tf_op jit(solution)/shard_map/ppermute | solution.py:384
  77.6 3.9 %copy-start = (bf16[512,768]{1,0:T(8,128)(2,1)}, bf16[512,768]{1,0:T(8,128)(2,1)S(1)}, u32[]{:S(2)}) copy-start(bf16[512,768]{1,0:T(8,128)(2,1)S(1)} %collective-permute-done.8.refs_0_.refs_5_) | copy-start | bytes 2359300
  78.9 2.6 %copy-start.1 = (bf16[512,768]{1,0:T(8,128)(2,1)}, bf16[512,768]{1,0:T(8,128)(2,1)S(1)}, u32[]{:S(2)}) copy-start(bf16[512,768]{1,0:T(8,128)(2,1)S(1)} %collective-permute-done.9.refs_1_.refs_6_) | copy-start | bytes 2359300
  79.0 8.9 %collective-permute-start.11 = (bf16[512,384]{1,0:T(8,128)(2,1)S(1)}, bf16[512,384]{1,0:T(8,128)(2,1)S(1)}, u32[]{:S(2)}, u32[]{:S(2)}) collective-permute-start(bf16[512,384]{1,0:T(8,128)(2,1)S(1)} %slice.12), channel_id=1, source_target_pairs={{0,1},{1,0},{2,3},{3,2},{4,5},{5,4},{6,7},{7,6},{8,9},{9,8},{10,11... | collective-permute-start | bytes 1179656 | tf_op jit(solution)/shard_map/ppermute | solution.py:367
  79.6 9.0 %collective-permute-start.12 = (bf16[512,384]{1,0:T(8,128)(2,1)S(1)}, bf16[512,384]{1,0:T(8,128)(2,1)S(1)}, u32[]{:S(2)}, u32[]{:S(2)}) collective-permute-start(bf16[512,384]{1,0:T(8,128)(2,1)S(1)} %slice.13), channel_id=1, source_target_pairs={{0,7},{1,2},{2,1},{3,4},{4,3},{5,6},{6,5},{7,0},{8,15},{9,10},{10,... | collective-permute-start | bytes 1179656 | tf_op jit(solution)/shard_map/ppermute | solution.py:370
  87.9 0.8 copy-start.6
  88.5 0.7 copy-start.7
  88.6 21.4 %copy-start.21 = (bf16[2,192,384]{2,1,0:T(8,128)(2,1)S(1)}, bf16[2,192,384]{2,1,0:T(8,128)(2,1)}, u32[]{:S(2)}) copy-start(bf16[2,192,384]{2,1,0:T(8,128)(2,1)} %get-tuple-element.97) | copy-start | bytes 884740
  88.6 110.7 %all-gather.7.cloned.1.call-start = ((), (), s32[]{:S(2)}) async-start(), calls=%async_computation.1 | async-start | bytes 4866048 | tf_op jit(solution)/shard_map/all_gather | solution.py:441
  88.6 6.8 %collective-permute-start.16 = (bf16[4,192,384]{2,1,0:T(8,128)(2,1)}, bf16[4,192,384]{2,1,0:T(8,128)(2,1)S(1)}, u32[]{:S(2)}, u32[]{:S(2)}) collective-permute-start(bf16[4,192,384]{2,1,0:T(8,128)(2,1)} %get-tuple-element.99), channel_id=1, source_target_pairs={{0,8},{8,0},{16,24},{24,16},{32,40},{40,32},{48,56},{56,48},{64,72... | collective-permute-start | bytes 1769480 | tf_op jit(solution)/shard_map/ppermute | solution.py:384
  93.5 1.9 collective-permute-start.17
  95.4 0.7 copy-start.17
  95.4 1.0 copy-start.9
  99.9 10.0 %collective-permute-start.18 = (bf16[2,192,384]{2,1,0:T(8,128)(2,1)}, bf16[2,192,384]{2,1,0:T(8,128)(2,1)S(1)}, u32[]{:S(2)}, u32[]{:S(2)}) collective-permute-start(bf16[2,192,384]{2,1,0:T(8,128)(2,1)} %get-tuple-element.106), channel_id=1, source_target_pairs={{0,16},{8,24},{16,32},{24,40},{32,48},{40,56},{48,0},{56,8},{64,80... | collective-permute-start | bytes 884744 | tf_op jit(solution)/shard_map/ppermute | solution.py:387
  101.4 18.3 %collective-permute-start.19 = (bf16[2,192,384]{2,1,0:T(8,128)(2,1)}, bf16[2,192,384]{2,1,0:T(8,128)(2,1)S(1)}, u32[]{:S(2)}, u32[]{:S(2)}) collective-permute-start(bf16[2,192,384]{2,1,0:T(8,128)(2,1)} %get-tuple-element.107), channel_id=1, source_target_pairs={{0,32},{8,40},{16,48},{24,56},{32,0},{40,8},{48,16},{56,24},{64,96... | collective-permute-start | bytes 884744 | tf_op jit(solution)/shard_map/ppermute | solution.py:387
  102.5 17.2 %collective-permute-start.20 = (bf16[2,192,384]{2,1,0:T(8,128)(2,1)}, bf16[2,192,384]{2,1,0:T(8,128)(2,1)S(1)}, u32[]{:S(2)}, u32[]{:S(2)}) collective-permute-start(bf16[2,192,384]{2,1,0:T(8,128)(2,1)} %get-tuple-element.108), channel_id=1, source_target_pairs={{0,48},{8,56},{16,0},{24,8},{32,16},{40,24},{48,32},{56,40},{64,11... | collective-permute-start | bytes 884744 | tf_op jit(solution)/shard_map/ppermute | solution.py:387
  104.6 18.0 %collective-permute-start.13 = (bf16[2,192,384]{2,1,0:T(8,128)(2,1)}, bf16[2,192,384]{2,1,0:T(8,128)(2,1)S(1)}, u32[]{:S(2)}, u32[]{:S(2)}) collective-permute-start(bf16[2,192,384]{2,1,0:T(8,128)(2,1)} %get-tuple-element.95), channel_id=1, source_target_pairs={{0,16},{8,24},{16,32},{24,40},{32,48},{40,56},{48,0},{56,8},{64,80... | collective-permute-start | bytes 884744 | tf_op jit(solution)/shard_map/ppermute | solution.py:387
  104.6 21.0 %collective-permute-start.14 = (bf16[2,192,384]{2,1,0:T(8,128)(2,1)}, bf16[2,192,384]{2,1,0:T(8,128)(2,1)S(1)}, u32[]{:S(2)}, u32[]{:S(2)}) collective-permute-start(bf16[2,192,384]{2,1,0:T(8,128)(2,1)} %get-tuple-element.96), channel_id=1, source_target_pairs={{0,32},{8,40},{16,48},{24,56},{32,0},{40,8},{48,16},{56,24},{64,96... | collective-permute-start | bytes 884744 | tf_op jit(solution)/shard_map/ppermute | solution.py:387
  109.9 9.8 %copy-start.10 = (bf16[2,192,384]{2,1,0:T(8,128)(2,1)}, bf16[2,192,384]{2,1,0:T(8,128)(2,1)S(1)}, u32[]{:S(2)}) copy-start(bf16[2,192,384]{2,1,0:T(8,128)(2,1)S(1)} %collective-permute-done.18.refs_5_) | copy-start | bytes 884740
  109.9 20.6 %collective-permute-start.15 = (bf16[2,192,384]{2,1,0:T(8,128)(2,1)S(1)}, bf16[2,192,384]{2,1,0:T(8,128)(2,1)S(1)}, u32[]{:S(2)}, u32[]{:S(2)}) collective-permute-start(bf16[2,192,384]{2,1,0:T(8,128)(2,1)S(1)} %copy-done.21), channel_id=1, source_target_pairs={{0,48},{8,56},{16,0},{24,8},{32,16},{40,24},{48,32},{56,40},{64,11... | collective-permute-start | bytes 884744 | tf_op jit(solution)/shard_map/ppermute | solution.py:387
  119.7 10.8 %copy-start.11 = (bf16[2,192,384]{2,1,0:T(8,128)(2,1)}, bf16[2,192,384]{2,1,0:T(8,128)(2,1)S(1)}, u32[]{:S(2)}) copy-start(bf16[2,192,384]{2,1,0:T(8,128)(2,1)S(1)} %collective-permute-done.19.refs_6_) | copy-start | bytes 884740
  119.8 10.8 %copy-start.12 = (bf16[2,192,384]{2,1,0:T(8,128)(2,1)}, bf16[2,192,384]{2,1,0:T(8,128)(2,1)S(1)}, u32[]{:S(2)}) copy-start(bf16[2,192,384]{2,1,0:T(8,128)(2,1)S(1)} %collective-permute-done.20.refs_7_) | copy-start | bytes 884740
  122.6 7.9 %copy-start.13 = (bf16[2,192,384]{2,1,0:T(8,128)(2,1)}, bf16[2,192,384]{2,1,0:T(8,128)(2,1)S(1)}, u32[]{:S(2)}) copy-start(bf16[2,192,384]{2,1,0:T(8,128)(2,1)S(1)} %collective-permute-done.13.refs_1_) | copy-start | bytes 884740
  125.7 4.9 %copy-start.15 = (bf16[2,192,384]{2,1,0:T(8,128)(2,1)}, bf16[2,192,384]{2,1,0:T(8,128)(2,1)S(1)}, u32[]{:S(2)}) copy-start(bf16[2,192,384]{2,1,0:T(8,128)(2,1)S(1)} %collective-permute-done.14.refs_2_) | copy-start | bytes 884740
  130.6 0.7 copy-start.16
  134.9 7.3 %collective-permute-start.21 = (bf16[192,384]{1,0:T(8,128)(2,1)}, bf16[192,384]{1,0:T(8,128)(2,1)S(1)}, u32[]{:S(2)}, u32[]{:S(2)}) collective-permute-start(bf16[192,384]{1,0:T(8,128)(2,1)} %get-tuple-element.114), channel_id=1, source_target_pairs={{0,64},{8,72},{16,80},{24,88},{32,96},{40,104},{48,112},{56,120},{... | collective-permute-start | bytes 442376 | tf_op jit(solution)/shard_map/ppermute | solution.py:437
  135.7 10.9 %collective-permute-start.22 = (bf16[192,384]{1,0:T(8,128)(2,1)}, bf16[192,384]{1,0:T(8,128)(2,1)S(1)}, u32[]{:S(2)}, u32[]{:S(2)}) collective-permute-start(bf16[192,384]{1,0:T(8,128)(2,1)} %get-tuple-element.115), channel_id=1, source_target_pairs={{0,128},{8,136},{16,144},{24,152},{32,160},{40,168},{48,176},{56,1... | collective-permute-start | bytes 442376 | tf_op jit(solution)/shard_map/ppermute | solution.py:437
  139.4 7.2 %collective-permute-start.23 = (bf16[192,384]{1,0:T(8,128)(2,1)}, bf16[192,384]{1,0:T(8,128)(2,1)S(1)}, u32[]{:S(2)}, u32[]{:S(2)}) collective-permute-start(bf16[192,384]{1,0:T(8,128)(2,1)} %get-tuple-element.116), channel_id=1, source_target_pairs={{0,192},{8,200},{16,208},{24,216},{32,224},{40,232},{48,240},{56,2... | collective-permute-start | bytes 442376 | tf_op jit(solution)/shard_map/ppermute | solution.py:437
  142.3 4.3 %copy-start.18 = (bf16[192,384]{1,0:T(8,128)(2,1)}, bf16[192,384]{1,0:T(8,128)(2,1)S(1)}, u32[]{:S(2)}) copy-start(bf16[192,384]{1,0:T(8,128)(2,1)S(1)} %collective-permute-done.21.g1) | copy-start | bytes 442372
  146.6 0.7 copy-start.19
  146.6 0.7 copy-start.20
  150.1 1.5 collective-permute-start.24
  152.2 3.6 %collective-permute-start.25 = (f32[8,128]{1,0:T(8,128)S(1)}, f32[8,128]{1,0:T(8,128)S(1)}, u32[]{:S(2)}, u32[]{:S(2)}) collective-permute-start(f32[8,128]{1,0:T(8,128)S(1)} %add.125), channel_id=1, source_target_pairs={{0,16},{8,24},{16,0},{24,8},{32,48},{40,56},{48,32},{56,40},{64,80... | collective-permute-start | bytes 12296 | tf_op jit(solution)/shard_map/ppermute | solution.py:452
  155.8 5.1 %collective-permute-start.26 = (f32[8,128]{1,0:T(8,128)S(1)}, f32[8,128]{1,0:T(8,128)S(1)}, u32[]{:S(2)}, u32[]{:S(2)}) collective-permute-start(f32[8,128]{1,0:T(8,128)S(1)} %add.126), channel_id=1, source_target_pairs={{0,32},{8,40},{16,48},{24,56},{32,0},{40,8},{48,16},{56,24},{64,96... | collective-permute-start | bytes 12296 | tf_op jit(solution)/shard_map/ppermute | solution.py:452
  161.0 3.6 %collective-permute-start.27 = (f32[8,128]{1,0:T(8,128)S(1)}, f32[8,128]{1,0:T(8,128)S(1)}, u32[]{:S(2)}, u32[]{:S(2)}) collective-permute-start(f32[8,128]{1,0:T(8,128)S(1)} %add.127), channel_id=1, source_target_pairs={{0,64},{8,72},{16,80},{24,88},{32,96},{40,104},{48,112},{56,120},{... | collective-permute-start | bytes 12296 | tf_op jit(solution)/shard_map/ppermute | solution.py:452
  164.6 5.1 %collective-permute-start.28 = (f32[8,128]{1,0:T(8,128)S(1)}, f32[8,128]{1,0:T(8,128)S(1)}, u32[]{:S(2)}, u32[]{:S(2)}) collective-permute-start(f32[8,128]{1,0:T(8,128)S(1)} %add.128), channel_id=1, source_target_pairs={{0,128},{8,136},{16,144},{24,152},{32,160},{40,168},{48,176},{56,1... | collective-permute-start | bytes 12296 | tf_op jit(solution)/shard_map/ppermute | solution.py:452
  169.7 3.6 %collective-permute-start.29 = (f32[8,128]{1,0:T(8,128)S(1)}, f32[8,128]{1,0:T(8,128)S(1)}, u32[]{:S(2)}, u32[]{:S(2)}) collective-permute-start(f32[8,128]{1,0:T(8,128)S(1)} %add.129), channel_id=1, source_target_pairs={{0,1},{1,0},{2,3},{3,2},{4,5},{5,4},{6,7},{7,6},{8,9},{9,8},{10,11... | collective-permute-start | bytes 12296 | tf_op jit(solution)/shard_map/ppermute | solution.py:452
  173.3 4.5 %collective-permute-start.30 = (f32[8,128]{1,0:T(8,128)S(1)}, f32[8,128]{1,0:T(8,128)S(1)}, u32[]{:S(2)}, u32[]{:S(2)}) collective-permute-start(f32[8,128]{1,0:T(8,128)S(1)} %add.130), channel_id=1, source_target_pairs={{0,2},{1,3},{2,0},{3,1},{4,6},{5,7},{6,4},{7,5},{8,10},{9,11},{10,... | collective-permute-start | bytes 12296 | tf_op jit(solution)/shard_map/ppermute | solution.py:452
  177.8 13.0 %collective-permute-start.31 = (f32[8,128]{1,0:T(8,128)S(1)}, f32[8,128]{1,0:T(8,128)S(1)}, u32[]{:S(2)}, u32[]{:S(2)}) collective-permute-start(f32[8,128]{1,0:T(8,128)S(1)} %add.131), channel_id=1, source_target_pairs={{0,4},{1,5},{2,6},{3,7},{4,0},{5,1},{6,2},{7,3},{8,12},{9,13},{10,... | collective-permute-start | bytes 12296 | tf_op jit(solution)/shard_map/ppermute | solution.py:452
Sparse Core Ops, SparseCore 0:
  38.6 60.9 all-gather.4
  101.4 44.6 all-gather.8
  150.2 48.9 all-gather.6

commit v3 on v2

--- a/solution.py
+++ b/solution.py
@@ -30,6 +30,11 @@
     return [(d, flat_dp((y + r) % NY, x, c)) for d in range(32) for y, x, c in [coords(d)]]
 
 
+def cross_shift(r, turn):
+    both = (y_shift(r), x_shift(r))
+    return [both[(d % NC + turn) % 2][d] for d in range(32)]
+
+
 def xor_perm(n, bit):
     return [(i, i ^ bit) for i in range(n)]
 
@@ -42,7 +47,8 @@
     return pltpu.CompilerParams(vmem_limit_bytes=mib * MIB)
 
 
-CORE, X, PARITY, SLOT = 8, 9, 10, 11
+CORE, X, PARITY, SLOT, Y = 8, 9, 10, 11, 15
+SUM_ROWS = 16
 
 
 def shard_body(n_parts, ks, fresh, factor, sc, *refs):
@@ -185,12 +191,18 @@
             scratch_shapes=[pltpu.VMEM((NY,) + tail, F32)],
         ),
         out_shape=[jax.ShapeDtypeStruct(tail, F32 if r == 0 else BF) for r in range(NY)],
-        compiler_params=params(),
+        compiler_params=params(8),
         name="x_sum",
     )(sc, *args)
 
 
-def update_body(g0, g1, g2, g3, w, mom, var, err, mom_out, err_out, dir_out, sums):
+def three_parts(value):
+    high = value.astype(BF).astype(F32)
+    middle = (value - high).astype(BF).astype(F32)
+    return high, middle, value - high - middle
+
+
+def update_body(sc, g0, g1, g2, g3, w, mom, var, err, mom_out, err_out, stay, leave, held_dir):
     gradient = (
         g0[...] + g1[...].astype(F32) + g2[...].astype(F32) + g3[...].astype(F32)
     )
@@ -201,88 +213,131 @@
     squeezed = level * jnp.tanh(held / level)
     err_out[...] = held - squeezed
     direction = (squeezed / (jnp.sqrt(var[...]) + 1e-06)).astype(BF)
-    dir_out[...] = direction
+    held_dir[...] = direction
     wf = w[...].astype(F32)
     df = direction.astype(F32)
     total_w = jnp.sum(wf * wf, axis=(0, 1), keepdims=True)
     total_d = jnp.sum(df * df, axis=(0, 1), keepdims=True)
-    row = lax.broadcasted_iota(jnp.int32, sums.shape, 0)
-    sums[...] = jnp.where(row == 0, total_w, total_d)
-
-
-def update(mine, got, weight, momentum, variance, server_error):
+    half, cols = direction.shape[0] // 2, direction.shape[1]
+    row = lax.broadcasted_iota(jnp.int32, (SUM_ROWS, cols), 0)
+    extra = jnp.zeros((SUM_ROWS, cols), F32)
+    for k, part in enumerate(three_parts(total_w) + three_parts(total_d)):
+        extra = jnp.where(row == k, part, extra)
+    for out, which in ((stay, sc[CORE]), (leave, 1 - sc[CORE])):
+        out[0:half] = held_dir[pl.ds(pl.multiple_of(which * half, half), half), :]
+        out[half:] = extra.astype(BF)
+
+
+def update(sc, mine, got, weight, momentum, variance, server_error):
     shape = weight.shape
-    one = pl.BlockSpec(shape, lambda i: (0, 0))
+    part = (shape[0] // 2 + SUM_ROWS, shape[1])
+    one = pl.BlockSpec(shape, lambda i, s: (0, 0))
+    half = pl.BlockSpec(part, lambda i, s: (0, 0))
     return pl.pallas_call(
         update_body,
-        grid=(1,),
-        in_specs=[one] * 8,
-        out_specs=[one, one, one, pl.BlockSpec((8, 128), lambda i: (0, 0))],
+        grid_spec=pltpu.PrefetchScalarGridSpec(
+            num_scalar_prefetch=1,
+            grid=(1,),
+            in_specs=[one] * 8,
+            out_specs=[one, one, half, half],
+            scratch_shapes=[pltpu.VMEM(shape, BF)],
+        ),
         out_shape=[
             jax.ShapeDtypeStruct(shape, F32),
             jax.ShapeDtypeStruct(shape, F32),
-            jax.ShapeDtypeStruct(shape, BF),
-            jax.ShapeDtypeStruct((8, 128), F32),
+            jax.ShapeDtypeStruct(part, BF),
+            jax.ShapeDtypeStruct(part, BF),
         ],
-        compiler_params=params(),
+        compiler_params=params(8),
         name="update",
-    )(mine, *got, weight, momentum, variance, server_error)
+    )(sc, mine, *got, weight, momentum, variance, server_error)
+
+
+def plane_sums_body(a, b, c, d, out):
+    total = sum(jnp.sum(v[...].astype(F32), axis=(0, 1)) for v in (a, b, c, d))
+    weights = total[0:1] + total[1:2] + total[2:3]
+    directions = total[3:4] + total[4:5] + total[5:6]
+    row = lax.broadcasted_iota(jnp.int32, out.shape, 0)
+    out[...] = jnp.where(row == 0, weights, directions)
+
+
+def plane_sums(gathered):
+    lead = gathered[0].shape[:2]
+    at = gathered[0].shape[2] // SUM_ROWS - 1
+    return pl.pallas_call(
+        plane_sums_body,
+        grid=(1,),
+        in_specs=[pl.BlockSpec(lead + (SUM_ROWS, 128), lambda i: (0, 0, at, 0))] * 4,
+        out_specs=pl.BlockSpec((8, 128), lambda i: (0, 0)),
+        out_shape=jax.ShapeDtypeStruct((8, 128), F32),
+        compiler_params=params(8),
+        name="plane_sums",
+    )(*gathered)
 
 
 def forward_body(n_parts, ending, sc, *refs):
     n = sum(n_parts)
-    pieces, b_hbm = refs[:n], refs[n]
-    base = refs[n + 1 : n + 3] if ending else ()
+    pieces = refs[:n]
     out, a_held, b_held, a_sems, b_sems = refs[-5:]
-    rows = b_held.shape[1]
+    quarter = b_held.shape[1] // 4
     waits = []
     at = 0
     for k, parts in enumerate(n_parts):
-        wide = rows // parts
+        wide = 4 * quarter // parts
         mine = []
         for j in range(parts):
             target = a_held.at[k] if parts == 1 else a_held.at[k, :, j * wide : (j + 1) * wide]
             mine.append(pltpu.make_async_copy(pieces[at], target, a_sems.at[at]))
             at += 1
-        if len(b_hbm.shape) == 5:
+        if not ending:
             for i in range(4):
-                target = b_held.at[k, i * (rows // 4) : (i + 1) * (rows // 4)]
-                mine.append(pltpu.make_async_copy(b_hbm.at[sc[k], i, 0], target, b_sems.at[k]))
-        else:
-            mine.append(pltpu.make_async_copy(b_hbm.at[sc[k]], b_held.at[k], b_sems.at[k]))
+                target = b_held.at[k, i * quarter : (i + 1) * quarter]
+                mine.append(pltpu.make_async_copy(refs[n].at[sc[k], i, 0], target, b_sems.at[k]))
         for copy in mine:
             copy.start()
         waits.append(mine)
+    if ending:
+        half = quarter // 2
+        for r2 in range(4):
+            for refs_of, core in ((refs[n : n + 4], sc[CORE]), (refs[n + 4 : n + 8], 1 - sc[CORE])):
+                for r1 in range(4):
+                    x = lax.rem(sc[X] - jnp.where(core == 0, r2, r1) + NX, NX)
+                    y = lax.rem(sc[Y] - jnp.where(core == 0, r1, r2) + NY, NY)
+                    for other in range(2):
+                        block = 2 * lax.rem(x, 2) + (core if other == 0 else 1 - core)
+                        row = pl.multiple_of(block * quarter + core * half, half)
+                        m = 2 * y + x // 2
+                        pltpu.make_async_copy(
+                            refs_of[r2].at[r1, other, 0:half],
+                            b_held.at[m, pl.ds(row, half)],
+                            b_sems.at[m],
+                        ).start()
+        for k, mine in enumerate(waits):
+            m = sc[k]
+            for i in range(8):
+                target = b_held.at[m, i * half : (i + 1) * half]
+                mine.append(pltpu.make_async_copy(refs[n].at[0, 0, 0:half], target, b_sems.at[m]))
     total = None
     for k, mine in enumerate(waits):
         for copy in mine:
             copy.wait()
-        part = jnp.dot(a_held[k], b_held[k], preferred_element_type=F32)
+        part = jnp.dot(a_held[k], b_held[sc[k] if ending else k], preferred_element_type=F32)
         total = part if total is None else total + part
-    if ending:
-        total = base[0][...] - base[1][0:1, 0:1] * total
     out[...] = total.astype(out.dtype)
 
 
-def forward(sc, parts, matrix, base=None, scale=None):
-    tokens = parts[0][0].shape[0]
-    rows, cols = parts[0][0].shape[1], matrix.shape[-1]
+def forward(sc, parts, matrices, ending):
+    tokens, rows = parts[0][0].shape
+    cols = matrices[0].shape[-1]
     args = [v for part in parts for v in part]
     n = len(args)
-    args = args + [matrix]
-    in_specs = [pl.BlockSpec(memory_space=pl.ANY)] * (n + 1)
-    if base is not None:
-        args += [base, scale]
-        in_specs += [
-            pl.BlockSpec((tokens, cols), lambda i, s: (0, 0)),
-            pl.BlockSpec(scale.shape, lambda i, s: (0, 0)),
-        ]
-    return pl.pallas_call(
-        functools.partial(forward_body, [len(p) for p in parts], base is not None),
+    args = args + list(matrices)
+    return pl.pallas_call(
+        functools.partial(forward_body, [len(p) for p in parts], ending),
         grid_spec=pltpu.PrefetchScalarGridSpec(
             num_scalar_prefetch=1,
             grid=(1,),
-            in_specs=in_specs,
+            in_specs=[pl.BlockSpec(memory_space=pl.ANY)] * len(args),
             out_specs=pl.BlockSpec((tokens, cols), lambda i, s: (0, 0)),
             scratch_shapes=[
                 pltpu.VMEM((NZ, tokens, rows), BF),
@@ -291,10 +346,10 @@
                 pltpu.SemaphoreType.DMA((NZ,)),
             ],
         ),
-        out_shape=jax.ShapeDtypeStruct((tokens, cols), F32 if base is None else BF),
+        out_shape=jax.ShapeDtypeStruct((tokens, cols), F32),
         compiler_params=params(),
         cost_estimate=pl.CostEstimate(
-            flops=2 * NZ * tokens * cols * rows, bytes_accessed=2 * matrix.size * 3, transcendentals=0
+            flops=2 * NZ * tokens * cols * rows, bytes_accessed=6 * NZ * rows * cols, transcendentals=0
         ),
         name="forward",
     )(sc, *args)
@@ -374,7 +429,7 @@
 
     ms = [at(0), at(1), at(-1), at(-2), at(2), at(3), at(-3), at(4)]
     slots = [lax.rem(ms[k] // 2 - y + NY, NY) for k in (0, 3, 4, 7)]
-    sc = jnp.stack(ms + [core, x, parity] + slots).astype(jnp.int32)
+    sc = jnp.stack(ms + [core, x, parity] + slots + [y]).astype(jnp.int32)
     tie = lax.optimization_barrier
 
     def grad(parts, ks, wn):
@@ -429,32 +484,32 @@
             ((keep4, recv4, 0), (keep3, recv3, 1)),
         ],
     )
+    sums23, blocks01 = tie((sums23, blocks01))
     blocks23 = spread(sums23)
     parts = [(inputs,), (u1,), (v1,), (v2,), (u2,), (u3,), (v3,), (f0, f1)]
-    base = forward(sc, parts, both)
+    base = forward(sc, parts, [both], False)
     blocks23, base = tie((blocks23, base))
     by_y = x_sum(sc, [blocks01, blocks23])
     got = [lax.ppermute(by_y[r], "dp", y_shift(r)) for r in (1, 2, 3)]
-    momentum_next, server_next, direction, sums = update(
-        by_y[0], got, weight, momentum, variance, server_error
+    momentum_next, server_next, stay, leave = update(
+        sc, by_y[0], got, weight, momentum, variance, server_error
     )
-    directions = lax.all_gather(direction, "dp", axis=0, tiled=True)
-    for axis, n, bit in (
-        ("dp", 32, 1),
-        ("dp", 32, 2),
-        ("dp", 32, 4),
-        ("dp", 32, 8),
-        ("dp", 32, 16),
-        ("mp", NZ, 1),
-        ("mp", NZ, 2),
-        ("mp", NZ, 4),
-    ):
-        sums = sums + lax.ppermute(sums, axis, xor_perm(n, bit))
-    ratio = jnp.sqrt(sums[0:1] / (sums[1:2] + 1e-12))
-
+    halves = jnp.stack([stay, swap(leave)])
+    line = jnp.stack([halves] + [lax.ppermute(halves, "dp", cross_shift(r, 0)) for r in (1, 2, 3)])
+    square = [line] + [lax.ppermute(line, "dp", cross_shift(r, 1)) for r in (1, 2, 3)]
     input_grad = input_grad_of(sc, og_all, both)
-
-    refreshed = forward(sc, parts, directions.reshape(NZ, 4 * rows, cols), base, 0.25 * ratio)
+    theirs = [swap(line)]
+    *square, theirs[0], input_grad = tie((*square, theirs[0], input_grad))
+    theirs += [swap(v) for v in square[1:]]
+    sums = plane_sums(square)
+    sums = sums + lax.ppermute(sums, "mp", xor_perm(NZ, 1))
+    *theirs, sums = tie((*theirs, sums))
+    others = [lax.ppermute(sums, "mp", xor_perm(NZ, k)) for k in (2, 4, 6)]
+    change = forward(sc, parts, square + theirs, True)
+    change, *others = tie((change, *others))
+    sums = sums + others[0] + others[1] + others[2]
+    ratio = jnp.sqrt(sums[0, 0] / (sums[1, 0] + 1e-12))
+    refreshed = (base - 0.25 * ratio * change).astype(BF)
     return (input_grad, momentum_next, server_next, wn, refreshed)
 
 

time: 217 us -> 210 us (0.968)
  waiting for transfers between devices: 85.1 us -> 67.6 us
  starting transfers between devices: 40.5 us -> 51.2 us
  Pallas kernels: 67.8 us -> 64.4 us
    ppermute x8 -> x10, starting transfers between devices: 8.53 us -> 17.5 us  [the longest x3 6.5 us: shards(): others = [lax.ppermute(sums, 'mp', xor_perm(NZ, k)) for k in (2, 4, 6)]]
    ppermute x8 -> x10, waiting for transfers between devices: 21.1 us -> 12.2 us  [the longest x3 5.6 us: shards(): lax.ppermute(line, 'dp', cross_shift(r, 1))]
    all_gather x1 -> x0, waiting for transfers between devices: 7.93 us -> none  [shards(): directions = lax.all_gather(direction, 'dp', axis=0, tiled=True)]
    pallas_call x1, Pallas kernels: 3.66 us -> 0.92 us  [x_sum(): pl.pallas_call(functools.partial(x_sum_body, [g[0].shape[0] for g in grou...]
    pallas_call x3 -> x4, Pallas kernels: 19.1 us -> 18.5 us  [the longest x2 16.6 us: forward(): pl.pallas_call(functools.partial(forward_body, [len(p) for p in parts], e...]
    ppermute x5 -> x10, waiting for transfers between devices: 6.02 us -> 5.55 us  [swap(): return lax.ppermute(send, 'dp', xor_perm(32, 1))]
  transfers between devices with their start and end apart: 35 -> 41, of which waited for: 24 -> 22; matrix products, arithmetic and copies ran while one was open for 1% -> 0% of each run, Pallas kernels for 28% -> 31%
where the time goes in v3:
time: 210 us; the launch traced here: 207 us
  waiting for transfers between devices  67.6 us (32%)
  Pallas kernels  64.4 us (31%)
  starting transfers between devices  51.2 us (24%)
  between operations  15.8 us (8%)
  other arithmetic  3.92 us (2%)
  local copies, waits for them, and re-layouts  3.74 us (2%)
    pallas_call x5, Pallas kernels, shard_grad(): pl.pallas_call(functools.partial(shard_body, [len(p) for p in parts], ks,...  27.4 us
    ppermute x4, waiting for transfers between devices, away(): return lax.ppermute(a, 'mp', FAR)  21.7 us
    pallas_call x2, Pallas kernels, forward(): pl.pallas_call(functools.partial(forward_body, [len(p) for p in parts], e...  16.6 us
    ppermute x6, waiting for transfers between devices, spread(): lax.ppermute(mine[r], 'dp', x_shift(r))  12.6 us
    pallas_call x1, Pallas kernels, input_grad_of(): pl.pallas_call(input_grad_body, grid_spec=pltpu.PrefetchScalarGridSpec(nu...  10.4 us
    ppermute x4, starting transfers between devices, away(): return lax.ppermute(a, 'mp', FAR)  10.2 us
    ppermute x4, waiting for transfers between devices, near(): return lax.ppermute(a, 'mp', NEAR)  10 us
    ppermute x6, starting transfers between devices, spread(): lax.ppermute(mine[r], 'dp', x_shift(r))  9.32 us
  transfers between devices with their start and end apart: 41, of which 22 were waited for; matrix products, arithmetic and copies ran while one was open for 0% of the time, Pallas kernels for 31%

profile of v3, /device:TPU:2, one launch (start us, length us, event | category | flops | bytes accessed | tf_op | source)
XLA Modules:
  0.0 206.6 jit_solution(10054741949309521694)
XLA Ops:
  7.2 5.9 %collective-permute-start.1 = (bf16[512,768]{1,0:T(8,128)(2,1)}, bf16[512,768]{1,0:T(8,128)(2,1)S(1)}, u32[]{:S(2)}, u32[]{:S(2)}) collective-permute-start(bf16[512,768]{1,0:T(8,128)(2,1)} %refs_0_.5), channel_id=1, source_target_pairs={{0,7},{1,2},{2,1},{3,4},{4,3},{5,6},{6,5},{7,0},{8,15},{9,10},{10,... | collective-permute-start | bytes 2359304 | tf_op jit(solution)/shard_map/ppermute | solution.py:425
  13.2 1.6 collective-permute-start.2
  14.7 0.7 collective-permute-start.3
  15.4 17.0 %collective-permute-done.1.refs_1_.refs_2_ = bf16[512,768]{1,0:T(8,128)(2,1)S(1)} collective-permute-done((bf16[512,768]{1,0:T(8,128)(2,1)}, bf16[512,768]{1,0:T(8,128)(2,1)S(1)}, u32[]{:S(2)}, u32[]{:S(2)}) %collective-permute-start.1) | collective-permute-done | bytes 786464 | tf_op jit(solution)/shard_map/ppermute | solution.py:425
  32.4 4.2 %collective-permute-done.refs_0_.refs_1_ = bf16[512,768]{1,0:T(8,128)(2,1)S(1)} collective-permute-done((bf16[512,768]{1,0:T(8,128)(2,1)}, bf16[512,768]{1,0:T(8,128)(2,1)S(1)}, u32[]{:S(2)}, u32[]{:S(2)}) %collective-permute-start) | collective-permute-done | bytes 786464 | tf_op jit(solution)/shard_map/ppermute | solution.py:422
  36.7 1.8 pad_maximum_fusion.1
  38.5 2.5 %collective-permute-start.4 = (bf16[512,768]{1,0:T(8,128)(2,1)S(1)}, bf16[512,768]{1,0:T(8,128)(2,1)S(1)}, u32[]{:S(2)}, u32[]{:S(2)}) collective-permute-start(bf16[512,768]{1,0:T(8,128)(2,1)S(1)} %collective-permute-done.1.refs_1_.refs_2_), channel_id=1, source_target_pairs={{0,1},{1,0},{2,3},{3,2},{4,5},{5,4},{6,7},{7,6},{8,9},{9,8},{10,11... | collective-permute-start | bytes 2359304 | tf_op jit(solution)/shard_map/ppermute | solution.py:422
  41.0 1.2 collective-permute-start.5
  42.2 0.6 stack.91.sc
  42.8 4.1 %shard_grad.5 = (bf16[1,6144,384]{2,1,0:T(8,128)(2,1)}, bf16[2,192,384]{2,1,0:T(8,128)(2,1)}, bf16[2,192,384]{2,1,0:T(8,128)(2,1)}) custom-call(s32[16]{0:T(128)} %stack.91.sc, bf16[512,768]{1,0:T(8,128)(2,1)} %refs_0_.5, bf16[512,384]{1,0:T(8,128)(2,1)} %refs_2_.9, bf16[1,6144,384]{2,1,0:T(8,128)(2,1)} %refs_3_.7), custom_call_target="tpu_custom_call" | custom-call | flops 301989888 | bytes 1769472 | tf_op jit(solution)/shard_map/shard_grad/pallas_call | solution.py:115
  47.0 6.4 %shard_grad.6 = (bf16[1,6144,384]{2,1,0:T(8,128)(2,1)}, bf16[4,192,384]{2,1,0:T(8,128)(2,1)}, bf16[4,192,384]{2,1,0:T(8,128)(2,1)}) custom-call(s32[16]{0:T(128)} %stack.91.sc, bf16[512,768]{1,0:T(8,128)(2,1)} %copy-done.14, bf16[512,768]{1,0:T(8,128)(2,1)} %copy-done.13, bf16[512,384]{1,0:T(8,128)(2,1)} %refs_2_.9, ...), custom_call_target="tpu_custom_call", output_to_operand_aliasing={{0}: (5, {})} | custom-call | flops 603979776 | bytes 3538944 | tf_op jit(solution)/shard_map/shard_grad/pallas_call | solution.py:115
  53.9 1.9 collective-permute-done.6.refs_1_
  55.8 1.9 collective-permute-done.4.refs_1_.refs_4_
  57.7 2.7 %collective-permute-done.5.refs_0_.refs_3_ = bf16[512,768]{1,0:T(8,128)(2,1)S(1)} collective-permute-done((bf16[512,768]{1,0:T(8,128)(2,1)S(1)}, bf16[512,768]{1,0:T(8,128)(2,1)S(1)}, u32[]{:S(2)}, u32[]{:S(2)}) %collective-permute-start.5) | collective-permute-done | bytes 786464 | tf_op jit(solution)/shard_map/ppermute | solution.py:425
  60.4 1.1 collective-permute-start.10
  61.4 6.3 %shard_grad.7 = (bf16[1,6144,384]{2,1,0:T(8,128)(2,1)}, bf16[4,192,384]{2,1,0:T(8,128)(2,1)}, bf16[4,192,384]{2,1,0:T(8,128)(2,1)}) custom-call(s32[16]{0:T(128)} %stack.91.sc, bf16[512,768]{1,0:T(8,128)(2,1)} %copy-done.16, bf16[512,768]{1,0:T(8,128)(2,1)} %copy-done.15, bf16[512,384]{1,0:T(8,128)(2,1)} %refs_2_.9, ...), custom_call_target="tpu_custom_call", output_to_operand_aliasing={{0}: (5, {})} | custom-call | flops 603979776 | bytes 3538944 | tf_op jit(solution)/shard_map/shard_grad/pallas_call | solution.py:115
  67.7 2.3 %collective-permute-done.8.refs_5_.refs_1_ = bf16[4,192,384]{2,1,0:T(8,128)(2,1)} collective-permute-done((bf16[4,192,384]{2,1,0:T(8,128)(2,1)}, bf16[4,192,384]{2,1,0:T(8,128)(2,1)}, u32[]{:S(2)}, u32[]{:S(2)}) %collective-permute-start.8) | collective-permute-done | bytes 589856 | tf_op jit(solution)/shard_map/ppermute | solution.py:439
  70.1 3.6 %core_sum.2 = (f32[2,192,384]{2,1,0:T(8,128)}, bf16[2,192,384]{2,1,0:T(8,128)(2,1)}, bf16[2,192,384]{2,1,0:T(8,128)(2,1)}, bf16[2,192,384]{2,1,0:T(8,128)(2,1)}) custom-call(s32[16]{0:T(128)} %stack.91.sc, bf16[2,192,384]{2,1,0:T(8,128)(2,1)} %get-tuple-element.99.refs_0_, bf16[2,192,384]{2,1,0:T(8,128)(2,1)} %copy-done.26, ...), custom_call_target="tpu_custom_call" | custom-call | tf_op jit(solution)/shard_map/core_sum/pallas_call | solution.py:157
  73.7 3.9 %collective-permute-done.9.refs_0_.refs_5_ = bf16[512,768]{1,0:T(8,128)(2,1)S(1)} collective-permute-done((bf16[512,768]{1,0:T(8,128)(2,1)S(1)}, bf16[512,768]{1,0:T(8,128)(2,1)S(1)}, u32[]{:S(2)}, u32[]{:S(2)}) %collective-permute-start.9) | collective-permute-done | bytes 786464 | tf_op jit(solution)/shard_map/ppermute | solution.py:422
  77.6 1.3 collective-permute-done.10.refs_1_.refs_6_
  79.6 2.0 collective-permute-start.12
  81.5 6.4 %shard_grad.8 = (bf16[1,6144,384]{2,1,0:T(8,128)(2,1)}, bf16[4,192,384]{2,1,0:T(8,128)(2,1)}, bf16[4,192,384]{2,1,0:T(8,128)(2,1)}) custom-call(s32[16]{0:T(128)} %stack.91.sc, bf16[512,768]{1,0:T(8,128)(2,1)} %copy-done.11, bf16[512,768]{1,0:T(8,128)(2,1)} %copy-done.12, bf16[512,384]{1,0:T(8,128)(2,1)} %refs_2_.9, ...), custom_call_target="tpu_custom_call", output_to_operand_aliasing={{0}: (5, {})} | custom-call | flops 603979776 | bytes 3538944 | tf_op jit(solution)/shard_map/shard_grad/pallas_call | solution.py:115
  87.9 0.7 collective-permute-done.12.refs_1_.refs_8_
  88.7 0.6 copy-done.18
  89.3 4.3 %shard_grad.9 = (bf16[1,6144,384]{2,1,0:T(8,128)(2,1)}, bf16[2,192,384]{2,1,0:T(8,128)(2,1)}, bf16[2,192,384]{2,1,0:T(8,128)(2,1)}) custom-call(s32[16]{0:T(128)} %stack.91.sc, bf16[512,384]{1,0:T(8,128)(2,1)} %copy-done.17, bf16[512,384]{1,0:T(8,128)(2,1)} %copy-done.18, bf16[512,384]{1,0:T(8,128)(2,1)} %refs_2_.9, ...), custom_call_target="tpu_custom_call", output_to_operand_aliasing={{0}: (5, {})} | custom-call | flops 301989888 | bytes 1769472 | tf_op jit(solution)/shard_map/shard_grad/pallas_call | solution.py:115
  93.6 1.6 collective-permute-start.15
  95.2 1.2 collective-permute-start.16
  96.4 2.1 %collective-permute-start.17 = (bf16[2,192,384]{2,1,0:T(8,128)(2,1)S(1)}, bf16[2,192,384]{2,1,0:T(8,128)(2,1)S(1)}, u32[]{:S(2)}, u32[]{:S(2)}) collective-permute-start(bf16[2,192,384]{2,1,0:T(8,128)(2,1)S(1)} %copy-done.28), channel_id=1, source_target_pairs={{0,48},{8,56},{16,0},{24,8},{32,16},{40,24},{48,32},{56,40},{64,11... | collective-permute-start | bytes 884744 | tf_op jit(solution)/shard_map/ppermute | solution.py:442
  98.5 0.7 copy-done.27
  99.5 3.6 %core_sum.3 = (f32[2,192,384]{2,1,0:T(8,128)}, bf16[2,192,384]{2,1,0:T(8,128)(2,1)}, bf16[2,192,384]{2,1,0:T(8,128)(2,1)}, bf16[2,192,384]{2,1,0:T(8,128)(2,1)}) custom-call(s32[16]{0:T(128)} %stack.91.sc, bf16[4,192,384]{2,1,0:T(8,128)(2,1)} %get-tuple-element.96.refs_4_.refs_0_, bf16[4,192,384]{2,1,0:T(8,128)(2,1)} %collective-permute-done.8.refs_5_.refs_1_, ...), custom_call_target="tpu_custom_call" | custom-call | tf_op jit(solution)/shard_map/core_sum/pallas_call | solution.py:157
  103.0 0.6 collective-permute-done.15.refs_1_
  103.7 3.0 %collective-permute-done.16.refs_2_ = bf16[2,192,384]{2,1,0:T(8,128)(2,1)S(1)} collective-permute-done((bf16[2,192,384]{2,1,0:T(8,128)(2,1)S(1)}, bf16[2,192,384]{2,1,0:T(8,128)(2,1)S(1)}, u32[]{:S(2)}, u32[]{:S(2)}) %collective-permute-start.16) | collective-permute-done | bytes 294944 | tf_op jit(solution)/shard_map/ppermute | solution.py:442
  106.6 4.7 %collective-permute-done.17.refs_3_ = bf16[2,192,384]{2,1,0:T(8,128)(2,1)S(1)} collective-permute-done((bf16[2,192,384]{2,1,0:T(8,128)(2,1)S(1)}, bf16[2,192,384]{2,1,0:T(8,128)(2,1)S(1)}, u32[]{:S(2)}, u32[]{:S(2)}) %collective-permute-start.17) | collective-permute-done | bytes 294944 | tf_op jit(solution)/shard_map/ppermute | solution.py:442
  111.3 1.2 collective-permute-start.18
  112.6 1.5 collective-permute-start.19
  114.0 1.7 collective-permute-start.20
  115.8 8.2 %forward.2 = f32[512,384]{1,0:T(8,128)} custom-call(s32[16]{0:T(128)} %stack.91.sc, bf16[512,768]{1,0:T(8,128)(2,1)} %refs_0_.5, bf16[512,768]{1,0:T(8,128)(2,1)} %copy-done.14, bf16[512,768]{1,0:T(8,128)(2,1)} %copy-done.13, bf16[512,768]{1,0:T(8,128)(2,1)} %copy-done.16, bf16[512,768]{1,0:T(8,128)(2,1)} %copy-done.15, bf16[512,768]{1,0:T(8,128)(2,1)} %copy-done.11, ...), custom_call_target="tpu_custom_call" | custom-call | flops 2415919104 | bytes 14155776 | tf_op jit(solution)/shard_map/forward/pallas_call | solution.py:335
  124.2 4.1 %collective-permute-done.20.refs_7_ = bf16[2,192,384]{2,1,0:T(8,128)(2,1)S(1)} collective-permute-done((bf16[2,192,384]{2,1,0:T(8,128)(2,1)}, bf16[2,192,384]{2,1,0:T(8,128)(2,1)S(1)}, u32[]{:S(2)}, u32[]{:S(2)}) %collective-permute-start.20) | collective-permute-done | bytes 294944 | tf_op jit(solution)/shard_map/ppermute | solution.py:442
  128.4 0.9 x_sum.1
  129.3 0.8 collective-permute-start.21
  130.1 3.8 %collective-permute-start.22 = (bf16[192,384]{1,0:T(8,128)(2,1)S(1)}, bf16[192,384]{1,0:T(8,128)(2,1)S(1)}, u32[]{:S(2)}, u32[]{:S(2)}) collective-permute-start(bf16[192,384]{1,0:T(8,128)(2,1)S(1)} %get-tuple-element.145), channel_id=1, source_target_pairs={{0,128},{8,136},{16,144},{24,152},{32,160},{40,168},{48,176},{56,1... | collective-permute-start | bytes 442376 | tf_op jit(solution)/shard_map/ppermute | solution.py:493
  133.9 1.5 collective-permute-start.23
  135.4 1.2 collective-permute-done.21.g1
  136.6 4.3 %collective-permute-done.22.g2 = bf16[192,384]{1,0:T(8,128)(2,1)S(1)} collective-permute-done((bf16[192,384]{1,0:T(8,128)(2,1)S(1)}, bf16[192,384]{1,0:T(8,128)(2,1)S(1)}, u32[]{:S(2)}, u32[]{:S(2)}) %collective-permute-start.22) | collective-permute-done | bytes 147488 | tf_op jit(solution)/shard_map/ppermute | solution.py:493
  140.9 1.9 update.1
  142.8 1.3 collective-permute-done.24
  144.1 2.8 %collective-permute-start.26 = (bf16[2,112,384]{2,1,0:T(8,128)(2,1)S(1)}, bf16[2,112,384]{2,1,0:T(8,128)(2,1)S(1)}, u32[]{:S(2)}, u32[]{:S(2)}) collective-permute-start(bf16[2,112,384]{2,1,0:T(8,128)(2,1)S(1)} %get-tuple-element.170), channel_id=1, source_target_pairs={{0,128},{8,40},{16,144},{24,56},{32,160},{40,8},{48,176},{56,24},{... | collective-permute-start | bytes 516104 | tf_op jit(solution)/shard_map/ppermute | solution.py:498
  147.2 2.9 %collective-permute-start.27 = (bf16[2,112,384]{2,1,0:T(8,128)(2,1)S(1)}, bf16[2,112,384]{2,1,0:T(8,128)(2,1)S(1)}, u32[]{:S(2)}, u32[]{:S(2)}) collective-permute-start(bf16[2,112,384]{2,1,0:T(8,128)(2,1)S(1)} %get-tuple-element.170), channel_id=1, source_target_pairs={{0,192},{8,56},{16,208},{24,8},{32,224},{40,24},{48,240},{56,40},{... | collective-permute-start | bytes 516104 | tf_op jit(solution)/shard_map/ppermute | solution.py:498
  150.1 1.0 collective-permute-done.26
  151.1 2.4 %collective-permute-done.25 = bf16[2,112,384]{2,1,0:T(8,128)(2,1)S(1)} collective-permute-done((bf16[2,112,384]{2,1,0:T(8,128)(2,1)S(1)}, bf16[2,112,384]{2,1,0:T(8,128)(2,1)S(1)}, u32[]{:S(2)}, u32[]{:S(2)}) %collective-permute-start.25) | collective-permute-done | bytes 172064 | tf_op jit(solution)/shard_map/ppermute | solution.py:498
  154.1 1.9 collective-permute-start.29
  156.0 2.5 %collective-permute-start.28 = (bf16[4,2,112,384]{3,2,1,0:T(8,128)(2,1)S(1)}, bf16[4,2,112,384]{3,2,1,0:T(8,128)(2,1)S(1)}, u32[]{:S(2)}, u32[]{:S(2)}) collective-permute-start(bf16[4,2,112,384]{3,2,1,0:T(8,128)(2,1)S(1)} %pad_maximum_fusion.a.refs_9_), channel_id=1, source_target_pairs={{0,16},{8,72},{16,32},{24,88},{32,48},{40,104},{48,0},{56,120},{64... | collective-permute-start | bytes 2064392 | tf_op jit(solution)/shard_map/ppermute | solution.py:499
  158.5 10.4 %input_grad.1 = bf16[512,768]{1,0:T(8,128)(2,1)} custom-call(s32[16]{0:T(128)} %stack.91.sc, bf16[8,512,384]{2,1,0:T(8,128)(2,1)} %bitcast.29, bf16[8,4,2,192,384]{4,3,2,1,0:T(8,128)(2,1)} %bitcast.28), custom_call_target="tpu_custom_call" | custom-call | flops 2415919104 | bytes 3145728 | tf_op jit(solution)/shard_map/input_grad/pallas_call | solution.py:379
  168.9 3.5 %collective-permute-done.30.d.refs_12_ = bf16[4,2,112,384]{3,2,1,0:T(8,128)(2,1)S(1)} collective-permute-done((bf16[4,2,112,384]{3,2,1,0:T(8,128)(2,1)S(1)}, bf16[4,2,112,384]{3,2,1,0:T(8,128)(2,1)S(1)}, u32[]{:S(2)}, u32[]{:S(2)}) %collective-permute-start.30) | collective-permute-done | bytes 688160 | tf_op jit(solution)/shard_map/ppermute | solution.py:499
  172.4 2.1 %collective-permute-done.28.b.refs_10_ = bf16[4,2,112,384]{3,2,1,0:T(8,128)(2,1)S(1)} collective-permute-done((bf16[4,2,112,384]{3,2,1,0:T(8,128)(2,1)S(1)}, bf16[4,2,112,384]{3,2,1,0:T(8,128)(2,1)S(1)}, u32[]{:S(2)}, u32[]{:S(2)}) %collective-permute-start.28) | collective-permute-done | bytes 688160 | tf_op jit(solution)/shard_map/ppermute | solution.py:499
  174.5 1.3 collective-permute-start.32
  176.8 3.2 %collective-permute-done.35 = f32[8,128]{1,0:T(8,128)S(1)} collective-permute-done((f32[8,128]{1,0:T(8,128)S(1)}, f32[8,128]{1,0:T(8,128)S(1)}, u32[]{:S(2)}, u32[]{:S(2)}) %collective-permute-start.35) | collective-permute-done | bytes 4128 | tf_op jit(solution)/shard_map/ppermute | solution.py:505
  180.1 0.8 copy-done.23
  180.9 2.0 collective-permute-start.38
  183.0 2.2 %collective-permute-start.37 = (f32[8,128]{1,0:T(8,128)S(1)}, f32[8,128]{1,0:T(8,128)S(1)}, u32[]{:S(2)}, u32[]{:S(2)}) collective-permute-start(f32[8,128]{1,0:T(8,128)S(1)} %add.111), channel_id=1, source_target_pairs={{0,4},{1,5},{2,6},{3,7},{4,0},{5,1},{6,2},{7,3},{8,12},{9,13},{10,... | collective-permute-start | bytes 12296 | tf_op jit(solution)/shard_map/ppermute | solution.py:507
  185.2 2.2 %collective-permute-start.36 = (f32[8,128]{1,0:T(8,128)S(1)}, f32[8,128]{1,0:T(8,128)S(1)}, u32[]{:S(2)}, u32[]{:S(2)}) collective-permute-start(f32[8,128]{1,0:T(8,128)S(1)} %add.111), channel_id=1, source_target_pairs={{0,2},{1,3},{2,0},{3,1},{4,6},{5,7},{6,4},{7,5},{8,10},{9,11},{10,... | collective-permute-start | bytes 12296 | tf_op jit(solution)/shard_map/ppermute | solution.py:507
  187.5 8.3 %forward.3 = f32[512,384]{1,0:T(8,128)} custom-call(s32[16]{0:T(128)} %stack.91.sc, bf16[512,768]{1,0:T(8,128)(2,1)} %refs_0_.5, bf16[512,768]{1,0:T(8,128)(2,1)} %copy-done.14, bf16[512,768]{1,0:T(8,128)(2,1)} %copy-done.13, bf16[512,768]{1,0:T(8,128)(2,1)} %copy-done.16, bf16[512,768]{1,0:T(8,128)(2,1)} %copy-done.15, bf16[512,768]{1,0:T(8,128)(2,1)} %copy-done.11, ...), custom_call_target="tpu_custom_call" | custom-call | flops 2415919104 | bytes 14155776 | tf_op jit(solution)/shard_map/forward/pallas_call | solution.py:335
  195.8 0.6 fusion.1
  197.8 2.0 subtract_convert_fusion
  (107 shorter events, 3.8 us)
Async XLA Ops:
  7.2 108.6 %all-gather.4.cloned.1.call-start = ((), (), s32[]{:S(2)}) async-start(), calls=%async_computation | async-start | bytes 9732096 | tf_op jit(solution)/shard_map/all_gather | solution.py:449
  7.2 25.2 %collective-permute-start.1 = (bf16[512,768]{1,0:T(8,128)(2,1)}, bf16[512,768]{1,0:T(8,128)(2,1)S(1)}, u32[]{:S(2)}, u32[]{:S(2)}) collective-permute-start(bf16[512,768]{1,0:T(8,128)(2,1)} %refs_0_.5), channel_id=1, source_target_pairs={{0,7},{1,2},{2,1},{3,4},{4,3},{5,6},{6,5},{7,0},{8,15},{9,10},{10,... | collective-permute-start | bytes 2359304 | tf_op jit(solution)/shard_map/ppermute | solution.py:425
  13.2 23.5 %collective-permute-start = (bf16[512,768]{1,0:T(8,128)(2,1)}, bf16[512,768]{1,0:T(8,128)(2,1)S(1)}, u32[]{:S(2)}, u32[]{:S(2)}) collective-permute-start(bf16[512,768]{1,0:T(8,128)(2,1)} %refs_0_.5), channel_id=1, source_target_pairs={{0,1},{1,0},{2,3},{3,2},{4,5},{5,4},{6,7},{7,6},{8,9},{9,8},{10,11... | collective-permute-start | bytes 2359304 | tf_op jit(solution)/shard_map/ppermute | solution.py:422
  13.2 1.6 collective-permute-start.2
  14.7 0.7 collective-permute-start.3
  32.4 14.5 %copy-start.13 = (bf16[512,768]{1,0:T(8,128)(2,1)}, bf16[512,768]{1,0:T(8,128)(2,1)S(1)}, u32[]{:S(2)}) copy-start(bf16[512,768]{1,0:T(8,128)(2,1)S(1)} %collective-permute-done.1.refs_1_.refs_2_) | copy-start | bytes 2359300
  36.7 10.3 %copy-start.14 = (bf16[512,768]{1,0:T(8,128)(2,1)}, bf16[512,768]{1,0:T(8,128)(2,1)S(1)}, u32[]{:S(2)}) copy-start(bf16[512,768]{1,0:T(8,128)(2,1)S(1)} %collective-permute-done.refs_0_.refs_1_) | copy-start | bytes 2359300
  38.5 120.0 %all-gather.6.cloned.1.call-start = ((), (), s32[]{:S(2)}) async-start(), calls=%async_computation.1 | async-start | bytes 3538944 | tf_op jit(solution)/shard_map/all_gather | solution.py:475
  38.5 19.2 %collective-permute-start.4 = (bf16[512,768]{1,0:T(8,128)(2,1)S(1)}, bf16[512,768]{1,0:T(8,128)(2,1)S(1)}, u32[]{:S(2)}, u32[]{:S(2)}) collective-permute-start(bf16[512,768]{1,0:T(8,128)(2,1)S(1)} %collective-permute-done.1.refs_1_.refs_2_), channel_id=1, source_target_pairs={{0,1},{1,0},{2,3},{3,2},{4,5},{5,4},{6,7},{7,6},{8,9},{9,8},{10,11... | collective-permute-start | bytes 2359304 | tf_op jit(solution)/shard_map/ppermute | solution.py:422
  41.0 19.4 %collective-permute-start.5 = (bf16[512,768]{1,0:T(8,128)(2,1)S(1)}, bf16[512,768]{1,0:T(8,128)(2,1)S(1)}, u32[]{:S(2)}, u32[]{:S(2)}) collective-permute-start(bf16[512,768]{1,0:T(8,128)(2,1)S(1)} %collective-permute-done.refs_0_.refs_1_), channel_id=1, source_target_pairs={{0,7},{1,2},{2,1},{3,4},{4,3},{5,6},{6,5},{7,0},{8,15},{9,10},{10,... | collective-permute-start | bytes 2359304 | tf_op jit(solution)/shard_map/ppermute | solution.py:425
  47.0 6.5 %copy-start.31 = (bf16[2,192,384]{2,1,0:T(8,128)(2,1)S(1)}, bf16[2,192,384]{2,1,0:T(8,128)(2,1)}, u32[]{:S(2)}) copy-start(bf16[2,192,384]{2,1,0:T(8,128)(2,1)} %get-tuple-element.91) | copy-start | bytes 884740
  53.4 2.4 %collective-permute-start.7 = (bf16[4,192,384]{2,1,0:T(8,128)(2,1)}, bf16[4,192,384]{2,1,0:T(8,128)(2,1)S(1)}, u32[]{:S(2)}, u32[]{:S(2)}) collective-permute-start(bf16[4,192,384]{2,1,0:T(8,128)(2,1)} %get-tuple-element.92), channel_id=1, source_target_pairs={{0,8},{8,0},{16,24},{24,16},{32,40},{40,32},{48,56},{56,48},{64,72... | collective-permute-start | bytes 1769480 | tf_op jit(solution)/shard_map/ppermute | solution.py:439
  53.4 2.4 %collective-permute-start.6 = (bf16[2,192,384]{2,1,0:T(8,128)(2,1)S(1)}, bf16[2,192,384]{2,1,0:T(8,128)(2,1)S(1)}, u32[]{:S(2)}, u32[]{:S(2)}) collective-permute-start(bf16[2,192,384]{2,1,0:T(8,128)(2,1)S(1)} %copy-done.31), channel_id=1, source_target_pairs={{0,8},{8,0},{16,24},{24,16},{32,40},{40,32},{48,56},{56,48},{64,72... | collective-permute-start | bytes 884744 | tf_op jit(solution)/shard_map/ppermute | solution.py:439
  55.8 14.2 %copy-start.26 = (bf16[2,192,384]{2,1,0:T(8,128)(2,1)}, bf16[2,192,384]{2,1,0:T(8,128)(2,1)S(1)}, u32[]{:S(2)}) copy-start(bf16[2,192,384]{2,1,0:T(8,128)(2,1)S(1)} %collective-permute-done.6.refs_1_) | copy-start | bytes 884740
  55.8 4.5 %copy-start.20 = (bf16[4,192,384]{2,1,0:T(8,128)(2,1)}, bf16[4,192,384]{2,1,0:T(8,128)(2,1)S(1)}, u32[]{:S(2)}) copy-start(bf16[4,192,384]{2,1,0:T(8,128)(2,1)S(1)} %collective-permute-done.7.refs_3_.refs_7_) | copy-start | bytes 1769476
  60.4 17.2 %collective-permute-start.9 = (bf16[512,768]{1,0:T(8,128)(2,1)S(1)}, bf16[512,768]{1,0:T(8,128)(2,1)S(1)}, u32[]{:S(2)}, u32[]{:S(2)}) collective-permute-start(bf16[512,768]{1,0:T(8,128)(2,1)S(1)} %collective-permute-done.5.refs_0_.refs_3_), channel_id=1, source_target_pairs={{0,1},{1,0},{2,3},{3,2},{4,5},{5,4},{6,7},{7,6},{8,9},{9,8},{10,11... | collective-permute-start | bytes 2359304 | tf_op jit(solution)/shard_map/ppermute | solution.py:422
  60.4 18.5 %collective-permute-start.10 = (bf16[512,768]{1,0:T(8,128)(2,1)S(1)}, bf16[512,768]{1,0:T(8,128)(2,1)S(1)}, u32[]{:S(2)}, u32[]{:S(2)}) collective-permute-start(bf16[512,768]{1,0:T(8,128)(2,1)S(1)} %collective-permute-done.4.refs_1_.refs_4_), channel_id=1, source_target_pairs={{0,7},{1,2},{2,1},{3,4},{4,3},{5,6},{6,5},{7,0},{8,15},{9,10},{10,... | collective-permute-start | bytes 2359304 | tf_op jit(solution)/shard_map/ppermute | solution.py:425
  67.7 2.3 %collective-permute-start.8 = (bf16[4,192,384]{2,1,0:T(8,128)(2,1)}, bf16[4,192,384]{2,1,0:T(8,128)(2,1)}, u32[]{:S(2)}, u32[]{:S(2)}) collective-permute-start(bf16[4,192,384]{2,1,0:T(8,128)(2,1)} %get-tuple-element.97), channel_id=1, source_target_pairs={{0,8},{8,0},{16,24},{24,16},{32,40},{40,32},{48,56},{56,48},{64,72... | collective-permute-start | bytes 1769480 | tf_op jit(solution)/shard_map/ppermute | solution.py:439
  77.6 3.9 %copy-start.11 = (bf16[512,768]{1,0:T(8,128)(2,1)}, bf16[512,768]{1,0:T(8,128)(2,1)S(1)}, u32[]{:S(2)}) copy-start(bf16[512,768]{1,0:T(8,128)(2,1)S(1)} %collective-permute-done.9.refs_0_.refs_5_) | copy-start | bytes 2359300
  79.0 8.9 %collective-permute-start.11 = (bf16[512,384]{1,0:T(8,128)(2,1)S(1)}, bf16[512,384]{1,0:T(8,128)(2,1)S(1)}, u32[]{:S(2)}, u32[]{:S(2)}) collective-permute-start(bf16[512,384]{1,0:T(8,128)(2,1)S(1)} %slice.12), channel_id=1, source_target_pairs={{0,1},{1,0},{2,3},{3,2},{4,5},{5,4},{6,7},{7,6},{8,9},{9,8},{10,11... | collective-permute-start | bytes 1179656 | tf_op jit(solution)/shard_map/ppermute | solution.py:422
  79.6 9.0 %collective-permute-start.12 = (bf16[512,384]{1,0:T(8,128)(2,1)S(1)}, bf16[512,384]{1,0:T(8,128)(2,1)S(1)}, u32[]{:S(2)}, u32[]{:S(2)}) collective-permute-start(bf16[512,384]{1,0:T(8,128)(2,1)S(1)} %slice.13), channel_id=1, source_target_pairs={{0,7},{1,2},{2,1},{3,4},{4,3},{5,6},{6,5},{7,0},{8,15},{9,10},{10,... | collective-permute-start | bytes 1179656 | tf_op jit(solution)/shard_map/ppermute | solution.py:425
  88.6 5.0 %copy-start.30 = (bf16[2,192,384]{2,1,0:T(8,128)(2,1)S(1)}, bf16[2,192,384]{2,1,0:T(8,128)(2,1)}, u32[]{:S(2)}) copy-start(bf16[2,192,384]{2,1,0:T(8,128)(2,1)} %get-tuple-element.127) | copy-start | bytes 884740
  88.6 6.7 %copy-start.29 = (bf16[2,192,384]{2,1,0:T(8,128)(2,1)S(1)}, bf16[2,192,384]{2,1,0:T(8,128)(2,1)}, u32[]{:S(2)}) copy-start(bf16[2,192,384]{2,1,0:T(8,128)(2,1)} %get-tuple-element.128) | copy-start | bytes 884740
  88.6 7.8 %copy-start.28 = (bf16[2,192,384]{2,1,0:T(8,128)(2,1)S(1)}, bf16[2,192,384]{2,1,0:T(8,128)(2,1)}, u32[]{:S(2)}) copy-start(bf16[2,192,384]{2,1,0:T(8,128)(2,1)} %get-tuple-element.129) | copy-start | bytes 884740
  88.6 9.9 %collective-permute-start.13 = (bf16[4,192,384]{2,1,0:T(8,128)(2,1)}, bf16[4,192,384]{2,1,0:T(8,128)(2,1)S(1)}, u32[]{:S(2)}, u32[]{:S(2)}) collective-permute-start(bf16[4,192,384]{2,1,0:T(8,128)(2,1)} %get-tuple-element.116), channel_id=1, source_target_pairs={{0,8},{8,0},{16,24},{24,16},{32,40},{40,32},{48,56},{56,48},{64,72... | collective-permute-start | bytes 1769480 | tf_op jit(solution)/shard_map/ppermute | solution.py:439
  93.5 5.0 %collective-permute-start.14 = (bf16[2,192,384]{2,1,0:T(8,128)(2,1)}, bf16[2,192,384]{2,1,0:T(8,128)(2,1)S(1)}, u32[]{:S(2)}, u32[]{:S(2)}) collective-permute-start(bf16[2,192,384]{2,1,0:T(8,128)(2,1)} %get-tuple-element.121), channel_id=1, source_target_pairs={{0,8},{8,0},{16,24},{24,16},{32,40},{40,32},{48,56},{56,48},{64,72... | collective-permute-start | bytes 884744 | tf_op jit(solution)/shard_map/ppermute | solution.py:439
  93.6 10.1 %collective-permute-start.15 = (bf16[2,192,384]{2,1,0:T(8,128)(2,1)S(1)}, bf16[2,192,384]{2,1,0:T(8,128)(2,1)S(1)}, u32[]{:S(2)}, u32[]{:S(2)}) collective-permute-start(bf16[2,192,384]{2,1,0:T(8,128)(2,1)S(1)} %copy-done.30), channel_id=1, source_target_pairs={{0,16},{8,24},{16,32},{24,40},{32,48},{40,56},{48,0},{56,8},{64,80... | collective-permute-start | bytes 884744 | tf_op jit(solution)/shard_map/ppermute | solution.py:442
  95.2 11.4 %collective-permute-start.16 = (bf16[2,192,384]{2,1,0:T(8,128)(2,1)S(1)}, bf16[2,192,384]{2,1,0:T(8,128)(2,1)S(1)}, u32[]{:S(2)}, u32[]{:S(2)}) collective-permute-start(bf16[2,192,384]{2,1,0:T(8,128)(2,1)S(1)} %copy-done.29), channel_id=1, source_target_pairs={{0,32},{8,40},{16,48},{24,56},{32,0},{40,8},{48,16},{56,24},{64,96... | collective-permute-start | bytes 884744 | tf_op jit(solution)/shard_map/ppermute | solution.py:442
  96.4 14.9 %collective-permute-start.17 = (bf16[2,192,384]{2,1,0:T(8,128)(2,1)S(1)}, bf16[2,192,384]{2,1,0:T(8,128)(2,1)S(1)}, u32[]{:S(2)}, u32[]{:S(2)}) collective-permute-start(bf16[2,192,384]{2,1,0:T(8,128)(2,1)S(1)} %copy-done.28), channel_id=1, source_target_pairs={{0,48},{8,56},{16,0},{24,8},{32,16},{40,24},{48,32},{56,40},{64,11... | collective-permute-start | bytes 884744 | tf_op jit(solution)/shard_map/ppermute | solution.py:442
  111.3 12.7 %collective-permute-start.18 = (bf16[2,192,384]{2,1,0:T(8,128)(2,1)}, bf16[2,192,384]{2,1,0:T(8,128)(2,1)S(1)}, u32[]{:S(2)}, u32[]{:S(2)}) collective-permute-start(bf16[2,192,384]{2,1,0:T(8,128)(2,1)} %get-tuple-element.135), channel_id=1, source_target_pairs={{0,16},{8,24},{16,32},{24,40},{32,48},{40,56},{48,0},{56,8},{64,80... | collective-permute-start | bytes 884744 | tf_op jit(solution)/shard_map/ppermute | solution.py:442
  112.6 11.7 %collective-permute-start.19 = (bf16[2,192,384]{2,1,0:T(8,128)(2,1)}, bf16[2,192,384]{2,1,0:T(8,128)(2,1)S(1)}, u32[]{:S(2)}, u32[]{:S(2)}) collective-permute-start(bf16[2,192,384]{2,1,0:T(8,128)(2,1)} %get-tuple-element.136), channel_id=1, source_target_pairs={{0,32},{8,40},{16,48},{24,56},{32,0},{40,8},{48,16},{56,24},{64,96... | collective-permute-start | bytes 884744 | tf_op jit(solution)/shard_map/ppermute | solution.py:442
  114.0 14.3 %collective-permute-start.20 = (bf16[2,192,384]{2,1,0:T(8,128)(2,1)}, bf16[2,192,384]{2,1,0:T(8,128)(2,1)S(1)}, u32[]{:S(2)}, u32[]{:S(2)}) collective-permute-start(bf16[2,192,384]{2,1,0:T(8,128)(2,1)} %get-tuple-element.137), channel_id=1, source_target_pairs={{0,48},{8,56},{16,0},{24,8},{32,16},{40,24},{48,32},{56,40},{64,11... | collective-permute-start | bytes 884744 | tf_op jit(solution)/shard_map/ppermute | solution.py:442
  115.7 12.6 %copy-start.4 = (f32[2,192,384]{2,1,0:T(8,128)S(1)}, f32[2,192,384]{2,1,0:T(8,128)}, u32[]{:S(2)}) copy-start(f32[2,192,384]{2,1,0:T(8,128)} %get-tuple-element.130.refs_0_) | copy-start | bytes 1769476
  115.7 12.6 %copy-start.5 = (f32[2,192,384]{2,1,0:T(8,128)S(1)}, f32[2,192,384]{2,1,0:T(8,128)}, u32[]{:S(2)}) copy-start(f32[2,192,384]{2,1,0:T(8,128)} %get-tuple-element.139.refs_4_) | copy-start | bytes 1769476
  115.8 12.6 %copy-start.10 = (s32[16]{0:T(128)S(1)}, s32[16]{0:T(128)}, u32[]{:S(2)}) copy-start(s32[16]{0:T(128)} %stack.91.sc) | copy-start | bytes 196
  115.8 25.1 %copy-start.6 = (bf16[192,384]{1,0:T(8,128)(2,1)S(1)}, bf16[192,384]{1,0:T(8,128)(2,1)}, u32[]{:S(2)}) copy-start(bf16[192,384]{1,0:T(8,128)(2,1)} %w.1) | copy-start | bytes 442372
  115.8 25.1 %copy-start.7 = (f32[192,384]{1,0:T(8,128)S(1)}, f32[192,384]{1,0:T(8,128)}, u32[]{:S(2)}) copy-start(f32[192,384]{1,0:T(8,128)} %mom.1) | copy-start | bytes 884740
  115.8 25.1 %copy-start.8 = (f32[192,384]{1,0:T(8,128)S(1)}, f32[192,384]{1,0:T(8,128)}, u32[]{:S(2)}) copy-start(f32[192,384]{1,0:T(8,128)} %var.1) | copy-start | bytes 884740
  115.8 25.1 %copy-start.9 = (f32[192,384]{1,0:T(8,128)S(1)}, f32[192,384]{1,0:T(8,128)}, u32[]{:S(2)}) copy-start(f32[192,384]{1,0:T(8,128)} %err.1) | copy-start | bytes 884740
  129.3 7.3 %collective-permute-start.21 = (bf16[192,384]{1,0:T(8,128)(2,1)S(1)}, bf16[192,384]{1,0:T(8,128)(2,1)S(1)}, u32[]{:S(2)}, u32[]{:S(2)}) collective-permute-start(bf16[192,384]{1,0:T(8,128)(2,1)S(1)} %get-tuple-element.144), channel_id=1, source_target_pairs={{0,64},{8,72},{16,80},{24,88},{32,96},{40,104},{48,112},{56,120},{... | collective-permute-start | bytes 442376 | tf_op jit(solution)/shard_map/ppermute | solution.py:493
  130.1 10.8 %collective-permute-start.22 = (bf16[192,384]{1,0:T(8,128)(2,1)S(1)}, bf16[192,384]{1,0:T(8,128)(2,1)S(1)}, u32[]{:S(2)}, u32[]{:S(2)}) collective-permute-start(bf16[192,384]{1,0:T(8,128)(2,1)S(1)} %get-tuple-element.145), channel_id=1, source_target_pairs={{0,128},{8,136},{16,144},{24,152},{32,160},{40,168},{48,176},{56,1... | collective-permute-start | bytes 442376 | tf_op jit(solution)/shard_map/ppermute | solution.py:493
  133.9 7.0 %collective-permute-start.23 = (bf16[192,384]{1,0:T(8,128)(2,1)S(1)}, bf16[192,384]{1,0:T(8,128)(2,1)S(1)}, u32[]{:S(2)}, u32[]{:S(2)}) collective-permute-start(bf16[192,384]{1,0:T(8,128)(2,1)S(1)} %get-tuple-element.146), channel_id=1, source_target_pairs={{0,192},{8,200},{16,208},{24,216},{32,224},{40,232},{48,240},{56,2... | collective-permute-start | bytes 442376 | tf_op jit(solution)/shard_map/ppermute | solution.py:493
  142.8 1.3 collective-permute-start.24
  144.1 7.0 %collective-permute-start.26 = (bf16[2,112,384]{2,1,0:T(8,128)(2,1)S(1)}, bf16[2,112,384]{2,1,0:T(8,128)(2,1)S(1)}, u32[]{:S(2)}, u32[]{:S(2)}) collective-permute-start(bf16[2,112,384]{2,1,0:T(8,128)(2,1)S(1)} %get-tuple-element.170), channel_id=1, source_target_pairs={{0,128},{8,40},{16,144},{24,56},{32,160},{40,8},{48,176},{56,24},{... | collective-permute-start | bytes 516104 | tf_op jit(solution)/shard_map/ppermute | solution.py:498
  146.9 6.6 %collective-permute-start.25 = (bf16[2,112,384]{2,1,0:T(8,128)(2,1)S(1)}, bf16[2,112,384]{2,1,0:T(8,128)(2,1)S(1)}, u32[]{:S(2)}, u32[]{:S(2)}) collective-permute-start(bf16[2,112,384]{2,1,0:T(8,128)(2,1)S(1)} %get-tuple-element.170), channel_id=1, source_target_pairs={{0,64},{8,24},{16,80},{24,40},{32,96},{40,56},{48,112},{56,8},{64,... | collective-permute-start | bytes 516104 | tf_op jit(solution)/shard_map/ppermute | solution.py:498
  147.2 6.3 %collective-permute-start.27 = (bf16[2,112,384]{2,1,0:T(8,128)(2,1)S(1)}, bf16[2,112,384]{2,1,0:T(8,128)(2,1)S(1)}, u32[]{:S(2)}, u32[]{:S(2)}) collective-permute-start(bf16[2,112,384]{2,1,0:T(8,128)(2,1)S(1)} %get-tuple-element.170), channel_id=1, source_target_pairs={{0,192},{8,56},{16,208},{24,8},{32,224},{40,24},{48,240},{56,40},{... | collective-permute-start | bytes 516104 | tf_op jit(solution)/shard_map/ppermute | solution.py:498
  153.6 22.7 %copy-start = (bf16[4,2,112,384]{3,2,1,0:T(8,128)(2,1)}, bf16[4,2,112,384]{3,2,1,0:T(8,128)(2,1)S(1)}, u32[]{:S(2)}) copy-start(bf16[4,2,112,384]{3,2,1,0:T(8,128)(2,1)S(1)} %pad_maximum_fusion.a.refs_9_) | copy-start | bytes 2064388
  153.7 15.2 %collective-permute-start.31 = (bf16[4,2,112,384]{3,2,1,0:T(8,128)(2,1)S(1)}, bf16[4,2,112,384]{3,2,1,0:T(8,128)(2,1)S(1)}, u32[]{:S(2)}, u32[]{:S(2)}) collective-permute-start(bf16[4,2,112,384]{3,2,1,0:T(8,128)(2,1)S(1)} %pad_maximum_fusion.a.refs_9_), channel_id=1, source_target_pairs={{0,8},{8,0},{16,24},{24,16},{32,40},{40,32},{48,56},{56,48},{64,72... | collective-permute-start | bytes 2064392 | tf_op jit(solution)/shard_map/ppermute | solution.py:439
  154.0 18.4 %collective-permute-start.30 = (bf16[4,2,112,384]{3,2,1,0:T(8,128)(2,1)S(1)}, bf16[4,2,112,384]{3,2,1,0:T(8,128)(2,1)S(1)}, u32[]{:S(2)}, u32[]{:S(2)}) collective-permute-start(bf16[4,2,112,384]{3,2,1,0:T(8,128)(2,1)S(1)} %pad_maximum_fusion.a.refs_9_), channel_id=1, source_target_pairs={{0,48},{8,200},{16,0},{24,216},{32,16},{40,232},{48,32},{56,248},{... | collective-permute-start | bytes 2064392 | tf_op jit(solution)/shard_map/ppermute | solution.py:499
  154.1 18.3 %collective-permute-start.29 = (bf16[4,2,112,384]{3,2,1,0:T(8,128)(2,1)S(1)}, bf16[4,2,112,384]{3,2,1,0:T(8,128)(2,1)S(1)}, u32[]{:S(2)}, u32[]{:S(2)}) collective-permute-start(bf16[4,2,112,384]{3,2,1,0:T(8,128)(2,1)S(1)} %pad_maximum_fusion.a.refs_9_), channel_id=1, source_target_pairs={{0,32},{8,136},{16,48},{24,152},{32,0},{40,168},{48,16},{56,184},{... | collective-permute-start | bytes 2064392 | tf_op jit(solution)/shard_map/ppermute | solution.py:499
  156.0 18.5 %collective-permute-start.28 = (bf16[4,2,112,384]{3,2,1,0:T(8,128)(2,1)S(1)}, bf16[4,2,112,384]{3,2,1,0:T(8,128)(2,1)S(1)}, u32[]{:S(2)}, u32[]{:S(2)}) collective-permute-start(bf16[4,2,112,384]{3,2,1,0:T(8,128)(2,1)S(1)} %pad_maximum_fusion.a.refs_9_), channel_id=1, source_target_pairs={{0,16},{8,72},{16,32},{24,88},{32,48},{40,104},{48,0},{56,120},{64... | collective-permute-start | bytes 2064392 | tf_op jit(solution)/shard_map/ppermute | solution.py:499
  168.9 18.6 %copy-start.22 = (bf16[4,2,112,384]{3,2,1,0:T(8,128)(2,1)}, bf16[4,2,112,384]{3,2,1,0:T(8,128)(2,1)S(1)}, u32[]{:S(2)}) copy-start(bf16[4,2,112,384]{3,2,1,0:T(8,128)(2,1)S(1)} %collective-permute-done.31.refs_13_) | copy-start | bytes 2064388
  172.4 15.1 %copy-start.1 = (bf16[4,2,112,384]{3,2,1,0:T(8,128)(2,1)}, bf16[4,2,112,384]{3,2,1,0:T(8,128)(2,1)S(1)}, u32[]{:S(2)}) copy-start(bf16[4,2,112,384]{3,2,1,0:T(8,128)(2,1)S(1)} %collective-permute-done.30.d.refs_12_) | copy-start | bytes 2064388
  172.4 15.1 %copy-start.2 = (bf16[4,2,112,384]{3,2,1,0:T(8,128)(2,1)}, bf16[4,2,112,384]{3,2,1,0:T(8,128)(2,1)S(1)}, u32[]{:S(2)}) copy-start(bf16[4,2,112,384]{3,2,1,0:T(8,128)(2,1)S(1)} %collective-permute-done.29.c.refs_11_) | copy-start | bytes 2064388
  174.5 13.0 %copy-start.3 = (bf16[4,2,112,384]{3,2,1,0:T(8,128)(2,1)}, bf16[4,2,112,384]{3,2,1,0:T(8,128)(2,1)S(1)}, u32[]{:S(2)}) copy-start(bf16[4,2,112,384]{3,2,1,0:T(8,128)(2,1)S(1)} %collective-permute-done.28.b.refs_10_) | copy-start | bytes 2064388
  174.5 5.6 %collective-permute-start.32 = (bf16[4,2,112,384]{3,2,1,0:T(8,128)(2,1)S(1)}, bf16[4,2,112,384]{3,2,1,0:T(8,128)(2,1)S(1)}, u32[]{:S(2)}, u32[]{:S(2)}) collective-permute-start(bf16[4,2,112,384]{3,2,1,0:T(8,128)(2,1)S(1)} %collective-permute-done.28.b.refs_10_), channel_id=1, source_target_pairs={{0,8},{8,0},{16,24},{24,16},{32,40},{40,32},{48,56},{56,48},{64,72... | collective-permute-start | bytes 2064392 | tf_op jit(solution)/shard_map/ppermute | solution.py:439
  175.8 4.3 %collective-permute-start.33 = (bf16[4,2,112,384]{3,2,1,0:T(8,128)(2,1)S(1)}, bf16[4,2,112,384]{3,2,1,0:T(8,128)(2,1)S(1)}, u32[]{:S(2)}, u32[]{:S(2)}) collective-permute-start(bf16[4,2,112,384]{3,2,1,0:T(8,128)(2,1)S(1)} %collective-permute-done.29.c.refs_11_), channel_id=1, source_target_pairs={{0,8},{8,0},{16,24},{24,16},{32,40},{40,32},{48,56},{56,48},{64,72... | collective-permute-start | bytes 2064392 | tf_op jit(solution)/shard_map/ppermute | solution.py:439
  175.8 4.3 %collective-permute-start.34 = (bf16[4,2,112,384]{3,2,1,0:T(8,128)(2,1)S(1)}, bf16[4,2,112,384]{3,2,1,0:T(8,128)(2,1)S(1)}, u32[]{:S(2)}, u32[]{:S(2)}) collective-permute-start(bf16[4,2,112,384]{3,2,1,0:T(8,128)(2,1)S(1)} %collective-permute-done.30.d.refs_12_), channel_id=1, source_target_pairs={{0,8},{8,0},{16,24},{24,16},{32,40},{40,32},{48,56},{56,48},{64,72... | collective-permute-start | bytes 2064392 | tf_op jit(solution)/shard_map/ppermute | solution.py:439
  176.3 3.7 %collective-permute-start.35 = (f32[8,128]{1,0:T(8,128)S(1)}, f32[8,128]{1,0:T(8,128)S(1)}, u32[]{:S(2)}, u32[]{:S(2)}) collective-permute-start(f32[8,128]{1,0:T(8,128)S(1)} %plane_sums.1), channel_id=1, source_target_pairs={{0,1},{1,0},{2,3},{3,2},{4,5},{5,4},{6,7},{7,6},{8,9},{9,8},{10,11... | collective-permute-start | bytes 12296 | tf_op jit(solution)/shard_map/ppermute | solution.py:505
  180.0 17.8 %copy-start.19 = (f32[512,384]{1,0:T(8,128)S(1)}, f32[512,384]{1,0:T(8,128)}, u32[]{:S(2)}) copy-start(f32[512,384]{1,0:T(8,128)} %forward.2) | copy-start | bytes 2359300
  180.9 4.3 %copy-start.25 = (bf16[4,2,112,384]{3,2,1,0:T(8,128)(2,1)}, bf16[4,2,112,384]{3,2,1,0:T(8,128)(2,1)S(1)}, u32[]{:S(2)}) copy-start(bf16[4,2,112,384]{3,2,1,0:T(8,128)(2,1)S(1)} %collective-permute-done.34.refs_16_) | copy-start | bytes 2064388
  180.9 14.8 %collective-permute-start.38 = (f32[8,128]{1,0:T(8,128)S(1)}, f32[8,128]{1,0:T(8,128)S(1)}, u32[]{:S(2)}, u32[]{:S(2)}) collective-permute-start(f32[8,128]{1,0:T(8,128)S(1)} %add.111), channel_id=1, source_target_pairs={{0,6},{1,7},{2,4},{3,5},{4,2},{5,3},{6,0},{7,1},{8,14},{9,15},{10,... | collective-permute-start | bytes 12296 | tf_op jit(solution)/shard_map/ppermute | solution.py:507
  183.0 12.8 %collective-permute-start.37 = (f32[8,128]{1,0:T(8,128)S(1)}, f32[8,128]{1,0:T(8,128)S(1)}, u32[]{:S(2)}, u32[]{:S(2)}) collective-permute-start(f32[8,128]{1,0:T(8,128)S(1)} %add.111), channel_id=1, source_target_pairs={{0,4},{1,5},{2,6},{3,7},{4,0},{5,1},{6,2},{7,3},{8,12},{9,13},{10,... | collective-permute-start | bytes 12296 | tf_op jit(solution)/shard_map/ppermute | solution.py:507
  185.2 10.6 %collective-permute-start.36 = (f32[8,128]{1,0:T(8,128)S(1)}, f32[8,128]{1,0:T(8,128)S(1)}, u32[]{:S(2)}, u32[]{:S(2)}) collective-permute-start(f32[8,128]{1,0:T(8,128)S(1)} %add.111), channel_id=1, source_target_pairs={{0,2},{1,3},{2,0},{3,1},{4,6},{5,7},{6,4},{7,5},{8,10},{9,11},{10,... | collective-permute-start | bytes 12296 | tf_op jit(solution)/shard_map/ppermute | solution.py:507
  (9 other events, 14.4 us)
Sparse Core Ops, SparseCore 0:
  38.6 60.9 all-gather.3
  101.4 50.6 all-gather.5
